TPU v7x, 256 devices: a whole 4x4x8 slice. The times are simulated.
256 devices in a mesh: slab: 2 (over core), scan: 128 (over y, x, z).
Axes of the slice: x: 4, y: 4, z: 8, core: 2. Of those that a mesh axis runs over, the one named last changes fastest.
Arguments:
- probe_modes: bfloat16 [4, 256, 512], replicated, may hold values from -6 to 6
- tap_weights: bfloat16 [2, 2, 31], replicated, may hold values from -0.75 to 0.75
- object_slices: float32 [2, 1024, 128, 256], P('slab', 'scan'), may hold values from -5 to 5
- exit_residual: bfloat16 [128, 2, 4, 256, 512], P('scan'), may hold values from -6 to 6
- offsets: int32 [128, 2, 2], P('scan'), may hold values from 0 to 127
- owners: int32 [128, 2, 9], P('scan'), may hold values from 0 to 1023, as said below
Outputs:
- updated_slices: float32 [2, 1024, 128, 256], P('slab', 'scan')
Inputs may be any that keep to these rules, and one draw needn't show every extreme that they name: `owners`: for position p of group g, entry 3 i + j names the tile in block row i and block column j; its value is c * 8 + q, with c = (g - 1 + j) mod 128 the group that holds the tile and q one of its 8 slots. The nine entries of a position are distinct.
All inputs are finite; a program needn't handle non-finite values.
Results may differ from a plain program's by a relative error of at most 0.01.
Values may be sent and summed in bfloat16 or wider, within the bound.
No kernel may reach another device: no remote copies, remote signals or barrier semaphores. Data moves between devices by JAX's collectives and lax.ppermute only.
A program may use at most 64 MiB of HBM per device.

v0:
```python
import jax
import jax.numpy as jnp
from jax import lax
from jax.sharding import PartitionSpec as P

step_rate = 0.125


def passed_along(block, axis, distance):
    devices = range(lax.axis_size(axis))
    route = [((i - distance) % len(devices), i) for i in devices]
    return lax.ppermute(block, axis, route)


def padded(value, sides, width):
    for axis, dim in sides:
        count, length = (lax.axis_size(axis), value.shape[dim])
        up = [(i, (i + 1) % count) for i in range(count)]
        down = [(j, i) for i, j in up]
        last = lax.slice_in_dim(value, length - width, length, axis=dim)
        first = lax.slice_in_dim(value, 0, width, axis=dim)
        before = lax.ppermute(last, axis, up)
        after = lax.ppermute(first, axis, down)
        value = jnp.concatenate([before, value, after], axis=dim)
    return value


def passed_along_2(value, axis, by):
    count = lax.axis_size(axis)
    pairs = [(i, i + by) for i in range(count) if 0 <= i + by < count]
    return lax.ppermute(value, axis, pairs)


def band_matrix(weights, extent):
    tap_count = weights.shape[0]
    half_width = (tap_count - 1) // 2
    tap_line = jnp.concatenate(
        [
            weights[half_width:],
            jnp.zeros((2 * extent - 1 - tap_count,), weights.dtype),
            weights[:half_width],
        ]
    )
    repeated = jnp.tile(tap_line, extent)
    return repeated[: extent * (2 * extent - 2)].reshape(extent, 2 * extent - 2)[:, :extent]


def kernels(tap_weights, extent):
    rows_re = band_matrix(tap_weights[0, 0], extent)
    rows_im = band_matrix(tap_weights[0, 1], extent)
    cols_re = band_matrix(tap_weights[1, 0], extent)
    cols_im = band_matrix(tap_weights[1, 1], extent)
    left_mat = jnp.concatenate([rows_re, rows_im], 0)
    left_adj = jnp.concatenate([rows_re.T, rows_im.T], 0)
    right_mat = jnp.concatenate(
        [jnp.concatenate([cols_re.T, cols_im.T], 1), jnp.concatenate([-cols_im.T, cols_re.T], 1)], 0
    )
    return (left_mat, left_adj, right_mat)


def matmul(spec, left_op, right_op):
    return jnp.einsum(spec, left_op, right_op, preferred_element_type=jnp.float32)


def combine(product, extent, sign_flip):
    top_half = product[..., :extent, :]
    low_half = product[..., extent:, :]
    real_part = top_half[..., :extent] - sign_flip * low_half[..., extent:]
    imag_part = top_half[..., extent:] + sign_flip * low_half[..., :extent]
    return jnp.concatenate([real_part, imag_part], -1)


def propagate(wavefield, matrices):
    extent = wavefield.shape[-2]
    mixed_rows = combine(matmul("rk,...kc->...rc", matrices[0], wavefield), extent, 1.0).astype(
        jnp.bfloat16
    )
    return matmul("...rk,kc->...rc", mixed_rows, matrices[2]).astype(jnp.bfloat16)


def adjoint(wavefield, matrices):
    extent = wavefield.shape[-2]
    mixed_rows = matmul("...rk,ck->...rc", wavefield, matrices[2]).astype(jnp.bfloat16)
    return combine(matmul("rk,...kc->...rc", matrices[1], mixed_rows), extent, -1.0).astype(
        jnp.bfloat16
    )


def complex_product(left_op, right_op, conjugate):
    extent = left_op.shape[-1] // 2
    left_re = left_op[..., :extent].astype(jnp.float32)
    left_im = left_op[..., extent:].astype(jnp.float32)
    right_re = right_op[..., :extent].astype(jnp.float32)
    right_im = right_op[..., extent:].astype(jnp.float32)
    if conjugate:
        real_part = left_re * right_re + left_im * right_im
        imag_part = left_re * right_im - left_im * right_re
    else:
        real_part = left_re * right_re - left_im * right_im
        imag_part = left_re * right_im + left_im * right_re
    return jnp.concatenate([real_part, imag_part], -1)


def selectors(row_shift, col_shift, extent, tile_side, dtype):
    block_pos = jnp.arange(3, dtype=jnp.int32)[:, None, None] * tile_side
    row_pick = (
        block_pos + jnp.arange(tile_side, dtype=jnp.int32)[None, None, :]
        == jnp.arange(extent, dtype=jnp.int32)[None, :, None] + row_shift
    ).astype(dtype)
    col_pick = (
        block_pos + jnp.arange(tile_side, dtype=jnp.int32)[None, :, None]
        == jnp.arange(extent, dtype=jnp.int32)[None, None, :] + col_shift
    ).astype(dtype)
    return (row_pick, col_pick)


def assemble(tiles, row_shift, col_shift, extent):
    layers = tiles.shape[0]
    tile_side = tiles.shape[-2]
    tile_grid = tiles.reshape(layers, 3, 3, tile_side, 2, tile_side)
    row_pick, col_pick = selectors(row_shift, col_shift, extent, tile_side, jnp.bfloat16)
    picked_rows = jnp.einsum(
        "ira,lijaph->ljrph", row_pick, tile_grid, preferred_element_type=jnp.float32
    ).astype(jnp.bfloat16)
    window = jnp.einsum(
        "ljrph,jhc->lrpc", picked_rows, col_pick, preferred_element_type=jnp.float32
    ).astype(jnp.bfloat16)
    return window.reshape(layers, extent, 2 * extent)


def disassemble(window_terms, row_shift, col_shift, tile_side):
    layers = window_terms.shape[0]
    extent = window_terms.shape[-2]
    row_pick, col_pick = selectors(row_shift, col_shift, extent, tile_side, jnp.float32)
    split_terms = window_terms.reshape(layers, extent, 2, extent)
    row_tiles = jnp.einsum(
        "ira,lrpc->liapc", row_pick, split_terms, precision=lax.Precision.HIGHEST
    )
    placed = jnp.einsum("liapc,jhc->lijaph", row_tiles, col_pick, precision=lax.Precision.HIGHEST)
    return placed.reshape(layers, 9, tile_side, 2 * tile_side)


def forward(wavefield, windows, matrices, finish):
    layer_count = windows.shape[0]
    inputs = [wavefield]
    if 1 < layer_count or finish:
        product = complex_product(wavefield, windows[0][:, None], False).astype(jnp.bfloat16)
        wavefield = propagate(product, matrices)
    return (jnp.stack(inputs), wavefield)


def backward(incoming, inputs, windows, matrices, finish):
    layer_count = windows.shape[0]
    slice_terms = [None] * layer_count
    for layer_index in reversed(range(layer_count)):
        adjoint_wave = adjoint(incoming, matrices)
        slice_terms[layer_index] = jnp.sum(
            complex_product(inputs[layer_index], adjoint_wave, True), axis=1
        )
        if layer_index > 0 or finish:
            incoming = complex_product(windows[layer_index][:, None], adjoint_wave, True).astype(
                jnp.bfloat16
            )
    return (jnp.stack(slice_terms), incoming)


def windows_for(tile_stack, local_slots, shifts, extent):
    pieces = []
    for item_index in range(local_slots.shape[0]):
        tiles = jnp.take(tile_stack, local_slots[item_index], axis=1)
        pieces.append(assemble(tiles, shifts[item_index, 0], shifts[item_index, 1], extent))
    return jnp.stack(pieces, 1)


def gather_terms(window_terms, local_slots, shifts, tile_side, slot_count):
    pieces = []
    for item_index in range(local_slots.shape[0]):
        pieces.append(
            disassemble(
                window_terms[:, item_index], shifts[item_index, 0], shifts[item_index, 1], tile_side
            )
        )
    stacked = jnp.concatenate(pieces, 1)
    selector = (
        jnp.arange(3 * slot_count, dtype=jnp.int32)[:, None] == local_slots.reshape(-1)[None, :]
    ).astype(jnp.float32)
    return jnp.einsum("nk,skab->snab", selector, stacked, precision=lax.Precision.HIGHEST)


def deliver(tile_sums, slot_count):
    before = tile_sums[:, :slot_count]
    own_part = tile_sums[:, slot_count : 2 * slot_count]
    beyond = tile_sums[:, 2 * slot_count :]
    from_right = passed_along(before, "scan", -1)
    from_left = passed_along(beyond, "scan", 1)
    return own_part + from_right + from_left


def shards(probe_modes, tap_weights, object_slices, exit_residual, offsets, owners):
    extent = probe_modes.shape[-2]
    tile_side = object_slices.shape[-2]
    layers = object_slices.shape[0]
    slot_count = object_slices.shape[1]
    positions = offsets.shape[1]
    matrices = kernels(tap_weights, extent)
    group_index = lax.axis_index("scan")
    groups = lax.axis_size("scan")
    section_index = lax.axis_index("slab")
    is_head = section_index == 0
    owned_tiles = object_slices.astype(jnp.bfloat16)[:, None]
    beside_all = padded(owned_tiles, (("scan", 1),), 1)
    beside_all = beside_all.reshape(layers, 3 * slot_count, tile_side, 2 * tile_side)
    local_slots = (owners[0] // slot_count - group_index + 1) % groups * slot_count + owners[
        0
    ] % slot_count
    shifts = offsets[0]
    windows = windows_for(beside_all, local_slots, shifts, extent)
    starts = jnp.broadcast_to(probe_modes[None], (positions,) + probe_modes.shape)
    blank_wave = jnp.zeros(starts.shape, jnp.bfloat16)
    blank_terms = jnp.zeros((layers, positions, extent, 2 * extent), jnp.float32)
    blank_inputs = jnp.zeros((layers,) + starts.shape, jnp.bfloat16)

    def head_forward(unused):
        return forward(starts, windows, matrices, True)

    def head_waiting(unused):
        return (blank_inputs, blank_wave)

    kept_inputs, leaving = lax.cond(is_head, head_forward, head_waiting, 0)
    arriving = passed_along_2(leaving, "slab", 1)

    def tail_sweep(unused):
        inputs = forward(arriving, windows, matrices, False)[0]
        return backward(exit_residual[0], inputs, windows, matrices, True)

    def tail_waiting(unused):
        return (blank_terms, blank_wave)

    tail_terms, returning = lax.cond(is_head, tail_waiting, tail_sweep, 0)
    coming = passed_along_2(returning, "slab", -1)

    def head_backward(unused):
        return backward(coming, kept_inputs, windows, matrices, False)[0]

    def head_resting(unused):
        return blank_terms

    head_terms = lax.cond(is_head, head_backward, head_resting, 0)
    window_terms = head_terms + tail_terms
    tile_sums = gather_terms(window_terms, local_slots, shifts, tile_side, slot_count)
    gradient_sum = deliver(tile_sums, slot_count)
    return object_slices - step_rate * gradient_sum


def solution(mesh):
    placed = (
        P(),
        P(),
        P("slab", "scan", None, None),
        P("scan", None, None, None, None),
        P("scan", None, None),
        P("scan", None, None),
    )
    return jax.shard_map(
        shards, mesh=mesh, in_specs=placed, out_specs=P("slab", "scan", None, None), check_vma=False
    )
```

profile of v0, /device:TPU:0, one launch (start us, length us, event | category | flops | bytes accessed | tf_op | source)
XLA Modules:
  0.0 129.4 jit_solution(11958731016048803923)
XLA Ops:
  0.0 1.3 convert_bitcast_fusion
  1.3 8.8 %collective-permute-start.1 = (bf16[1,1,8,128,256]{4,3,2,1,0:T(8,128)(2,1)S(1)}, bf16[1,1,8,128,256]{4,3,2,1,0:T(8,128)(2,1)S(1)}, u32[]{:S(2)}, u32[]{:S(2)}) collective-permute-start(bf16[1,1,8,128,256]{4,3,2,1,0:T(8,128)(2,1)S(1)} %convert_bitcast_fusion), channel_id=1, source_target_pairs={{1,0},{2,1},{3,2},{4,3},{5,4},{6,5},{7,6},{8,7},{9,8},{10,9},{11,1... | collective-permute-start | bytes 1572872 | tf_op jit(solution)/shard_map/ppermute | solution.py:23
  10.1 0.7 slice_bitcast_fusion.6
  10.9 0.8 slice_bitcast_fusion.7
  11.7 0.7 fusion.95
  12.4 1.4 %fusion.108 = (s32[1,1]{1,0:T(1,128)}, s32[1,1]{1,0:T(1,128)}, s32[1,1]{1,0:T(1,128)}, s32[1,1]{1,0:T(1,128)}) fusion(s32[2,2]{1,0:T(2,128)} %bitcast.267), kind=kLoop, calls=%fused_computation.199 | loop fusion | bytes 32 | tf_op jit(solution)/shard_map/slice | solution.py:180
  13.8 1.2 iota_add_fusion.4
  15.1 1.2 iota_add_fusion.1
  16.3 1.2 iota_add_fusion.2
  17.5 1.2 iota_add_fusion.3
  18.8 0.6 tile.43
  19.4 0.5 reshape.241
  19.9 0.6 tile.19
  20.5 0.5 reshape.239
  21.0 0.6 tile.41
  21.6 0.5 reshape.240
  22.1 0.6 tile.17
  22.7 0.5 reshape.238
  23.2 0.7 slice_bitcast_fusion.14
  24.1 0.8 copy-done.5
  24.9 4.1 %collective-permute-done = bf16[1,1,8,128,256]{4,3,2,1,0:T(8,128)(2,1)} collective-permute-done((bf16[1,1,8,128,256]{4,3,2,1,0:T(8,128)(2,1)S(1)}, bf16[1,1,8,128,256]{4,3,2,1,0:T(8,128)(2,1)}, u32[]{:S(2)}, u32[]{:S(2)}) %collective-permute-start) | collective-permute-done | bytes 524320 | tf_op jit(solution)/shard_map/ppermute | solution.py:22
  29.0 1.4 %pad_maximum_fusion.1 = bf16[1,3,8,128,256]{4,3,2,1,0:T(8,128)(2,1)S(1)} fusion(bf16[1,1,8,128,256]{4,3,2,1,0:T(8,128)(2,1)} %copy-done.5, bf16[1,1,8,128,256]{4,3,2,1,0:T(8,128)(2,1)S(1)} %convert_bitcast_fusion, bf16[1,1,8,128,256]{4,3,2,1,0:T(8,128)(2,1)} %collective-permute-done), kind=kLoop, calls=%fused_computation.82 | loop fusion | flops 1572864 | bytes 3145728 | tf_op jit(solution)/shard_map/concatenate | solution.py:24
  30.4 0.6 gather_fusion.1
  31.0 0.6 gather_fusion
  32.5 0.5 fusion.63
  32.9 0.4 fusion.57
  33.4 0.5 fusion.65
  33.9 0.4 fusion.56
  34.4 8.0 %conditional.3 = (bf16[1,2,4,256,512]{4,3,2,1,0:T(8,128)(2,1)}, bf16[2,4,256,512]{3,2,1,0:T(8,128)(2,1)S(1)}) conditional(s32[]{:T(128)} %convert_element_type.95, () %tuple.29, (bf16[4,256,512]{2,1,0:T(8,128)(2,1)}, bf16[1,2,256,512]{2,3,1,0:T(8,128)(2,1)S(1)}, bf16[512,256]{1,0:T(8,128)(2,1)S(1)}, bf16[512,512]{0,1:T(8,128)(2,1)S(1)}) %tuple.30), branch_computations={%region_0.2_spmd, %region_1.3_spmd} | conditional | flops 2163998720 | bytes 45350956 | solution.py:229
  34.6 1.5 %copy.94 = bf16[4,256,512]{1,2,0:T(8,128)(2,1)S(1)} copy(bf16[4,256,512]{2,1,0:T(8,128)(2,1)} %get-tuple-element.97) | data formatting | bytes 2097152 | tf_op jit(solution)/shard_map
  36.3 0.6 subtract_convert_fusion
  37.0 0.6 copy-done
  37.6 1.5 %stack_broadcast_in_dim.0 = bf16[1,2,4,256,512]{4,3,2,1,0:T(8,128)(2,1)} broadcast(bf16[4,256,512]{2,1,0:T(8,128)(2,1)S(1)} %copy-done), dimensions={2,3,4} | broadcast | bytes 3145728 | tf_op jit(solution)/shard_map/cond/branch_1_fun/stack;broadcast_in_dim | solution.py:149
  39.1 1.3 convolution_bitcast_fusion
  40.4 0.6 fusion.1
  41.0 1.3 %fusion.9 = bf16[2,4,256,512]{3,2,1,0:T(8,128)(2,1)S(1)} fusion(bf16[2,4,256,256]{2,3,1,0:T(8,128)(2,1)S(1)} %get-tuple-element.121, bf16[2,4,256,256]{2,3,1,0:T(8,128)(2,1)S(1)} %get-tuple-element.120, bf16[512,512]{0,1:T(8,128)(2,1)S(1)} %get-tuple-element.100), kind=kOutput, calls=%fused_computation.16 | convolution fusion | flops 1078984704 | bytes 4718592 | tf_op jit(solution)/shard_map/cond/branch_1_fun/...rk,kc->...rc/dot_general | solution.py:62
  42.4 2.4 %copy.96 = bf16[2,4,256,512]{2,3,1,0:T(8,128)(2,1)} copy(bf16[2,4,256,512]{3,2,1,0:T(8,128)(2,1)S(1)} %get-tuple-element.56) | data formatting | bytes 4194304 | tf_op jit(solution)/shard_map/cond | solution.py:229
  44.7 1.4 %collective-permute-start.2 = (bf16[2,4,256,512]{2,3,1,0:T(8,128)(2,1)}, bf16[2,4,256,512]{2,3,1,0:T(8,128)(2,1)S(1)}, u32[]{:S(2)}, u32[]{:S(2)}) collective-permute-start(bf16[2,4,256,512]{2,3,1,0:T(8,128)(2,1)} %copy.96), channel_id=1, source_target_pairs={{0,128},{1,129},{2,130},{3,131},{4,132},{5,133},{6,134},{7,135},{8... | collective-permute-start | bytes 6291464 | tf_op jit(solution)/shard_map/ppermute | solution.py:31
  46.2 3.8 %collective-permute-done.2 = bf16[2,4,256,512]{2,3,1,0:T(8,128)(2,1)S(1)} collective-permute-done((bf16[2,4,256,512]{2,3,1,0:T(8,128)(2,1)}, bf16[2,4,256,512]{2,3,1,0:T(8,128)(2,1)S(1)}, u32[]{:S(2)}, u32[]{:S(2)}) %collective-permute-start.2) | collective-permute-done | bytes 2097184 | tf_op jit(solution)/shard_map/ppermute | solution.py:31
  50.0 1.2 conditional.4
  50.0 1.0 broadcast_in_dim.25
  51.2 2.4 %copy.99 = bf16[2,4,256,512]{3,2,1,0:T(8,128)(2,1)} copy(bf16[2,4,256,512]{2,3,1,0:T(8,128)(2,1)S(1)} %get-tuple-element.57) | data formatting | bytes 4194304 | tf_op jit(solution)/shard_map/cond | solution.py:239
  53.6 1.3 collective-permute-start.3
  55.0 18.6 %collective-permute-done.3 = bf16[2,4,256,512]{3,2,1,0:T(8,128)(2,1)S(1)} collective-permute-done((bf16[2,4,256,512]{3,2,1,0:T(8,128)(2,1)}, bf16[2,4,256,512]{3,2,1,0:T(8,128)(2,1)S(1)}, u32[]{:S(2)}, u32[]{:S(2)}) %collective-permute-start.3) | collective-permute-done | bytes 2097184 | tf_op jit(solution)/shard_map/ppermute | solution.py:31
  73.5 16.7 %conditional.5 = (f32[1,2,256,512]{2,3,1,0:T(8,128)S(1)}) conditional(s32[]{:T(128)} %convert_element_type.95, () %tuple.28, (bf16[1,2,4,256,512]{4,3,2,1,0:T(8,128)(2,1)}, bf16[2,4,256,512]{3,2,1,0:T(8,128)(2,1)S(1)}, bf16[512,512]{0,1:T(8,128)(2,1)S(1)}, bf16[512,256]{0,1:T(8,128)(2,1)S(1)}) %tuple.33), branch_computations={%region_5.7_spmd, %region_6.9_spmd} | conditional | flops 2160852992 | bytes 50069540 | solution.py:248
  73.5 1.4 %copy-done.4 = bf16[2,4,256,512]{3,2,1,0:T(8,128)(2,1)} copy-done((bf16[2,4,256,512]{3,2,1,0:T(8,128)(2,1)}, bf16[2,4,256,512]{3,2,1,0:T(8,128)(2,1)S(1)}, u32[]{:S(2)}) %copy-start.4) | copy-done | bytes 2097176 | tf_op jit(solution)/shard_map/cond
  74.9 2.8 %copy.100 = bf16[1,2,4,256,512]{3,4,2,1,0:T(8,128)(2,1)S(1)} copy(bf16[1,2,4,256,512]{4,3,2,1,0:T(8,128)(2,1)} %get-tuple-element.106) | data formatting | bytes 4194304 | tf_op jit(solution)/shard_map
  77.7 7.2 %convolution_bitcast_fusion.2 = f32[2,4,512,512]{2,3,1,0:T(8,128)} fusion(bf16[2,4,256,512]{3,2,1,0:T(8,128)(2,1)} %copy-done.4, bf16[512,512]{0,1:T(8,128)(2,1)S(1)} %get-tuple-element.108, bf16[512,256]{0,1:T(8,128)(2,1)S(1)} %get-tuple-element.109), kind=kOutput, calls=%fused_computation.60 | convolution fusion | flops 2148532224 | bytes 11272192 | tf_op jit(solution)/shard_map/cond/branch_1_fun/rk,...kc->...rc/dot_general | solution.py:62
  84.9 4.5 %fusion.40 = (f32[2,4,256,256]{2,3,1,0:T(8,128)S(1)}, bf16[2,4,256,256]{2,3,1,0:T(8,128)(2,1)S(1)}, bf16[2,4,256,256]{2,3,1,0:T(8,128)(2,1)S(1)}) fusion(bf16[2,4,256,512]{2,3,1,0:T(8,128)(2,1)S(1)} %bitcast.248, f32[2,4,512,512]{2,3,1,0:T(8,128)} %convolution_bitcast_fusion.2), kind=kLoop, calls=%fused_computation.65 | loop fusion | flops 6815744 | bytes 14680064 | tf_op jit(solution)/shard_map/cond/branch_1_fun/add | solution.py:96
  89.4 0.5 fusion.41
  90.2 1.4 %add.235 = f32[1,2,256,512]{2,3,1,0:T(8,128)S(1)} add(f32[1,2,256,512]{2,3,1,0:T(8,128)S(1)} %get-tuple-element.173, f32[1,2,256,512]{2,3,1,0:T(8,128)} %get-tuple-element.58) | non-fusion elementwise | flops 262144 | bytes 3145728 | tf_op jit(solution)/shard_map/add | solution.py:249
  91.7 0.7 convolution_bitcast_fusion.5
  92.4 0.7 convolution_bitcast_fusion.6
  93.0 0.8 convolution_bitcast_fusion.4
  93.9 0.8 convolution_bitcast_fusion.3
  94.7 1.2 copy.106
  95.8 2.1 %copy.108 = f32[1,9,128,256]{3,1,2,0:T(8,128)S(1)} copy(f32[1,9,128,256]{2,3,1,0:T(8,128)} %bitcast.255) | data formatting | bytes 2359296 | tf_op jit(solution)/shard_map/reshape | solution.py:140
  98.0 2.0 %copy.107 = f32[1,9,128,256]{3,1,2,0:T(8,128)} copy(f32[1,9,128,256]{2,3,1,0:T(8,128)S(1)} %bitcast.254) | data formatting | bytes 2359296 | tf_op jit(solution)/shard_map/reshape | solution.py:140
  99.9 3.6 %fusion.55 = f32[1,24,128,256]{3,1,2,0:T(8,128)S(1)} fusion(f32[1,9,128,256]{3,1,2,0:T(8,128)S(1)} %copy.108, f32[1,9,128,256]{3,1,2,0:T(8,128)} %copy.107, s32[18]{0:T(128)S(1)} %fusion.97), kind=kOutput, calls=%fused_computation.81 | convolution fusion | flops 170459568 | bytes 5505096 | tf_op jit(solution)/shard_map/nk,skab->snab/dot_general | solution.py:187
  103.7 3.4 %collective-permute-start.4 = (f32[1,8,128,256]{3,1,2,0:T(8,128)S(1)}, f32[1,8,128,256]{3,1,2,0:T(8,128)S(1)}, u32[]{:S(2)}, u32[]{:S(2)}) collective-permute-start(f32[1,8,128,256]{3,1,2,0:T(8,128)S(1)} %get-tuple-element.133), channel_id=1, source_target_pairs={{1,0},{2,1},{3,2},{4,3},{5,4},{6,5},{7,6},{8,7},{9,8},{10,9},{11,1... | collective-permute-start | bytes 3145736 | tf_op jit(solution)/shard_map/ppermute | solution.py:12
  107.1 12.3 %collective-permute-done.4 = f32[1,8,128,256]{3,1,2,0:T(8,128)S(1)} collective-permute-done((f32[1,8,128,256]{3,1,2,0:T(8,128)S(1)}, f32[1,8,128,256]{3,1,2,0:T(8,128)S(1)}, u32[]{:S(2)}, u32[]{:S(2)}) %collective-permute-start.4) | collective-permute-done | bytes 1048608 | tf_op jit(solution)/shard_map/ppermute | solution.py:12
  119.4 7.9 %collective-permute-done.5 = f32[1,8,128,256]{3,1,2,0:T(8,128)S(1)} collective-permute-done((f32[1,8,128,256]{3,1,2,0:T(8,128)S(1)}, f32[1,8,128,256]{3,1,2,0:T(8,128)S(1)}, u32[]{:S(2)}, u32[]{:S(2)}) %collective-permute-start.5) | collective-permute-done | bytes 1048608 | tf_op jit(solution)/shard_map/ppermute | solution.py:12
  127.4 0.7 fusion.60
  128.1 1.3 copy.110
  (53 shorter events, 2.4 us)
Async XLA Ops:
  1.3 22.9 %collective-permute-start.1 = (bf16[1,1,8,128,256]{4,3,2,1,0:T(8,128)(2,1)S(1)}, bf16[1,1,8,128,256]{4,3,2,1,0:T(8,128)(2,1)S(1)}, u32[]{:S(2)}, u32[]{:S(2)}) collective-permute-start(bf16[1,1,8,128,256]{4,3,2,1,0:T(8,128)(2,1)S(1)} %convert_bitcast_fusion), channel_id=1, source_target_pairs={{1,0},{2,1},{3,2},{4,3},{5,4},{6,5},{7,6},{8,7},{9,8},{10,9},{11,1... | collective-permute-start | bytes 1572872 | tf_op jit(solution)/shard_map/ppermute | solution.py:23
  10.1 18.9 %collective-permute-start = (bf16[1,1,8,128,256]{4,3,2,1,0:T(8,128)(2,1)S(1)}, bf16[1,1,8,128,256]{4,3,2,1,0:T(8,128)(2,1)}, u32[]{:S(2)}, u32[]{:S(2)}) collective-permute-start(bf16[1,1,8,128,256]{4,3,2,1,0:T(8,128)(2,1)S(1)} %convert_bitcast_fusion), channel_id=1, source_target_pairs={{0,1},{1,2},{2,3},{3,4},{4,5},{5,6},{6,7},{7,8},{8,9},{9,10},{10,1... | collective-permute-start | bytes 1572872 | tf_op jit(solution)/shard_map/ppermute | solution.py:22
  24.1 0.8 copy-start.5
  31.8 0.7 copy-start.12
  31.8 1.1 copy-start.8
  31.8 1.6 %copy-start.11 = (s32[256]{0:T(256)S(1)}, s32[256]{0:T(256)}, u32[]{:S(2)}) copy-start(s32[256]{0:T(256)} %iota_add_fusion.3) | copy-start | bytes 3076
  32.1 1.7 %copy-start.9 = (s32[256]{0:T(256)S(1)}, s32[256]{0:T(256)}, u32[]{:S(2)}) copy-start(s32[256]{0:T(256)} %iota_add_fusion.4) | copy-start | bytes 3076
  36.3 1.2 copy-start
  42.3 3.8 %copy-start.6 = (bf16[256,256]{0,1:T(8,128)(2,1)S(1)}, bf16[256,256]{0,1:T(8,128)(2,1)}, u32[]{:S(2)}) copy-start(bf16[256,256]{0,1:T(8,128)(2,1)} %get-tuple-element.139) | copy-start | bytes 393220
  42.3 3.8 %copy-start.7 = (bf16[256,256]{0,1:T(8,128)(2,1)S(1)}, bf16[256,256]{0,1:T(8,128)(2,1)}, u32[]{:S(2)}) copy-start(bf16[256,256]{0,1:T(8,128)(2,1)} %get-tuple-element.162) | copy-start | bytes 393220
  44.7 5.3 %collective-permute-start.2 = (bf16[2,4,256,512]{2,3,1,0:T(8,128)(2,1)}, bf16[2,4,256,512]{2,3,1,0:T(8,128)(2,1)S(1)}, u32[]{:S(2)}, u32[]{:S(2)}) collective-permute-start(bf16[2,4,256,512]{2,3,1,0:T(8,128)(2,1)} %copy.96), channel_id=1, source_target_pairs={{0,128},{1,129},{2,130},{3,131},{4,132},{5,133},{6,134},{7,135},{8... | collective-permute-start | bytes 6291464 | tf_op jit(solution)/shard_map/ppermute | solution.py:31
  51.2 3.7 %copy-start.10 = (s32[1,2,9]{2,1,0:T(2,128)S(1)}, s32[1,2,9]{2,1,0:T(2,128)}, u32[]{:S(2)}) copy-start(s32[1,2,9]{2,1,0:T(2,128)} %param.19) | copy-start | bytes 220
  53.6 20.0 %collective-permute-start.3 = (bf16[2,4,256,512]{3,2,1,0:T(8,128)(2,1)}, bf16[2,4,256,512]{3,2,1,0:T(8,128)(2,1)S(1)}, u32[]{:S(2)}, u32[]{:S(2)}) collective-permute-start(bf16[2,4,256,512]{3,2,1,0:T(8,128)(2,1)} %copy.99), channel_id=1, source_target_pairs={{128,0},{129,1},{130,2},{131,3},{132,4},{133,5},{134,6},{135,7},{1... | collective-permute-start | bytes 6291464 | tf_op jit(solution)/shard_map/ppermute | solution.py:31
  73.5 1.4 %copy-start.4 = (bf16[2,4,256,512]{3,2,1,0:T(8,128)(2,1)}, bf16[2,4,256,512]{3,2,1,0:T(8,128)(2,1)S(1)}, u32[]{:S(2)}) copy-start(bf16[2,4,256,512]{3,2,1,0:T(8,128)(2,1)S(1)} %get-tuple-element.48) | copy-start | bytes 6291460 | tf_op jit(solution)/shard_map/cond
  90.2 1.5 %copy-start.13 = (s32[256]{0:T(256)S(1)}, s32[256]{0:T(256)}, u32[]{:S(2)}) copy-start(s32[256]{0:T(256)} %iota_add_fusion.2) | copy-start | bytes 3076
  103.5 23.8 %copy-start.1 = (f32[1,8,128,256]{3,2,1,0:T(8,128)S(1)}, f32[1,8,128,256]{3,2,1,0:T(8,128)}, u32[]{:S(2)}) copy-start(f32[1,8,128,256]{3,2,1,0:T(8,128)} %param.16) | copy-start | bytes 3145732
  103.7 15.7 %collective-permute-start.4 = (f32[1,8,128,256]{3,1,2,0:T(8,128)S(1)}, f32[1,8,128,256]{3,1,2,0:T(8,128)S(1)}, u32[]{:S(2)}, u32[]{:S(2)}) collective-permute-start(f32[1,8,128,256]{3,1,2,0:T(8,128)S(1)} %get-tuple-element.133), channel_id=1, source_target_pairs={{1,0},{2,1},{3,2},{4,3},{5,4},{6,5},{7,6},{8,7},{9,8},{10,9},{11,1... | collective-permute-start | bytes 3145736 | tf_op jit(solution)/shard_map/ppermute | solution.py:12
  107.1 20.2 %collective-permute-start.5 = (f32[1,8,128,256]{3,1,2,0:T(8,128)S(1)}, f32[1,8,128,256]{3,1,2,0:T(8,128)S(1)}, u32[]{:S(2)}, u32[]{:S(2)}) collective-permute-start(f32[1,8,128,256]{3,1,2,0:T(8,128)S(1)} %get-tuple-element.134), channel_id=1, source_target_pairs={{127,0},{0,1},{1,2},{2,3},{3,4},{4,5},{5,6},{6,7},{7,8},{8,9},{9,1... | collective-permute-start | bytes 3145736 | tf_op jit(solution)/shard_map/ppermute | solution.py:12
where the time goes:
time: 130 us; the launch traced here: 129 us
  waiting for transfers between devices  46.7 us (36%)
  local copies, waits for them, and re-layouts  31.4 us (24%)
  matrix products  18.1 us (14%)
  other arithmetic  17.6 us (14%)
  starting transfers between devices  15 us (12%)
    ppermute x2, waiting for transfers between devices, passed_along_2(): return lax.ppermute(value, axis, pairs)  22.4 us
    ppermute x2, waiting for transfers between devices, passed_along(): return lax.ppermute(block, axis, route)  20.2 us
    dot_general x3, matrix products, matmul(): jnp.einsum(spec, left_op, right_op, preferred_element_type=jnp.float32)  9.81 us
    ppermute x1, starting transfers between devices, padded(): after = lax.ppermute(first, axis, down)  8.84 us
    add x1, other arithmetic, complex_product(): real_part = left_re * right_re + left_im * right_im  4.52 us
    another operation x3, local copies, waits for them, and re-layouts  4.25 us
    ppermute x1, waiting for transfers between devices, padded(): before = lax.ppermute(last, axis, up)  4.11 us
    reshape x2, local copies, waits for them, and re-layouts, disassemble(): return placed.reshape(layers, 9, tile_side, 2 * tile_side)  4.11 us
  transfers between devices with their start and end apart: 6, of which 5 were waited for; matrix products, arithmetic and copies ran while one was open for 11% of the time, Pallas kernels for 0%

commit v1 on v0

v1 whole, which is shorter than its diff:
```python
import functools

import jax
import jax.numpy as jnp
from jax import lax
from jax.experimental import pallas as pl
from jax.experimental.pallas import tpu as pltpu
from jax.sharding import PartitionSpec as P

step_rate = 0.125
F32, BF16 = jnp.float32, jnp.bfloat16
NP, TS, HALF = 256, 128, 15
MODES, POS, CAP = 4, 2, 8
ROWS = CAP * TS
SMEM = pl.BlockSpec(memory_space=pltpu.SMEM)
VMEM = pl.BlockSpec(memory_space=pltpu.VMEM)


def params(mib):
    return pltpu.CompilerParams(vmem_limit_bytes=mib * 1024 * 1024)


def dot(left, right):
    return jnp.dot(left, right, preferred_element_type=F32)


def lanes(rows):
    return lax.broadcasted_iota(jnp.int32, (rows, TS), 1)


def pack_kernel(owners, offsets, tiles, out):
    for q in range(CAP):
        out[q * TS : (q + 1) * TS, :] = tiles[0, q].astype(BF16)
    spot = lax.broadcasted_iota(jnp.int32, (16, 2 * TS), 1)
    notes = jnp.zeros((16, 2 * TS), jnp.int32)
    for p in range(POS):
        for k in range(9):
            notes = jnp.where(spot == p * 16 + k, owners[0, p, k] & (CAP - 1), notes)
        notes = jnp.where(spot == p * 16 + 9, offsets[0, p, 0], notes)
    out[ROWS : ROWS + 16, :] = notes.astype(F32).astype(BF16)


def pack(owners, offsets, tiles):
    return pl.pallas_call(
        pack_kernel,
        out_shape=jax.ShapeDtypeStruct((ROWS + 16, 2 * TS), BF16),
        in_specs=[SMEM, SMEM, VMEM],
        out_specs=VMEM,
        compiler_params=params(8),
        name="pack_tiles",
    )(owners, offsets, tiles)


def band(taps, row):
    wide = jnp.broadcast_to(taps[row : row + 1, :], (NP, NP))
    turned = pltpu.roll(wide, NP - HALF, 1, stride=1, stride_axis=0)
    gap = lax.broadcasted_iota(jnp.int32, (NP, NP), 1) - lax.broadcasted_iota(jnp.int32, (NP, NP), 0)
    return jnp.where(jnp.abs(gap) <= HALF, turned, 0.0)


def exit_kernel(taps, residual, left, left_adj, right, right_adj, wave, line):
    line[...] = jnp.zeros_like(line)
    for row in range(4):
        line[row : row + 1, 0 : 2 * HALF + 1] = taps[row // 2, row % 2 : row % 2 + 1, :].astype(F32)
    values = line[...]
    for first, plain, adj in ((0, left, left_adj), (2, right_adj, right)):
        re, im = band(values, first), band(values, first + 1)
        ret, imt = re.T, im.T
        plain[0:NP, 0:NP] = re.astype(BF16)
        plain[0:NP, NP:] = (-im).astype(BF16)
        plain[NP:, 0:NP] = im.astype(BF16)
        plain[NP:, NP:] = re.astype(BF16)
        adj[0:NP, 0:NP] = ret.astype(BF16)
        adj[0:NP, NP:] = imt.astype(BF16)
        adj[NP:, 0:NP] = (-imt).astype(BF16)
        adj[NP:, NP:] = ret.astype(BF16)
    for m in range(MODES):
        w = dot(residual[0, 0, m], right_adj[...]).astype(BF16)
        w = jnp.concatenate([w[:, :NP], w[:, NP:]], 0)
        wave[m] = dot(left_adj[...], w).astype(BF16)


def exit_adjoint(side, taps, residual):
    whole = lambda *shape: pl.BlockSpec(shape, lambda i, side: (0,) * len(shape))
    return pl.pallas_call(
        lambda side, *refs: exit_kernel(*refs),
        grid_spec=pltpu.PrefetchScalarGridSpec(
            num_scalar_prefetch=1,
            grid=(1,),
            in_specs=[
                whole(2, 2, 2 * HALF + 1),
                pl.BlockSpec((1, 1, MODES, NP, 2 * NP), lambda i, side: (0, side[0], 0, 0, 0)),
            ],
            out_specs=[whole(2 * NP, 2 * NP)] * 4 + [whole(MODES, 2 * NP, NP)],
            scratch_shapes=[pltpu.VMEM((8, NP), F32)],
        ),
        out_shape=[jax.ShapeDtypeStruct((2 * NP, 2 * NP), BF16)] * 4
        + [jax.ShapeDtypeStruct((MODES, 2 * NP, NP), BF16)],
        compiler_params=params(24),
        cost_estimate=pl.CostEstimate(flops=1_100_000_000, bytes_accessed=6_000_000, transcendentals=0),
        name="exit_adjoint",
    )(side, taps, residual)


def cut_window(p, owners, offsets, sources, stack, out):
    r, c = offsets[0, p, 0], offsets[0, p, 1]
    for j, tiles in enumerate(sources):
        for i in range(3):
            q = owners[0, p, 3 * i + j] & (CAP - 1)
            tile = tiles[pl.ds(pl.multiple_of(q * TS, TS), TS), :].astype(F32)
            stack[j, 0, i * TS : (i + 1) * TS, :] = tile[:, :TS]
            stack[j, 1, i * TS : (i + 1) * TS, :] = tile[:, TS:]
    back = (TS - c) & (TS - 1)
    step = 32
    near = lanes(step) < TS - c
    for at in range(0, NP, step):
        for part in range(2):
            cols = [pltpu.roll(stack[j, part, pl.ds(r + at, step), :], back, 1) for j in range(3)]
            out[part, at : at + step, 0:TS] = jnp.where(near, cols[0], cols[1]).astype(out.dtype)
            out[part, at : at + step, TS:] = jnp.where(near, cols[1], cols[2]).astype(out.dtype)


def window_kernel(owners, offsets, before, own, after, out, stack):
    p = 1 - lax.axis_index("slab")
    cut_window(p, owners, offsets, (before, own, after), stack, out)


def far_window(owners, offsets, before, own, after):
    return pl.pallas_call(
        window_kernel,
        out_shape=jax.ShapeDtypeStruct((2, NP, NP), BF16),
        in_specs=[SMEM, SMEM, VMEM, VMEM, VMEM],
        out_specs=VMEM,
        scratch_shapes=[pltpu.VMEM((3, 2, 3 * TS, TS), F32)],
        compiler_params=params(8),
        cost_estimate=pl.CostEstimate(flops=1_000_000, bytes_accessed=2_000_000, transcendentals=0),
        name="far_window",
    )(owners, offsets, before, own, after)


def times(a, b, conjugate):
    (ar, ai), (br, bi) = a, b
    if conjugate:
        return ar * br + ai * bi, ar * bi - ai * br
    return ar * br - ai * bi, ar * bi + ai * br


def beside(ref, m):
    return ref[m, :, :NP].astype(F32), ref[m, :, NP:].astype(F32)


def above(ref, m):
    return ref[m, :NP, :].astype(F32), ref[m, NP:, :].astype(F32)


def lower_terms(t, probe, wave, left, right, total):
    for m in range(MODES):
        window = (t[0].astype(F32), t[1].astype(F32))
        u = jnp.concatenate(times(beside(probe, m), window, False), 0).astype(BF16)
        v = dot(left[...], u).astype(BF16)
        v = jnp.concatenate([v[:NP], v[NP:]], 1)
        psi = dot(v, right[...]).astype(BF16).astype(F32)
        re, im = times((psi[:, :NP], psi[:, NP:]), above(wave, m), True)
        if m == 0:
            total[0], total[1] = re, im
        else:
            total[0] += re
            total[1] += im


def upper_terms(t, probe, wave, left_adj, right_adj, total):
    for m in range(MODES):
        window = (t[0].astype(F32), t[1].astype(F32))
        b = jnp.concatenate(times(window, above(wave, m), True), 1).astype(BF16)
        w = dot(b, right_adj[...]).astype(BF16)
        w = jnp.concatenate([w[:, :NP], w[:, NP:]], 0)
        a = dot(left_adj[...], w).astype(BF16).astype(F32)
        re, im = times(beside(probe, m), (a[:NP], a[NP:]), True)
        if m == 0:
            total[0], total[1] = re, im
        else:
            total[0] += re
            total[1] += im


def both_ways(chosen, t, probe, wave, left, left_adj, right, right_adj, total):
    @pl.when(chosen == 0)
    def _():
        lower_terms(t, probe, wave, left, right, total)

    @pl.when(chosen == 1)
    def _():
        upper_terms(t, probe, wave, left_adj, right_adj, total)


def near_kernel(owners, offsets, before, own, after, probe, wave, left, left_adj, right, right_adj, out, stack, t, total):
    side = lax.axis_index("slab")
    cut_window(side, owners, offsets, (before, own, after), stack, t)
    both_ways(side, t, probe, wave, left, left_adj, right, right_adj, total)
    out[...] = total[...].astype(BF16)


def far_kernel(t, probe, wave, left, left_adj, right, right_adj, out):
    side = lax.axis_index("slab")
    both_ways(1 - side, t, probe, wave, left, left_adj, right, right_adj, out)


COST = pl.CostEstimate(flops=1_100_000_000, bytes_accessed=5_000_000, transcendentals=0)


def near_terms(owners, offsets, before, own, after, probe, wave, mats):
    return pl.pallas_call(
        near_kernel,
        out_shape=jax.ShapeDtypeStruct((2, NP, NP), BF16),
        in_specs=[SMEM, SMEM] + [VMEM] * 9,
        out_specs=VMEM,
        scratch_shapes=[
            pltpu.VMEM((3, 2, 3 * TS, TS), F32),
            pltpu.VMEM((2, NP, NP), F32),
            pltpu.VMEM((2, NP, NP), F32),
        ],
        compiler_params=params(24),
        cost_estimate=COST,
        name="near_terms",
    )(owners, offsets, before, own, after, probe, wave, *mats)


def far_terms(t, probe, wave, mats):
    return pl.pallas_call(
        far_kernel,
        out_shape=jax.ShapeDtypeStruct((2, NP, NP), F32),
        in_specs=[VMEM] * 7,
        out_specs=VMEM,
        compiler_params=params(24),
        cost_estimate=COST,
        name="far_terms",
    )(t, probe, wave, *mats)


def split_kernel(offsets, mine, others, before, own, after):
    side = lax.axis_index("slab")
    step = 32
    spot = lanes(step)
    for k, terms in ((0, mine), (1, others)):
        p = side if k == 0 else 1 - side
        c = offsets[0, p, 1]
        for at in range(0, NP, step):
            for part in range(2):
                low = pltpu.roll(terms[part, at : at + step, 0:TS].astype(F32), c, 1)
                high = pltpu.roll(terms[part, at : at + step, TS:].astype(F32), c, 1)
                place = (pl.ds(p * NP + at, step), slice(part * TS, (part + 1) * TS))
                before[place] = jnp.where(spot >= c, low, 0.0).astype(BF16)
                own[place] = jnp.where(spot < c, low, high)
                after[place] = jnp.where(spot < c, high, 0.0).astype(BF16)


def split_terms(offsets, mine, others):
    shape = (POS * NP, 2 * TS)
    return pl.pallas_call(
        split_kernel,
        out_shape=[
            jax.ShapeDtypeStruct(shape, BF16),
            jax.ShapeDtypeStruct(shape, F32),
            jax.ShapeDtypeStruct(shape, BF16),
        ],
        in_specs=[SMEM, VMEM, VMEM],
        out_specs=[VMEM] * 3,
        compiler_params=params(8),
        name="split_terms",
    )(offsets, mine, others)


def take_off(terms, slot, row, stack, out):
    for p in range(POS):
        for part in range(2):
            cols = slice(part * TS, (part + 1) * TS)
            stack[part, TS : TS + NP, :] = terms[p * NP : (p + 1) * NP, cols].astype(F32) * step_rate
        r = row(p)
        for i in range(3):
            for part in range(2):
                cols = slice(part * TS, (part + 1) * TS)
                out[0, slot(p, i), :, cols] -= stack[part, pl.ds(TS + i * TS - r, TS), :]


def clear(stack):
    stack[:, 0:TS, :] = jnp.zeros((2, TS, TS), F32)
    stack[:, TS + NP :, :] = jnp.zeros((2, TS, TS), F32)


def own_kernel(owners, offsets, tiles, terms, out, stack):
    clear(stack)
    out[...] = tiles[...]
    take_off(terms, lambda p, i: owners[0, p, 3 * i + 1] & (CAP - 1), lambda p: offsets[0, p, 0], stack, out)


def own_update(owners, offsets, tiles, terms):
    return pl.pallas_call(
        own_kernel,
        out_shape=jax.ShapeDtypeStruct(tiles.shape, F32),
        in_specs=[SMEM, SMEM, VMEM, VMEM],
        out_specs=VMEM,
        scratch_shapes=[pltpu.VMEM((2, 2 * TS + NP, TS), F32)],
        compiler_params=params(8),
        cost_estimate=pl.CostEstimate(flops=1_000_000, bytes_accessed=3_000_000, transcendentals=0),
        name="own_update",
    )(owners, offsets, tiles, terms)


def last_kernel(notes_left, notes_right, tiles, from_left, from_right, out, stack):
    clear(stack)
    out[...] = tiles[...]
    take_off(from_right, lambda p, i: notes_right[0, p * 16 + 3 * i], lambda p: notes_right[0, p * 16 + 9], stack, out)
    take_off(from_left, lambda p, i: notes_left[0, p * 16 + 3 * i + 2], lambda p: notes_left[0, p * 16 + 9], stack, out)


def last_update(notes_left, notes_right, tiles, from_left, from_right):
    return pl.pallas_call(
        last_kernel,
        out_shape=jax.ShapeDtypeStruct(tiles.shape, F32),
        in_specs=[SMEM, SMEM, VMEM, VMEM, VMEM],
        out_specs=VMEM,
        scratch_shapes=[pltpu.VMEM((2, 2 * TS + NP, TS), F32)],
        compiler_params=params(8),
        name="last_update",
    )(notes_left, notes_right, tiles, from_left, from_right)


def along(value, distance):
    count = lax.axis_size("scan")
    return lax.ppermute(value, "scan", [(i, (i + distance) % count) for i in range(count)])


def across(value):
    return lax.ppermute(value, "slab", [(0, 1), (1, 0)])


def shards(probe_modes, tap_weights, object_slices, exit_residual, offsets, owners):
    side = lax.axis_index("slab").astype(jnp.int32).reshape(1)
    own = pack(owners, offsets, object_slices)
    before, after = along(own, 1), along(own, -1)
    *mats, wave = exit_adjoint(side, tap_weights, exit_residual)
    t_there = far_window(owners, offsets, before, own, after)
    t_here = across(t_there)
    terms_there = near_terms(owners, offsets, before, own, after, probe_modes, wave, mats)
    terms_far = across(terms_there)
    terms_here = far_terms(t_here, probe_modes, wave, mats)
    to_left, kept, to_right = split_terms(offsets, terms_here, terms_far)
    from_right, from_left = along(to_left, -1), along(to_right, 1)
    partly = own_update(owners, offsets, object_slices, kept)
    notes_left = before[ROWS : ROWS + 1, : 2 * 16].astype(jnp.int32)
    notes_right = after[ROWS : ROWS + 1, : 2 * 16].astype(jnp.int32)
    return last_update(notes_left, notes_right, partly, from_left, from_right)


def solution(mesh):
    placed = (
        P(),
        P(),
        P("slab", "scan", None, None),
        P("scan", None, None, None, None),
        P("scan", None, None),
        P("scan", None, None),
    )
    return jax.shard_map(
        shards, mesh=mesh, in_specs=placed, out_specs=P("slab", "scan", None, None), check_vma=False
    )
```

time: 130 us -> 55.6 us (0.43)
  the two profiles are of different devices: /device:TPU:0 before, /device:TPU:1 now
where the time goes in v1:
time: 55.6 us; the launch traced here: 55.4 us
  starting transfers between devices  20.1 us (36%)
  waiting for transfers between devices  19.1 us (34%)
  Pallas kernels  11.2 us (20%)
  local copies, waits for them, and re-layouts  4.87 us (9%)
    ppermute x4, waiting for transfers between devices, along(): lax.ppermute(value, 'scan', [(i, (i + distance) % count) for i in range(c...  19.1 us
    ppermute x4, starting transfers between devices, along(): lax.ppermute(value, 'scan', [(i, (i + distance) % count) for i in range(c...  18.1 us
    unnamed x18, local copies, waits for them, and re-layouts  4.87 us
    pallas_call x1, Pallas kernels, near_terms(): pl.pallas_call(near_kernel, out_shape=jax.ShapeDtypeStruct((2, NP, NP), B...  2.79 us
    ppermute x2, starting transfers between devices, across(): return lax.ppermute(value, 'slab', [(0, 1), (1, 0)])  2.04 us
    pallas_call x1, Pallas kernels, last_update(): pl.pallas_call(last_kernel, out_shape=jax.ShapeDtypeStruct(tiles.shape, F...  1.89 us
    pallas_call x1, Pallas kernels, far_terms(): pl.pallas_call(far_kernel, out_shape=jax.ShapeDtypeStruct((2, NP, NP), F3...  1.78 us
    pallas_call x1, Pallas kernels, exit_adjoint(): pl.pallas_call(lambda side, *refs: exit_kernel(*refs), grid_spec=pltpu.Pr...  1.73 us
  transfers between devices with their start and end apart: 6, of which 3 were waited for; matrix products, arithmetic and copies ran while one was open for 0% of the time, Pallas kernels for 13%

profile of v1, /device:TPU:1, one launch (start us, length us, event | category | flops | bytes accessed | tf_op | source)
XLA Modules:
  0.0 55.4 jit_solution(4515835954575189815)
XLA Ops:
  0.0 0.0 copy-start.1
  0.0 1.2 %copy-done.1 = f32[1,8,128,256]{3,2,1,0:T(8,128)S(1)} copy-done((f32[1,8,128,256]{3,2,1,0:T(8,128)S(1)}, f32[1,8,128,256]{3,2,1,0:T(8,128)}, u32[]{:S(2)}) %copy-start.1) | copy-done | bytes 1048600
  1.2 0.0 copy-start.3
  1.2 0.7 %copy-done.3 = s32[1,2,2]{2,1,0:T(2,128)S(1)} copy-done((s32[1,2,2]{2,1,0:T(2,128)S(1)}, s32[1,2,2]{2,1,0:T(2,128)}, u32[]{:S(2)}) %copy-start.3) | copy-done | bytes 40
  1.9 0.0 copy-start.5
  1.9 0.7 %copy-done.5 = s32[1,2,9]{2,1,0:T(2,128)S(1)} copy-done((s32[1,2,9]{2,1,0:T(2,128)S(1)}, s32[1,2,9]{2,1,0:T(2,128)}, u32[]{:S(2)}) %copy-start.5) | copy-done | bytes 96
  2.6 0.6 %pack_tiles.1.own = bf16[1040,256]{1,0:T(8,128)(2,1)S(1)} custom-call(s32[1,2,9]{2,1,0:T(2,128)S(1)} %copy-done.5, s32[1,2,2]{2,1,0:T(2,128)S(1)} %copy-done.3, f32[1,8,128,256]{3,2,1,0:T(8,128)S(1)} %copy-done.1), custom_call_target="tpu_custom_call" | custom-call | tf_op jit(solution)/shard_map/pack_tiles/pallas_call | solution.py:44
  3.2 0.0 copy-start.4
  3.2 0.0 copy-start.6
  3.2 11.1 %collective-permute-start.1 = (bf16[1040,256]{1,0:T(8,128)(2,1)S(1)}, bf16[1040,256]{1,0:T(8,128)(2,1)S(1)}, u32[]{:S(2)}, u32[]{:S(2)}) collective-permute-start(bf16[1040,256]{1,0:T(8,128)(2,1)S(1)} %pack_tiles.1.own), channel_id=1, source_target_pairs={{0,127},{1,0},{2,1},{3,2},{4,3},{5,4},{6,5},{7,6},{8,7},{9,8},{10,... | collective-permute-start | bytes 1597448 | tf_op jit(solution)/shard_map/ppermute | solution.py:330
  14.4 0.0 collective-permute-start
  14.4 0.0 copy-start.7
  14.4 1.6 %copy-done.7 = bf16[1,2,4,256,512]{4,3,2,1,0:T(8,128)(2,1)S(1)} copy-done((bf16[1,2,4,256,512]{4,3,2,1,0:T(8,128)(2,1)S(1)}, bf16[1,2,4,256,512]{4,3,2,1,0:T(8,128)(2,1)}, u32[]{:S(2)}) %copy-start.7) | copy-done | bytes 2097176
  16.0 0.0 copy-start.8
  16.0 0.7 %copy-done.8 = bf16[2,2,31]{2,1,0:T(2,128)(2,1)S(1)} copy-done((bf16[2,2,31]{2,1,0:T(2,128)(2,1)S(1)}, bf16[2,2,31]{2,1,0:T(2,128)(2,1)}, u32[]{:S(2)}) %copy-start.8) | copy-done | bytes 272
  16.6 0.0 copy-start
  16.6 1.7 %exit_adjoint.1 = (bf16[512,512]{1,0:T(8,128)(2,1)S(1)}, bf16[512,512]{1,0:T(8,128)(2,1)S(1)}, bf16[512,512]{1,0:T(8,128)(2,1)S(1)}, bf16[512,512]{1,0:T(8,128)(2,1)S(1)}, bf16[4,512,256]{2,1,0:T(8,128)(2,1)S(1)}) custom-call(s32[1]{0:T(128)} %bitcast.side, bf16[2,2,31]{2,1,0:T(2,128)(2,1)S(1)} %copy-done.8, bf16[1,2,4,256,512]{4,3,2,1,0:T(8,128)(2,1)S(1)} %copy-done.7), custom_call_target="tpu_custom_call" | custom-call | flops 1100000000 | bytes 6000000 | tf_op jit(solution)/shard_map/exit_adjoint/pallas_call | solution.py:85
  18.4 6.8 %collective-permute-done.1.after = bf16[1040,256]{1,0:T(8,128)(2,1)S(1)} collective-permute-done((bf16[1040,256]{1,0:T(8,128)(2,1)S(1)}, bf16[1040,256]{1,0:T(8,128)(2,1)S(1)}, u32[]{:S(2)}, u32[]{:S(2)}) %collective-permute-start.1) | collective-permute-done | bytes 532512 | tf_op jit(solution)/shard_map/ppermute | solution.py:330
  25.1 7.3 %collective-permute-done.before = bf16[1040,256]{1,0:T(8,128)(2,1)S(1)} collective-permute-done((bf16[1040,256]{1,0:T(8,128)(2,1)S(1)}, bf16[1040,256]{1,0:T(8,128)(2,1)S(1)}, u32[]{:S(2)}, u32[]{:S(2)}) %collective-permute-start) | collective-permute-done | bytes 532512 | tf_op jit(solution)/shard_map/ppermute | solution.py:330
  32.4 0.0 copy-done.4
  32.4 0.0 copy-done.6
  32.4 0.8 %far_window.1 = bf16[2,256,256]{2,1,0:T(8,128)(2,1)S(1)} custom-call(s32[1,2,9]{2,1,0:T(2,128)S(1)} %copy-done.6, s32[1,2,2]{2,1,0:T(2,128)S(1)} %copy-done.4, bf16[1040,256]{1,0:T(8,128)(2,1)S(1)} %collective-permute-done.before, bf16[1040,256]{1,0:T(8,128)(2,1)S(1)} %pack_tiles.1.own, bf16[1040,256]{1,0:T(8,128)(2,1)S(1)} %collective-permute-done.1.after), custom_call_target="tpu_custom_call" | custom-call | flops 1000000 | bytes 2000000 | tf_op jit(solution)/shard_map/far_window/pallas_call | solution.py:129
  33.3 2.0 %collective-permute-start.2 = (bf16[2,256,256]{2,1,0:T(8,128)(2,1)S(1)}, bf16[2,256,256]{2,1,0:T(8,128)(2,1)S(1)}, u32[]{:S(2)}, u32[]{:S(2)}) collective-permute-start(bf16[2,256,256]{2,1,0:T(8,128)(2,1)S(1)} %far_window.1), channel_id=1, source_target_pairs={{0,128},{128,0},{1,129},{129,1},{2,130},{130,2},{3,131},{131,3},{4... | collective-permute-start | bytes 786440 | tf_op jit(solution)/shard_map/ppermute | solution.py:334
  35.2 0.0 copy-done
  35.2 2.8 %near_terms.1 = bf16[2,256,256]{2,1,0:T(8,128)(2,1)S(1)} custom-call(s32[1,2,9]{2,1,0:T(2,128)S(1)} %copy-done.6, s32[1,2,2]{2,1,0:T(2,128)S(1)} %copy-done.4, bf16[1040,256]{1,0:T(8,128)(2,1)S(1)} %collective-permute-done.before, bf16[1040,256]{1,0:T(8,128)(2,1)S(1)} %pack_tiles.1.own, bf16[1040,256]{1,0:T(8,128)(2,1)S(1)} %collective-permute-done.1.after, ...), custom_call_target="tpu_custom_call" | custom-call | flops 1100000000 | bytes 5000000 | tf_op jit(solution)/shard_map/near_terms/pallas_call | solution.py:212
  38.0 0.0 copy-start.2
  38.0 0.1 collective-permute-start.3
  38.1 0.0 collective-permute-done.2.t
  38.2 1.8 %far_terms.1.mine = f32[2,256,256]{2,1,0:T(8,128)S(1)} custom-call(bf16[2,256,256]{2,1,0:T(8,128)(2,1)S(1)} %collective-permute-done.2.t, bf16[4,256,512]{2,1,0:T(8,128)(2,1)S(1)} %copy-done, bf16[4,512,256]{2,1,0:T(8,128)(2,1)S(1)} %get-tuple-element.13.wave, bf16[512,512]{1,0:T(8,128)(2,1)S(1)} %get-tuple-element.14.left, ...), custom_call_target="tpu_custom_call" | custom-call | flops 1100000000 | bytes 5000000 | tf_op jit(solution)/shard_map/far_terms/pallas_call | solution.py:229
  39.9 0.0 collective-permute-done.3.others
  39.9 0.8 %split_terms.1 = (bf16[512,256]{1,0:T(8,128)(2,1)S(1)}, f32[512,256]{1,0:T(8,128)S(1)}, bf16[512,256]{1,0:T(8,128)(2,1)S(1)}) custom-call(s32[1,2,2]{2,1,0:T(2,128)S(1)} %copy-done.4, f32[2,256,256]{2,1,0:T(8,128)S(1)} %far_terms.1.mine, bf16[2,256,256]{2,1,0:T(8,128)(2,1)S(1)} %collective-permute-done.3.others), custom_call_target="tpu_custom_call" | custom-call | tf_op jit(solution)/shard_map/split_terms/pallas_call | solution.py:259
  40.8 0.1 collective-permute-start.4
  40.9 6.9 %collective-permute-start.5 = (bf16[512,256]{1,0:T(8,128)(2,1)S(1)}, bf16[512,256]{1,0:T(8,128)(2,1)S(1)}, u32[]{:S(2)}, u32[]{:S(2)}) collective-permute-start(bf16[512,256]{1,0:T(8,128)(2,1)S(1)} %get-tuple-element.20), channel_id=1, source_target_pairs={{0,127},{1,0},{2,1},{3,2},{4,3},{5,4},{6,5},{7,6},{8,7},{9,8},{10,... | collective-permute-start | bytes 786440 | tf_op jit(solution)/shard_map/ppermute | solution.py:330
  47.8 0.0 copy-done.2
  47.8 0.8 %own_update.1.tiles = f32[1,8,128,256]{3,2,1,0:T(8,128)S(1)} custom-call(s32[1,2,9]{2,1,0:T(2,128)S(1)} %copy-done.6, s32[1,2,2]{2,1,0:T(2,128)S(1)} %copy-done.4, f32[1,8,128,256]{3,2,1,0:T(8,128)S(1)} %copy-done.2, f32[512,256]{1,0:T(8,128)S(1)} %get-tuple-element.18.terms), custom_call_target="tpu_custom_call" | custom-call | flops 1000000 | bytes 3000000 | tf_op jit(solution)/shard_map/own_update/pallas_call | solution.py:297
  48.5 5.0 %collective-permute-done.4.from_left = bf16[512,256]{1,0:T(8,128)(2,1)S(1)} collective-permute-done((bf16[512,256]{1,0:T(8,128)(2,1)S(1)}, bf16[512,256]{1,0:T(8,128)(2,1)S(1)}, u32[]{:S(2)}, u32[]{:S(2)}) %collective-permute-start.4) | collective-permute-done | bytes 262176 | tf_op jit(solution)/shard_map/ppermute | solution.py:330
  53.5 0.0 collective-permute-done.5.from_right
  53.5 1.9 %last_update.1 = f32[1,8,128,256]{3,2,1,0:T(8,128)} custom-call(s32[1,32]{1,0:T(1,128)S(1)} %slice_convert_fusion.1.notes_left, s32[1,32]{1,0:T(1,128)S(1)} %slice_convert_fusion.notes_right, f32[1,8,128,256]{3,2,1,0:T(8,128)S(1)} %own_update.1.tiles, bf16[512,256]{1,0:T(8,128)(2,1)S(1)} %collective-permute-done.4.from_left, ...), custom_call_target="tpu_custom_call" | custom-call | tf_op jit(solution)/shard_map/last_update/pallas_call | solution.py:317
  (2 shorter events, 0.0 us)
Async XLA Ops:
  0.0 1.2 %copy-start.1 = (f32[1,8,128,256]{3,2,1,0:T(8,128)S(1)}, f32[1,8,128,256]{3,2,1,0:T(8,128)}, u32[]{:S(2)}) copy-start(f32[1,8,128,256]{3,2,1,0:T(8,128)} %tiles.3) | copy-start | bytes 3145732
  1.2 0.7 %copy-start.3 = (s32[1,2,2]{2,1,0:T(2,128)S(1)}, s32[1,2,2]{2,1,0:T(2,128)}, u32[]{:S(2)}) copy-start(s32[1,2,2]{2,1,0:T(2,128)} %offsets.9) | copy-start | bytes 52
  1.9 0.7 %copy-start.5 = (s32[1,2,9]{2,1,0:T(2,128)S(1)}, s32[1,2,9]{2,1,0:T(2,128)}, u32[]{:S(2)}) copy-start(s32[1,2,9]{2,1,0:T(2,128)} %owners.7) | copy-start | bytes 220
  3.2 29.2 %copy-start.4 = (s32[1,2,2]{2,1,0:T(2,128)S(1)}, s32[1,2,2]{2,1,0:T(2,128)}, u32[]{:S(2)}) copy-start(s32[1,2,2]{2,1,0:T(2,128)} %offsets.9) | copy-start | bytes 52
  3.2 29.2 %copy-start.6 = (s32[1,2,9]{2,1,0:T(2,128)S(1)}, s32[1,2,9]{2,1,0:T(2,128)}, u32[]{:S(2)}) copy-start(s32[1,2,9]{2,1,0:T(2,128)} %owners.7) | copy-start | bytes 220
  3.2 21.9 %collective-permute-start.1 = (bf16[1040,256]{1,0:T(8,128)(2,1)S(1)}, bf16[1040,256]{1,0:T(8,128)(2,1)S(1)}, u32[]{:S(2)}, u32[]{:S(2)}) collective-permute-start(bf16[1040,256]{1,0:T(8,128)(2,1)S(1)} %pack_tiles.1.own), channel_id=1, source_target_pairs={{0,127},{1,0},{2,1},{3,2},{4,3},{5,4},{6,5},{7,6},{8,7},{9,8},{10,... | collective-permute-start | bytes 1597448 | tf_op jit(solution)/shard_map/ppermute | solution.py:330
  14.4 18.1 %collective-permute-start = (bf16[1040,256]{1,0:T(8,128)(2,1)S(1)}, bf16[1040,256]{1,0:T(8,128)(2,1)S(1)}, u32[]{:S(2)}, u32[]{:S(2)}) collective-permute-start(bf16[1040,256]{1,0:T(8,128)(2,1)S(1)} %pack_tiles.1.own), channel_id=1, source_target_pairs={{0,1},{1,2},{2,3},{3,4},{4,5},{5,6},{6,7},{7,8},{8,9},{9,10},{10,1... | collective-permute-start | bytes 1597448 | tf_op jit(solution)/shard_map/ppermute | solution.py:330
  14.4 1.6 %copy-start.7 = (bf16[1,2,4,256,512]{4,3,2,1,0:T(8,128)(2,1)S(1)}, bf16[1,2,4,256,512]{4,3,2,1,0:T(8,128)(2,1)}, u32[]{:S(2)}) copy-start(bf16[1,2,4,256,512]{4,3,2,1,0:T(8,128)(2,1)} %refs_1_.1) | copy-start | bytes 6291460
  16.0 0.7 %copy-start.8 = (bf16[2,2,31]{2,1,0:T(2,128)(2,1)S(1)}, bf16[2,2,31]{2,1,0:T(2,128)(2,1)}, u32[]{:S(2)}) copy-start(bf16[2,2,31]{2,1,0:T(2,128)(2,1)} %refs_0_.1) | copy-start | bytes 748
  16.6 18.6 %copy-start = (bf16[4,256,512]{2,1,0:T(8,128)(2,1)S(1)}, bf16[4,256,512]{2,1,0:T(8,128)(2,1)}, u32[]{:S(2)}) copy-start(bf16[4,256,512]{2,1,0:T(8,128)(2,1)} %probe.3) | copy-start | bytes 3145732
  33.3 4.9 %collective-permute-start.2 = (bf16[2,256,256]{2,1,0:T(8,128)(2,1)S(1)}, bf16[2,256,256]{2,1,0:T(8,128)(2,1)S(1)}, u32[]{:S(2)}, u32[]{:S(2)}) collective-permute-start(bf16[2,256,256]{2,1,0:T(8,128)(2,1)S(1)} %far_window.1), channel_id=1, source_target_pairs={{0,128},{128,0},{1,129},{129,1},{2,130},{130,2},{3,131},{131,3},{4... | collective-permute-start | bytes 786440 | tf_op jit(solution)/shard_map/ppermute | solution.py:334
  38.0 9.7 %copy-start.2 = (f32[1,8,128,256]{3,2,1,0:T(8,128)S(1)}, f32[1,8,128,256]{3,2,1,0:T(8,128)}, u32[]{:S(2)}) copy-start(f32[1,8,128,256]{3,2,1,0:T(8,128)} %tiles.3) | copy-start | bytes 3145732
  38.0 1.9 %collective-permute-start.3 = (bf16[2,256,256]{2,1,0:T(8,128)(2,1)S(1)}, bf16[2,256,256]{2,1,0:T(8,128)(2,1)S(1)}, u32[]{:S(2)}, u32[]{:S(2)}) collective-permute-start(bf16[2,256,256]{2,1,0:T(8,128)(2,1)S(1)} %near_terms.1), channel_id=1, source_target_pairs={{0,128},{128,0},{1,129},{129,1},{2,130},{130,2},{3,131},{131,3},{4... | collective-permute-start | bytes 786440 | tf_op jit(solution)/shard_map/ppermute | solution.py:334
  40.8 12.7 %collective-permute-start.4 = (bf16[512,256]{1,0:T(8,128)(2,1)S(1)}, bf16[512,256]{1,0:T(8,128)(2,1)S(1)}, u32[]{:S(2)}, u32[]{:S(2)}) collective-permute-start(bf16[512,256]{1,0:T(8,128)(2,1)S(1)} %get-tuple-element.19), channel_id=1, source_target_pairs={{0,1},{1,2},{2,3},{3,4},{4,5},{5,6},{6,7},{7,8},{8,9},{9,10},{10,1... | collective-permute-start | bytes 786440 | tf_op jit(solution)/shard_map/ppermute | solution.py:330
  40.9 12.7 %collective-permute-start.5 = (bf16[512,256]{1,0:T(8,128)(2,1)S(1)}, bf16[512,256]{1,0:T(8,128)(2,1)S(1)}, u32[]{:S(2)}, u32[]{:S(2)}) collective-permute-start(bf16[512,256]{1,0:T(8,128)(2,1)S(1)} %get-tuple-element.20), channel_id=1, source_target_pairs={{0,127},{1,0},{2,1},{3,2},{4,3},{5,4},{6,5},{7,6},{8,7},{9,8},{10,... | collective-permute-start | bytes 786440 | tf_op jit(solution)/shard_map/ppermute | solution.py:330

commit v2 on v1

--- a/solution.py
+++ b/solution.py
@@ -11,9 +11,11 @@
 F32, BF16 = jnp.float32, jnp.bfloat16
 NP, TS, HALF = 256, 128, 15
 MODES, POS, CAP = 4, 2, 8
+STEP = 32
 ROWS = CAP * TS
 SMEM = pl.BlockSpec(memory_space=pltpu.SMEM)
 VMEM = pl.BlockSpec(memory_space=pltpu.VMEM)
+HBM = pl.BlockSpec(memory_space=pltpu.HBM)
 
 
 def params(mib):
@@ -28,9 +30,21 @@
     return lax.broadcasted_iota(jnp.int32, (rows, TS), 1)
 
 
-def pack_kernel(owners, offsets, tiles, out):
+def pack_kernel(owners_hbm, offsets_hbm, tiles_hbm, out, owners, offsets, tiles, small, large):
+    copies = [pltpu.make_async_copy(tiles_hbm.at[0, q], tiles.at[q], large.at[q]) for q in range(CAP)]
+    for copy in copies:
+        copy.start()
+    notes_in = [
+        pltpu.make_async_copy(owners_hbm, owners, small.at[0]),
+        pltpu.make_async_copy(offsets_hbm, offsets, small.at[1]),
+    ]
+    for copy in notes_in:
+        copy.start()
     for q in range(CAP):
-        out[q * TS : (q + 1) * TS, :] = tiles[0, q].astype(BF16)
+        copies[q].wait()
+        out[q * TS : (q + 1) * TS, :] = tiles[q].astype(BF16)
+    for copy in notes_in:
+        copy.wait()
     spot = lax.broadcasted_iota(jnp.int32, (16, 2 * TS), 1)
     notes = jnp.zeros((16, 2 * TS), jnp.int32)
     for p in range(POS):
@@ -44,9 +58,16 @@
     return pl.pallas_call(
         pack_kernel,
         out_shape=jax.ShapeDtypeStruct((ROWS + 16, 2 * TS), BF16),
-        in_specs=[SMEM, SMEM, VMEM],
-        out_specs=VMEM,
-        compiler_params=params(8),
+        in_specs=[HBM] * 3,
+        out_specs=VMEM,
+        scratch_shapes=[
+            pltpu.SMEM(owners.shape, jnp.int32),
+            pltpu.SMEM(offsets.shape, jnp.int32),
+            pltpu.VMEM((CAP, TS, 2 * TS), F32),
+            pltpu.SemaphoreType.DMA((2,)),
+            pltpu.SemaphoreType.DMA((CAP,)),
+        ],
+        compiler_params=params(62),
         name="pack_tiles",
     )(owners, offsets, tiles)
 
@@ -102,40 +123,91 @@
     )(side, taps, residual)
 
 
-def cut_window(p, owners, offsets, sources, stack, out):
+def early_side():
+    return 1 - lax.axis_index("scan") % 2
+
+
+def cut_column(p, j, owners, offsets, tiles, stack, put):
+    for i in range(3):
+        q = owners[0, p, 3 * i + j] & (CAP - 1)
+        tile = tiles[pl.ds(pl.multiple_of(q * TS, TS), TS), :].astype(F32)
+        stack[0, i * TS : (i + 1) * TS, :] = tile[:, :TS]
+        stack[1, i * TS : (i + 1) * TS, :] = tile[:, TS:]
     r, c = offsets[0, p, 0], offsets[0, p, 1]
-    for j, tiles in enumerate(sources):
-        for i in range(3):
-            q = owners[0, p, 3 * i + j] & (CAP - 1)
-            tile = tiles[pl.ds(pl.multiple_of(q * TS, TS), TS), :].astype(F32)
-            stack[j, 0, i * TS : (i + 1) * TS, :] = tile[:, :TS]
-            stack[j, 1, i * TS : (i + 1) * TS, :] = tile[:, TS:]
     back = (TS - c) & (TS - 1)
-    step = 32
-    near = lanes(step) < TS - c
-    for at in range(0, NP, step):
+    for at in range(0, NP, STEP):
         for part in range(2):
-            cols = [pltpu.roll(stack[j, part, pl.ds(r + at, step), :], back, 1) for j in range(3)]
-            out[part, at : at + step, 0:TS] = jnp.where(near, cols[0], cols[1]).astype(out.dtype)
-            out[part, at : at + step, TS:] = jnp.where(near, cols[1], cols[2]).astype(out.dtype)
-
-
-def window_kernel(owners, offsets, before, own, after, out, stack):
-    p = 1 - lax.axis_index("slab")
-    cut_window(p, owners, offsets, (before, own, after), stack, out)
-
-
-def far_window(owners, offsets, before, own, after):
+            put(part, at, pltpu.roll(stack[part, pl.ds(r + at, STEP), :], back, 1))
+
+
+def half(side):
+    return pl.ds(pl.multiple_of(side * TS, TS), TS)
+
+
+def taken(side, c):
+    past = lanes(STEP) - (TS - c)
+    return past * (1 - 2 * side) - side < 0
+
+
+def early_kernel(owners, offsets, own, early, out, stack):
+    side = early_side()
+    for p in range(POS):
+
+        def put_own(part, at, turned):
+            out[p, part, at : at + STEP, :TS] = turned
+            out[p, part, at : at + STEP, TS:] = turned
+
+        cut_column(p, 1, owners, offsets, own, stack.at[0], put_own)
+        mask = taken(side, offsets[0, p, 1])
+
+        def put_early(part, at, turned):
+            place = (p, part, slice(at, at + STEP), half(side))
+            out[place] = jnp.where(mask, turned, out[place])
+
+        cut_column(p, 2 * side, owners, offsets, early, stack.at[1], put_early)
+
+
+def early_windows(owners, offsets, own, early):
+    return pl.pallas_call(
+        early_kernel,
+        out_shape=jax.ShapeDtypeStruct((POS, 2, NP, NP), F32),
+        in_specs=[SMEM, SMEM, VMEM, VMEM],
+        out_specs=VMEM,
+        scratch_shapes=[pltpu.VMEM((2, 2, 3 * TS, TS), F32)],
+        compiler_params=params(8),
+        cost_estimate=pl.CostEstimate(flops=2_000_000, bytes_accessed=2_000_000, transcendentals=0),
+        name="early_windows",
+    )(owners, offsets, own, early)
+
+
+def complete(p, owners, offsets, late, partly, stack, out):
+    side = 1 - early_side()
+    mask = taken(side, offsets[0, p, 1])
+
+    def put(part, at, turned):
+        rows = slice(at, at + STEP)
+        kept = partly[p, part, rows, half(side)]
+        out[part, rows, half(side)] = jnp.where(mask, turned, kept).astype(out.dtype)
+        out[part, rows, half(1 - side)] = partly[p, part, rows, half(1 - side)].astype(out.dtype)
+
+    cut_column(p, 2 * side, owners, offsets, late, stack, put)
+
+
+def window_kernel(owners, offsets, late, partly, out, stack):
+    complete(1 - lax.axis_index("slab"), owners, offsets, late, partly, stack, out)
+
+
+def far_window(owners, offsets, late, partly):
     return pl.pallas_call(
         window_kernel,
         out_shape=jax.ShapeDtypeStruct((2, NP, NP), BF16),
-        in_specs=[SMEM, SMEM, VMEM, VMEM, VMEM],
-        out_specs=VMEM,
-        scratch_shapes=[pltpu.VMEM((3, 2, 3 * TS, TS), F32)],
+        in_specs=[SMEM, SMEM, VMEM, VMEM],
+        out_specs=VMEM,
+        scratch_shapes=[pltpu.VMEM((2, 3 * TS, TS), F32)],
         compiler_params=params(8),
         cost_estimate=pl.CostEstimate(flops=1_000_000, bytes_accessed=2_000_000, transcendentals=0),
         name="far_window",
-    )(owners, offsets, before, own, after)
+    )(owners, offsets, late, partly)
 
 
 def times(a, b, conjugate):
@@ -193,9 +265,9 @@
         upper_terms(t, probe, wave, left_adj, right_adj, total)
 
 
-def near_kernel(owners, offsets, before, own, after, probe, wave, left, left_adj, right, right_adj, out, stack, t, total):
+def near_kernel(owners, offsets, late, partly, probe, wave, left, left_adj, right, right_adj, out, stack, t, total):
     side = lax.axis_index("slab")
-    cut_window(side, owners, offsets, (before, own, after), stack, t)
+    complete(side, owners, offsets, late, partly, stack, t)
     both_ways(side, t, probe, wave, left, left_adj, right, right_adj, total)
     out[...] = total[...].astype(BF16)
 
@@ -208,21 +280,21 @@
 COST = pl.CostEstimate(flops=1_100_000_000, bytes_accessed=5_000_000, transcendentals=0)
 
 
-def near_terms(owners, offsets, before, own, after, probe, wave, mats):
+def near_terms(owners, offsets, late, partly, probe, wave, mats):
     return pl.pallas_call(
         near_kernel,
         out_shape=jax.ShapeDtypeStruct((2, NP, NP), BF16),
-        in_specs=[SMEM, SMEM] + [VMEM] * 9,
+        in_specs=[SMEM, SMEM] + [VMEM] * 8,
         out_specs=VMEM,
         scratch_shapes=[
-            pltpu.VMEM((3, 2, 3 * TS, TS), F32),
+            pltpu.VMEM((2, 3 * TS, TS), F32),
             pltpu.VMEM((2, NP, NP), F32),
             pltpu.VMEM((2, NP, NP), F32),
         ],
         compiler_params=params(24),
         cost_estimate=COST,
         name="near_terms",
-    )(owners, offsets, before, own, after, probe, wave, *mats)
+    )(owners, offsets, late, partly, probe, wave, *mats)
 
 
 def far_terms(t, probe, wave, mats):
@@ -237,21 +309,23 @@
     )(t, probe, wave, *mats)
 
 
-def split_kernel(offsets, mine, others, before, own, after):
-    side = lax.axis_index("slab")
-    step = 32
-    spot = lanes(step)
+def split_kernel(offsets, mine, others, early, own, late):
+    here = lax.axis_index("slab")
+    to_right = early_side() == 1
+    spot = lanes(STEP)
     for k, terms in ((0, mine), (1, others)):
-        p = side if k == 0 else 1 - side
+        p = here if k == 0 else 1 - here
         c = offsets[0, p, 1]
-        for at in range(0, NP, step):
+        for at in range(0, NP, STEP):
             for part in range(2):
-                low = pltpu.roll(terms[part, at : at + step, 0:TS].astype(F32), c, 1)
-                high = pltpu.roll(terms[part, at : at + step, TS:].astype(F32), c, 1)
-                place = (pl.ds(p * NP + at, step), slice(part * TS, (part + 1) * TS))
-                before[place] = jnp.where(spot >= c, low, 0.0).astype(BF16)
+                low = pltpu.roll(terms[part, at : at + STEP, 0:TS].astype(F32), c, 1)
+                high = pltpu.roll(terms[part, at : at + STEP, TS:].astype(F32), c, 1)
+                place = (pl.ds(p * NP + at, STEP), slice(part * TS, (part + 1) * TS))
+                left = jnp.where(spot >= c, low, 0.0)
+                right = jnp.where(spot < c, high, 0.0)
                 own[place] = jnp.where(spot < c, low, high)
-                after[place] = jnp.where(spot < c, high, 0.0).astype(BF16)
+                early[place] = jnp.where(to_right, right, left).astype(BF16)
+                late[place] = jnp.where(to_right, left, right).astype(BF16)
 
 
 def split_terms(offsets, mine, others):
@@ -306,50 +380,65 @@
     )(owners, offsets, tiles, terms)
 
 
-def last_kernel(notes_left, notes_right, tiles, from_left, from_right, out, stack):
+def early_update_kernel(notes, tiles, terms, out, stack):
     clear(stack)
+    j = 2 - 2 * early_side()
     out[...] = tiles[...]
-    take_off(from_right, lambda p, i: notes_right[0, p * 16 + 3 * i], lambda p: notes_right[0, p * 16 + 9], stack, out)
-    take_off(from_left, lambda p, i: notes_left[0, p * 16 + 3 * i + 2], lambda p: notes_left[0, p * 16 + 9], stack, out)
-
-
-def last_update(notes_left, notes_right, tiles, from_left, from_right):
-    return pl.pallas_call(
-        last_kernel,
+    take_off(terms, lambda p, i: notes[0, p * 16 + 3 * i + j], lambda p: notes[0, p * 16 + 9], stack, out)
+
+
+def late_update_kernel(notes, tiles, terms, out, stack):
+    clear(stack)
+    j = 2 * early_side()
+    out[...] = tiles[...]
+    take_off(terms, lambda p, i: notes[0, p * 16 + 3 * i + j], lambda p: notes[0, p * 16 + 9], stack, out)
+
+
+def swap_update(kernel, notes, tiles, terms):
+    return pl.pallas_call(
+        kernel,
         out_shape=jax.ShapeDtypeStruct(tiles.shape, F32),
-        in_specs=[SMEM, SMEM, VMEM, VMEM, VMEM],
+        in_specs=[SMEM, VMEM, VMEM],
         out_specs=VMEM,
         scratch_shapes=[pltpu.VMEM((2, 2 * TS + NP, TS), F32)],
         compiler_params=params(8),
-        name="last_update",
-    )(notes_left, notes_right, tiles, from_left, from_right)
-
-
-def along(value, distance):
+        cost_estimate=pl.CostEstimate(flops=1_000_000, bytes_accessed=3_000_000, transcendentals=0),
+        name="swap_update",
+    )(notes, tiles, terms)
+
+
+def swap(value, first):
     count = lax.axis_size("scan")
-    return lax.ppermute(value, "scan", [(i, (i + distance) % count) for i in range(count)])
+    pairs = [(i, (i + 1) % count) for i in range(first, count, 2)]
+    return lax.ppermute(value, "scan", pairs + [(j, i) for i, j in pairs])
 
 
 def across(value):
     return lax.ppermute(value, "slab", [(0, 1), (1, 0)])
+
+
+def notes_of(packed):
+    return packed[ROWS : ROWS + 1, : 2 * 16].astype(jnp.int32)
 
 
 def shards(probe_modes, tap_weights, object_slices, exit_residual, offsets, owners):
     side = lax.axis_index("slab").astype(jnp.int32).reshape(1)
     own = pack(owners, offsets, object_slices)
-    before, after = along(own, 1), along(own, -1)
+    late = swap(own, 1)
+    early = swap(own, 0)
     *mats, wave = exit_adjoint(side, tap_weights, exit_residual)
-    t_there = far_window(owners, offsets, before, own, after)
+    partly = early_windows(owners, offsets, own, early)
+    t_there = far_window(owners, offsets, late, partly)
     t_here = across(t_there)
-    terms_there = near_terms(owners, offsets, before, own, after, probe_modes, wave, mats)
+    terms_there = near_terms(owners, offsets, late, partly, probe_modes, wave, mats)
     terms_far = across(terms_there)
     terms_here = far_terms(t_here, probe_modes, wave, mats)
-    to_left, kept, to_right = split_terms(offsets, terms_here, terms_far)
-    from_right, from_left = along(to_left, -1), along(to_right, 1)
-    partly = own_update(owners, offsets, object_slices, kept)
-    notes_left = before[ROWS : ROWS + 1, : 2 * 16].astype(jnp.int32)
-    notes_right = after[ROWS : ROWS + 1, : 2 * 16].astype(jnp.int32)
-    return last_update(notes_left, notes_right, partly, from_left, from_right)
+    early_out, kept, late_out = split_terms(offsets, terms_here, terms_far)
+    late_in = swap(late_out, 1)
+    early_in = swap(early_out, 0)
+    tiles = own_update(owners, offsets, object_slices, kept)
+    tiles = swap_update(early_update_kernel, notes_of(early), tiles, early_in)
+    return swap_update(late_update_kernel, notes_of(late), tiles, late_in)
 
 
 def solution(mesh):

time: 55.6 us -> 48.4 us (0.87)
  waiting for transfers between devices: 19.1 us -> 11 us
  Pallas kernels: 11.2 us -> 14.1 us
  local copies, waits for them, and re-layouts: 4.87 us -> 2.3 us
    ppermute x4, waiting for transfers between devices: 19.1 us -> 11 us  [swap(): return lax.ppermute(value, 'scan', pairs + [(j, i) for i, j in pairs])]
    unnamed x18 -> x14, local copies, waits for them, and re-layouts: 4.87 us -> 2.3 us
    pallas_call x1 -> x3, Pallas kernels: 1.89 us -> 3.48 us  [the longest x2 2.51 us: swap_update(): pl.pallas_call(kernel, out_shape=jax.ShapeDtypeStruct(tiles.shape, F32),...]
    pallas_call x1, Pallas kernels: 0.61 us -> 2.2 us  [pack(): pl.pallas_call(pack_kernel, out_shape=jax.ShapeDtypeStruct((ROWS + 16, 2...]
    ppermute x4, starting transfers between devices: 18.1 us -> 18.9 us  [swap(): return lax.ppermute(value, 'scan', pairs + [(j, i) for i, j in pairs])]
  transfers between devices with their start and end apart: 6 -> 6, of which waited for: 3 -> 2; matrix products, arithmetic and copies ran while one was open for 0% -> 0% of each run, Pallas kernels for 13% -> 18%
where the time goes in v2:
time: 48.4 us; the launch traced here: 48.2 us
  starting transfers between devices  20.6 us (43%)
  Pallas kernels  14.1 us (29%)
  waiting for transfers between devices  11 us (23%)
  local copies, waits for them, and re-layouts  2.3 us (5%)
    ppermute x4, starting transfers between devices, swap(): return lax.ppermute(value, 'scan', pairs + [(j, i) for i, j in pairs])  18.9 us
    ppermute x4, waiting for transfers between devices, swap(): return lax.ppermute(value, 'scan', pairs + [(j, i) for i, j in pairs])  11 us
    pallas_call x1, Pallas kernels, near_terms(): pl.pallas_call(near_kernel, out_shape=jax.ShapeDtypeStruct((2, NP, NP), B...  2.62 us
    pallas_call x2, Pallas kernels, swap_update(): pl.pallas_call(kernel, out_shape=jax.ShapeDtypeStruct(tiles.shape, F32),...  2.51 us
    unnamed x14, local copies, waits for them, and re-layouts  2.3 us
    pallas_call x1, Pallas kernels, pack(): pl.pallas_call(pack_kernel, out_shape=jax.ShapeDtypeStruct((ROWS + 16, 2...  2.2 us
    pallas_call x1, Pallas kernels, far_terms(): pl.pallas_call(far_kernel, out_shape=jax.ShapeDtypeStruct((2, NP, NP), F3...  1.78 us
    pallas_call x1, Pallas kernels, exit_adjoint(): pl.pallas_call(lambda side, *refs: exit_kernel(*refs), grid_spec=pltpu.Pr...  1.73 us
  transfers between devices with their start and end apart: 6, of which 2 were waited for; matrix products, arithmetic and copies ran while one was open for 0% of the time, Pallas kernels for 18%

profile of v2, /device:TPU:1, one launch (start us, length us, event | category | flops | bytes accessed | tf_op | source)
XLA Modules:
  0.0 48.2 jit_solution(13686198287969727187)
XLA Ops:
  0.0 2.2 %pack_tiles.1.own = bf16[1040,256]{1,0:T(8,128)(2,1)} custom-call(s32[1,2,9]{2,1,0:T(2,128)} %owners.7, s32[1,2,2]{2,1,0:T(2,128)} %offsets.9, f32[1,8,128,256]{3,2,1,0:T(8,128)} %tiles.1), custom_call_target="tpu_custom_call" | custom-call | tf_op jit(solution)/shard_map/pack_tiles/pallas_call | solution.py:58
  2.2 0.0 copy-start.2
  2.2 0.0 copy-start.3
  2.2 0.0 copy-start.4
  2.2 2.6 %collective-permute-start.1 = (bf16[1040,256]{1,0:T(8,128)(2,1)}, bf16[1040,256]{1,0:T(8,128)(2,1)S(1)}, u32[]{:S(2)}, u32[]{:S(2)}) collective-permute-start(bf16[1040,256]{1,0:T(8,128)(2,1)} %pack_tiles.1.own), channel_id=1, source_target_pairs={{0,1},{2,3},{4,5},{6,7},{8,9},{10,11},{12,13},{14,15},{16,17},{18,... | collective-permute-start | bytes 1597448 | tf_op jit(solution)/shard_map/ppermute | solution.py:413
  4.8 9.3 %collective-permute-start = (bf16[1040,256]{1,0:T(8,128)(2,1)}, bf16[1040,256]{1,0:T(8,128)(2,1)S(1)}, u32[]{:S(2)}, u32[]{:S(2)}) collective-permute-start(bf16[1040,256]{1,0:T(8,128)(2,1)} %pack_tiles.1.own), channel_id=1, source_target_pairs={{1,2},{3,4},{5,6},{7,8},{9,10},{11,12},{13,14},{15,16},{17,18},{19... | collective-permute-start | bytes 1597448 | tf_op jit(solution)/shard_map/ppermute | solution.py:413
  14.1 0.0 copy-start.5
  14.1 1.6 %copy-done.5 = bf16[1,2,4,256,512]{4,3,2,1,0:T(8,128)(2,1)S(1)} copy-done((bf16[1,2,4,256,512]{4,3,2,1,0:T(8,128)(2,1)S(1)}, bf16[1,2,4,256,512]{4,3,2,1,0:T(8,128)(2,1)}, u32[]{:S(2)}) %copy-start.5) | copy-done | bytes 2097176
  15.7 0.0 copy-start.6
  15.7 0.7 %copy-done.6 = bf16[2,2,31]{2,1,0:T(2,128)(2,1)S(1)} copy-done((bf16[2,2,31]{2,1,0:T(2,128)(2,1)S(1)}, bf16[2,2,31]{2,1,0:T(2,128)(2,1)}, u32[]{:S(2)}) %copy-start.6) | copy-done | bytes 272
  16.4 1.7 %exit_adjoint.1 = (bf16[512,512]{1,0:T(8,128)(2,1)S(1)}, bf16[512,512]{1,0:T(8,128)(2,1)S(1)}, bf16[512,512]{1,0:T(8,128)(2,1)S(1)}, bf16[512,512]{1,0:T(8,128)(2,1)S(1)}, bf16[4,512,256]{2,1,0:T(8,128)(2,1)S(1)}) custom-call(s32[1]{0:T(128)} %bitcast.side, bf16[2,2,31]{2,1,0:T(2,128)(2,1)S(1)} %copy-done.6, bf16[1,2,4,256,512]{4,3,2,1,0:T(8,128)(2,1)S(1)} %copy-done.5), custom_call_target="tpu_custom_call" | custom-call | flops 1100000000 | bytes 6000000 | tf_op jit(solution)/shard_map/exit_adjoint/pallas_call | solution.py:106
  18.1 0.0 copy-start
  18.1 0.0 collective-permute-done.1.early
  18.1 0.0 copy-done.2
  18.2 0.0 copy-done.3
  18.2 0.0 copy-done.4
  18.2 1.0 %early_windows.1.partly = f32[2,2,256,256]{3,2,1,0:T(8,128)S(1)} custom-call(s32[1,2,9]{2,1,0:T(2,128)S(1)} %copy-done.4, s32[1,2,2]{2,1,0:T(2,128)S(1)} %copy-done.3, bf16[1040,256]{1,0:T(8,128)(2,1)S(1)} %copy-done.2, bf16[1040,256]{1,0:T(8,128)(2,1)S(1)} %collective-permute-done.1.early), custom_call_target="tpu_custom_call" | custom-call | flops 2000000 | bytes 2000000 | tf_op jit(solution)/shard_map/early_windows/pallas_call | solution.py:171
  19.1 6.7 %collective-permute-done.late = bf16[1040,256]{1,0:T(8,128)(2,1)S(1)} collective-permute-done((bf16[1040,256]{1,0:T(8,128)(2,1)}, bf16[1040,256]{1,0:T(8,128)(2,1)S(1)}, u32[]{:S(2)}, u32[]{:S(2)}) %collective-permute-start) | collective-permute-done | bytes 532512 | tf_op jit(solution)/shard_map/ppermute | solution.py:413
  25.9 0.7 %far_window.1 = bf16[2,256,256]{2,1,0:T(8,128)(2,1)S(1)} custom-call(s32[1,2,9]{2,1,0:T(2,128)S(1)} %copy-done.4, s32[1,2,2]{2,1,0:T(2,128)S(1)} %copy-done.3, bf16[1040,256]{1,0:T(8,128)(2,1)S(1)} %collective-permute-done.late, f32[2,2,256,256]{3,2,1,0:T(8,128)S(1)} %early_windows.1.partly), custom_call_target="tpu_custom_call" | custom-call | flops 1000000 | bytes 2000000 | tf_op jit(solution)/shard_map/far_window/pallas_call | solution.py:201
  26.6 1.6 %collective-permute-start.2 = (bf16[2,256,256]{2,1,0:T(8,128)(2,1)S(1)}, bf16[2,256,256]{2,1,0:T(8,128)(2,1)S(1)}, u32[]{:S(2)}, u32[]{:S(2)}) collective-permute-start(bf16[2,256,256]{2,1,0:T(8,128)(2,1)S(1)} %far_window.1), channel_id=1, source_target_pairs={{0,128},{128,0},{1,129},{129,1},{2,130},{130,2},{3,131},{131,3},{4... | collective-permute-start | bytes 786440 | tf_op jit(solution)/shard_map/ppermute | solution.py:417
  28.2 0.0 copy-done
  28.2 2.6 %near_terms.1 = bf16[2,256,256]{2,1,0:T(8,128)(2,1)S(1)} custom-call(s32[1,2,9]{2,1,0:T(2,128)S(1)} %copy-done.4, s32[1,2,2]{2,1,0:T(2,128)S(1)} %copy-done.3, bf16[1040,256]{1,0:T(8,128)(2,1)S(1)} %collective-permute-done.late, f32[2,2,256,256]{3,2,1,0:T(8,128)S(1)} %early_windows.1.partly, bf16[4,256,512]{2,1,0:T(8,128)(2,1)S(1)} %copy-done, ...), custom_call_target="tpu_custom_call" | custom-call | flops 1100000000 | bytes 5000000 | tf_op jit(solution)/shard_map/near_terms/pallas_call | solution.py:284
  30.8 0.0 copy-start.1
  30.9 0.1 collective-permute-start.3
  31.0 0.0 collective-permute-done.2.t
  31.0 1.8 %far_terms.1.mine = f32[2,256,256]{2,1,0:T(8,128)S(1)} custom-call(bf16[2,256,256]{2,1,0:T(8,128)(2,1)S(1)} %collective-permute-done.2.t, bf16[4,256,512]{2,1,0:T(8,128)(2,1)S(1)} %copy-done, bf16[4,512,256]{2,1,0:T(8,128)(2,1)S(1)} %get-tuple-element.13.wave, bf16[512,512]{1,0:T(8,128)(2,1)S(1)} %get-tuple-element.14.left, ...), custom_call_target="tpu_custom_call" | custom-call | flops 1100000000 | bytes 5000000 | tf_op jit(solution)/shard_map/far_terms/pallas_call | solution.py:301
  32.8 0.0 collective-permute-done.3.others
  32.8 0.8 %split_terms.1 = (bf16[512,256]{1,0:T(8,128)(2,1)S(1)}, f32[512,256]{1,0:T(8,128)S(1)}, bf16[512,256]{1,0:T(8,128)(2,1)S(1)}) custom-call(s32[1,2,2]{2,1,0:T(2,128)S(1)} %copy-done.3, f32[2,256,256]{2,1,0:T(8,128)S(1)} %far_terms.1.mine, bf16[2,256,256]{2,1,0:T(8,128)(2,1)S(1)} %collective-permute-done.3.others), custom_call_target="tpu_custom_call" | custom-call | tf_op jit(solution)/shard_map/split_terms/pallas_call | solution.py:333
  33.6 0.1 collective-permute-start.4
  33.7 6.9 %collective-permute-start.5 = (bf16[512,256]{1,0:T(8,128)(2,1)S(1)}, bf16[512,256]{1,0:T(8,128)(2,1)S(1)}, u32[]{:S(2)}, u32[]{:S(2)}) collective-permute-start(bf16[512,256]{1,0:T(8,128)(2,1)S(1)} %get-tuple-element.20), channel_id=1, source_target_pairs={{1,2},{3,4},{5,6},{7,8},{9,10},{11,12},{13,14},{15,16},{17,18},{19... | collective-permute-start | bytes 786440 | tf_op jit(solution)/shard_map/ppermute | solution.py:413
  40.7 0.0 copy-done.1
  40.7 0.8 %own_update.1.tiles = f32[1,8,128,256]{3,2,1,0:T(8,128)S(1)} custom-call(s32[1,2,9]{2,1,0:T(2,128)S(1)} %copy-done.4, s32[1,2,2]{2,1,0:T(2,128)S(1)} %copy-done.3, f32[1,8,128,256]{3,2,1,0:T(8,128)S(1)} %copy-done.1, f32[512,256]{1,0:T(8,128)S(1)} %get-tuple-element.18.terms), custom_call_target="tpu_custom_call" | custom-call | flops 1000000 | bytes 3000000 | tf_op jit(solution)/shard_map/own_update/pallas_call | solution.py:371
  41.4 0.0 collective-permute-done.4.terms
  41.5 0.8 %swap_update.2.tiles = f32[1,8,128,256]{3,2,1,0:T(8,128)S(1)} custom-call(s32[1,32]{1,0:T(1,128)S(1)} %slice_convert_fusion.notes, f32[1,8,128,256]{3,2,1,0:T(8,128)S(1)} %own_update.1.tiles, bf16[512,256]{1,0:T(8,128)(2,1)S(1)} %collective-permute-done.4.terms), custom_call_target="tpu_custom_call" | custom-call | flops 1000000 | bytes 3000000 | tf_op jit(solution)/shard_map/swap_update/pallas_call | solution.py:398
  42.2 4.2 %collective-permute-done.5.terms = bf16[512,256]{1,0:T(8,128)(2,1)S(1)} collective-permute-done((bf16[512,256]{1,0:T(8,128)(2,1)S(1)}, bf16[512,256]{1,0:T(8,128)(2,1)S(1)}, u32[]{:S(2)}, u32[]{:S(2)}) %collective-permute-start.5) | collective-permute-done | bytes 262176 | tf_op jit(solution)/shard_map/ppermute | solution.py:413
  46.5 1.7 %swap_update.3 = f32[1,8,128,256]{3,2,1,0:T(8,128)} custom-call(s32[1,32]{1,0:T(1,128)S(1)} %slice_convert_fusion.1.notes, f32[1,8,128,256]{3,2,1,0:T(8,128)S(1)} %swap_update.2.tiles, bf16[512,256]{1,0:T(8,128)(2,1)S(1)} %collective-permute-done.5.terms), custom_call_target="tpu_custom_call" | custom-call | flops 1000000 | bytes 3000000 | tf_op jit(solution)/shard_map/swap_update/pallas_call | solution.py:398
  (2 shorter events, 0.0 us)
Async XLA Ops:
  2.2 15.9 %copy-start.2 = (bf16[1040,256]{1,0:T(8,128)(2,1)S(1)}, bf16[1040,256]{1,0:T(8,128)(2,1)}, u32[]{:S(2)}) copy-start(bf16[1040,256]{1,0:T(8,128)(2,1)} %pack_tiles.1.own) | copy-start | bytes 1597444
  2.2 15.9 %copy-start.3 = (s32[1,2,2]{2,1,0:T(2,128)S(1)}, s32[1,2,2]{2,1,0:T(2,128)}, u32[]{:S(2)}) copy-start(s32[1,2,2]{2,1,0:T(2,128)} %offsets.9) | copy-start | bytes 52
  2.2 15.9 %copy-start.4 = (s32[1,2,9]{2,1,0:T(2,128)S(1)}, s32[1,2,9]{2,1,0:T(2,128)}, u32[]{:S(2)}) copy-start(s32[1,2,9]{2,1,0:T(2,128)} %owners.7) | copy-start | bytes 220
  2.2 15.9 %collective-permute-start.1 = (bf16[1040,256]{1,0:T(8,128)(2,1)}, bf16[1040,256]{1,0:T(8,128)(2,1)S(1)}, u32[]{:S(2)}, u32[]{:S(2)}) collective-permute-start(bf16[1040,256]{1,0:T(8,128)(2,1)} %pack_tiles.1.own), channel_id=1, source_target_pairs={{0,1},{2,3},{4,5},{6,7},{8,9},{10,11},{12,13},{14,15},{16,17},{18,... | collective-permute-start | bytes 1597448 | tf_op jit(solution)/shard_map/ppermute | solution.py:413
  4.8 21.1 %collective-permute-start = (bf16[1040,256]{1,0:T(8,128)(2,1)}, bf16[1040,256]{1,0:T(8,128)(2,1)S(1)}, u32[]{:S(2)}, u32[]{:S(2)}) collective-permute-start(bf16[1040,256]{1,0:T(8,128)(2,1)} %pack_tiles.1.own), channel_id=1, source_target_pairs={{1,2},{3,4},{5,6},{7,8},{9,10},{11,12},{13,14},{15,16},{17,18},{19... | collective-permute-start | bytes 1597448 | tf_op jit(solution)/shard_map/ppermute | solution.py:413
  14.1 1.6 %copy-start.5 = (bf16[1,2,4,256,512]{4,3,2,1,0:T(8,128)(2,1)S(1)}, bf16[1,2,4,256,512]{4,3,2,1,0:T(8,128)(2,1)}, u32[]{:S(2)}) copy-start(bf16[1,2,4,256,512]{4,3,2,1,0:T(8,128)(2,1)} %refs_1_.1) | copy-start | bytes 6291460
  15.7 0.7 %copy-start.6 = (bf16[2,2,31]{2,1,0:T(2,128)(2,1)S(1)}, bf16[2,2,31]{2,1,0:T(2,128)(2,1)}, u32[]{:S(2)}) copy-start(bf16[2,2,31]{2,1,0:T(2,128)(2,1)} %refs_0_.1) | copy-start | bytes 748
  18.1 10.1 %copy-start = (bf16[4,256,512]{2,1,0:T(8,128)(2,1)S(1)}, bf16[4,256,512]{2,1,0:T(8,128)(2,1)}, u32[]{:S(2)}) copy-start(bf16[4,256,512]{2,1,0:T(8,128)(2,1)} %probe.3) | copy-start | bytes 3145732
  26.6 4.4 %collective-permute-start.2 = (bf16[2,256,256]{2,1,0:T(8,128)(2,1)S(1)}, bf16[2,256,256]{2,1,0:T(8,128)(2,1)S(1)}, u32[]{:S(2)}, u32[]{:S(2)}) collective-permute-start(bf16[2,256,256]{2,1,0:T(8,128)(2,1)S(1)} %far_window.1), channel_id=1, source_target_pairs={{0,128},{128,0},{1,129},{129,1},{2,130},{130,2},{3,131},{131,3},{4... | collective-permute-start | bytes 786440 | tf_op jit(solution)/shard_map/ppermute | solution.py:417
  30.8 9.8 %copy-start.1 = (f32[1,8,128,256]{3,2,1,0:T(8,128)S(1)}, f32[1,8,128,256]{3,2,1,0:T(8,128)}, u32[]{:S(2)}) copy-start(f32[1,8,128,256]{3,2,1,0:T(8,128)} %tiles.1) | copy-start | bytes 3145732
  30.9 1.9 %collective-permute-start.3 = (bf16[2,256,256]{2,1,0:T(8,128)(2,1)S(1)}, bf16[2,256,256]{2,1,0:T(8,128)(2,1)S(1)}, u32[]{:S(2)}, u32[]{:S(2)}) collective-permute-start(bf16[2,256,256]{2,1,0:T(8,128)(2,1)S(1)} %near_terms.1), channel_id=1, source_target_pairs={{0,128},{128,0},{1,129},{129,1},{2,130},{130,2},{3,131},{131,3},{4... | collective-permute-start | bytes 786440 | tf_op jit(solution)/shard_map/ppermute | solution.py:417
  33.6 7.8 %collective-permute-start.4 = (bf16[512,256]{1,0:T(8,128)(2,1)S(1)}, bf16[512,256]{1,0:T(8,128)(2,1)S(1)}, u32[]{:S(2)}, u32[]{:S(2)}) collective-permute-start(bf16[512,256]{1,0:T(8,128)(2,1)S(1)} %get-tuple-element.19), channel_id=1, source_target_pairs={{0,1},{2,3},{4,5},{6,7},{8,9},{10,11},{12,13},{14,15},{16,17},{18,... | collective-permute-start | bytes 786440 | tf_op jit(solution)/shard_map/ppermute | solution.py:413
  33.7 12.8 %collective-permute-start.5 = (bf16[512,256]{1,0:T(8,128)(2,1)S(1)}, bf16[512,256]{1,0:T(8,128)(2,1)S(1)}, u32[]{:S(2)}, u32[]{:S(2)}) collective-permute-start(bf16[512,256]{1,0:T(8,128)(2,1)S(1)} %get-tuple-element.20), channel_id=1, source_target_pairs={{1,2},{3,4},{5,6},{7,8},{9,10},{11,12},{13,14},{15,16},{17,18},{19... | collective-permute-start | bytes 786440 | tf_op jit(solution)/shard_map/ppermute | solution.py:413

commit v3 on v2

--- a/solution.py
+++ b/solution.py
@@ -12,7 +12,6 @@
 NP, TS, HALF = 256, 128, 15
 MODES, POS, CAP = 4, 2, 8
 STEP = 32
-ROWS = CAP * TS
 SMEM = pl.BlockSpec(memory_space=pltpu.SMEM)
 VMEM = pl.BlockSpec(memory_space=pltpu.VMEM)
 HBM = pl.BlockSpec(memory_space=pltpu.HBM)
@@ -28,48 +27,6 @@
 
 def lanes(rows):
     return lax.broadcasted_iota(jnp.int32, (rows, TS), 1)
-
-
-def pack_kernel(owners_hbm, offsets_hbm, tiles_hbm, out, owners, offsets, tiles, small, large):
-    copies = [pltpu.make_async_copy(tiles_hbm.at[0, q], tiles.at[q], large.at[q]) for q in range(CAP)]
-    for copy in copies:
-        copy.start()
-    notes_in = [
-        pltpu.make_async_copy(owners_hbm, owners, small.at[0]),
-        pltpu.make_async_copy(offsets_hbm, offsets, small.at[1]),
-    ]
-    for copy in notes_in:
-        copy.start()
-    for q in range(CAP):
-        copies[q].wait()
-        out[q * TS : (q + 1) * TS, :] = tiles[q].astype(BF16)
-    for copy in notes_in:
-        copy.wait()
-    spot = lax.broadcasted_iota(jnp.int32, (16, 2 * TS), 1)
-    notes = jnp.zeros((16, 2 * TS), jnp.int32)
-    for p in range(POS):
-        for k in range(9):
-            notes = jnp.where(spot == p * 16 + k, owners[0, p, k] & (CAP - 1), notes)
-        notes = jnp.where(spot == p * 16 + 9, offsets[0, p, 0], notes)
-    out[ROWS : ROWS + 16, :] = notes.astype(F32).astype(BF16)
-
-
-def pack(owners, offsets, tiles):
-    return pl.pallas_call(
-        pack_kernel,
-        out_shape=jax.ShapeDtypeStruct((ROWS + 16, 2 * TS), BF16),
-        in_specs=[HBM] * 3,
-        out_specs=VMEM,
-        scratch_shapes=[
-            pltpu.SMEM(owners.shape, jnp.int32),
-            pltpu.SMEM(offsets.shape, jnp.int32),
-            pltpu.VMEM((CAP, TS, 2 * TS), F32),
-            pltpu.SemaphoreType.DMA((2,)),
-            pltpu.SemaphoreType.DMA((CAP,)),
-        ],
-        compiler_params=params(62),
-        name="pack_tiles",
-    )(owners, offsets, tiles)
 
 
 def band(taps, row):
@@ -127,10 +84,17 @@
     return 1 - lax.axis_index("scan") % 2
 
 
-def cut_column(p, j, owners, offsets, tiles, stack, put):
+def packed_tile(tiles):
+    return lambda q: tiles[q].astype(F32)
+
+
+def plain_tile(tiles):
+    return lambda q: tiles[0, q].astype(BF16).astype(F32)
+
+
+def cut_column(p, j, owners, offsets, tile_at, stack, put):
     for i in range(3):
-        q = owners[0, p, 3 * i + j] & (CAP - 1)
-        tile = tiles[pl.ds(pl.multiple_of(q * TS, TS), TS), :].astype(F32)
+        tile = tile_at(owners[0, p, 3 * i + j] & (CAP - 1))
         stack[0, i * TS : (i + 1) * TS, :] = tile[:, :TS]
         stack[1, i * TS : (i + 1) * TS, :] = tile[:, TS:]
     r, c = offsets[0, p, 0], offsets[0, p, 1]
@@ -157,14 +121,14 @@
             out[p, part, at : at + STEP, :TS] = turned
             out[p, part, at : at + STEP, TS:] = turned
 
-        cut_column(p, 1, owners, offsets, own, stack.at[0], put_own)
+        cut_column(p, 1, owners, offsets, plain_tile(own), stack.at[0], put_own)
         mask = taken(side, offsets[0, p, 1])
 
         def put_early(part, at, turned):
             place = (p, part, slice(at, at + STEP), half(side))
             out[place] = jnp.where(mask, turned, out[place])
 
-        cut_column(p, 2 * side, owners, offsets, early, stack.at[1], put_early)
+        cut_column(p, 2 * side, owners, offsets, packed_tile(early), stack.at[1], put_early)
 
 
 def early_windows(owners, offsets, own, early):
@@ -190,23 +154,25 @@
         out[part, rows, half(side)] = jnp.where(mask, turned, kept).astype(out.dtype)
         out[part, rows, half(1 - side)] = partly[p, part, rows, half(1 - side)].astype(out.dtype)
 
-    cut_column(p, 2 * side, owners, offsets, late, stack, put)
-
-
-def window_kernel(owners, offsets, late, partly, out, stack):
-    complete(1 - lax.axis_index("slab"), owners, offsets, late, partly, stack, out)
-
-
-def far_window(owners, offsets, late, partly):
-    return pl.pallas_call(
-        window_kernel,
-        out_shape=jax.ShapeDtypeStruct((2, NP, NP), BF16),
+    cut_column(p, 2 * side, owners, offsets, packed_tile(late), stack, put)
+
+
+def late_kernel(owners, offsets, late, partly, far, near, stack):
+    here = lax.axis_index("slab")
+    complete(1 - here, owners, offsets, late, partly, stack.at[0], far)
+    complete(here, owners, offsets, late, partly, stack.at[1], near)
+
+
+def late_windows(owners, offsets, late, partly):
+    return pl.pallas_call(
+        late_kernel,
+        out_shape=[jax.ShapeDtypeStruct((2, NP, NP), BF16)] * 2,
         in_specs=[SMEM, SMEM, VMEM, VMEM],
-        out_specs=VMEM,
-        scratch_shapes=[pltpu.VMEM((2, 3 * TS, TS), F32)],
+        out_specs=[VMEM] * 2,
+        scratch_shapes=[pltpu.VMEM((2, 2, 3 * TS, TS), F32)],
         compiler_params=params(8),
         cost_estimate=pl.CostEstimate(flops=1_000_000, bytes_accessed=2_000_000, transcendentals=0),
-        name="far_window",
+        name="late_windows",
     )(owners, offsets, late, partly)
 
 
@@ -265,9 +231,8 @@
         upper_terms(t, probe, wave, left_adj, right_adj, total)
 
 
-def near_kernel(owners, offsets, late, partly, probe, wave, left, left_adj, right, right_adj, out, stack, t, total):
+def near_kernel(t, probe, wave, left, left_adj, right, right_adj, out, total):
     side = lax.axis_index("slab")
-    complete(side, owners, offsets, late, partly, stack, t)
     both_ways(side, t, probe, wave, left, left_adj, right, right_adj, total)
     out[...] = total[...].astype(BF16)
 
@@ -280,21 +245,17 @@
 COST = pl.CostEstimate(flops=1_100_000_000, bytes_accessed=5_000_000, transcendentals=0)
 
 
-def near_terms(owners, offsets, late, partly, probe, wave, mats):
+def near_terms(t, probe, wave, mats):
     return pl.pallas_call(
         near_kernel,
         out_shape=jax.ShapeDtypeStruct((2, NP, NP), BF16),
-        in_specs=[SMEM, SMEM] + [VMEM] * 8,
+        in_specs=[VMEM] * 7,
         out_specs=VMEM,
-        scratch_shapes=[
-            pltpu.VMEM((2, 3 * TS, TS), F32),
-            pltpu.VMEM((2, NP, NP), F32),
-            pltpu.VMEM((2, NP, NP), F32),
-        ],
+        scratch_shapes=[pltpu.VMEM((2, NP, NP), F32)],
         compiler_params=params(24),
         cost_estimate=COST,
         name="near_terms",
-    )(owners, offsets, late, partly, probe, wave, *mats)
+    )(t, probe, wave, *mats)
 
 
 def far_terms(t, probe, wave, mats):
@@ -309,8 +270,16 @@
     )(t, probe, wave, *mats)
 
 
-def split_kernel(offsets, mine, others, early, own, late):
+def split_kernel(owners, offsets, mine, others, early, own, late):
     here = lax.axis_index("slab")
+    place = lax.broadcasted_iota(jnp.int32, (16, 2 * TS), 1)
+    notes = jnp.zeros((16, 2 * TS), jnp.int32)
+    for p in range(POS):
+        for k in range(9):
+            notes = jnp.where(place == p * 16 + k, owners[0, p, k] & (CAP - 1), notes)
+        notes = jnp.where(place == p * 16 + 9, offsets[0, p, 0], notes)
+    early[POS * NP :, :] = notes.astype(F32).astype(BF16)
+    late[POS * NP :, :] = notes.astype(F32).astype(BF16)
     to_right = early_side() == 1
     spot = lanes(STEP)
     for k, terms in ((0, mine), (1, others)):
@@ -328,43 +297,56 @@
                 late[place] = jnp.where(to_right, left, right).astype(BF16)
 
 
-def split_terms(offsets, mine, others):
-    shape = (POS * NP, 2 * TS)
+def split_terms(owners, offsets, mine, others):
+    sent = jax.ShapeDtypeStruct((POS * NP + 16, 2 * TS), BF16)
     return pl.pallas_call(
         split_kernel,
-        out_shape=[
-            jax.ShapeDtypeStruct(shape, BF16),
-            jax.ShapeDtypeStruct(shape, F32),
-            jax.ShapeDtypeStruct(shape, BF16),
-        ],
-        in_specs=[SMEM, VMEM, VMEM],
+        out_shape=[sent, jax.ShapeDtypeStruct((POS * NP, 2 * TS), F32), sent],
+        in_specs=[SMEM, SMEM, VMEM, VMEM],
         out_specs=[VMEM] * 3,
         compiler_params=params(8),
         name="split_terms",
-    )(offsets, mine, others)
-
-
-def take_off(terms, slot, row, stack, out):
+    )(owners, offsets, mine, others)
+
+
+STACK = pltpu.VMEM((POS, 2, 2 * TS + NP, TS), F32)
+
+
+def fill(terms, stack):
     for p in range(POS):
         for part in range(2):
             cols = slice(part * TS, (part + 1) * TS)
-            stack[part, TS : TS + NP, :] = terms[p * NP : (p + 1) * NP, cols].astype(F32) * step_rate
-        r = row(p)
-        for i in range(3):
-            for part in range(2):
-                cols = slice(part * TS, (part + 1) * TS)
-                out[0, slot(p, i), :, cols] -= stack[part, pl.ds(TS + i * TS - r, TS), :]
-
-
-def clear(stack):
-    stack[:, 0:TS, :] = jnp.zeros((2, TS, TS), F32)
-    stack[:, TS + NP :, :] = jnp.zeros((2, TS, TS), F32)
+            stack[p, part, :TS, :] = jnp.zeros((TS, TS), F32)
+            stack[p, part, TS : TS + NP, :] = terms[p * NP : (p + 1) * NP, cols].astype(F32) * step_rate
+            stack[p, part, TS + NP :, :] = jnp.zeros((TS, TS), F32)
+
+
+def take_off(slots, rows, stack, tiles, done):
+    for q in range(CAP):
+        starts = []
+        for p in range(POS):
+            start = jnp.int32(0)
+            for i in range(3):
+                start = jnp.where(slots[p][i] == q, TS + i * TS - rows[p], start)
+            starts.append(start)
+        for part in range(2):
+            tile = tiles[0, q, :, part * TS : (part + 1) * TS]
+            for p in range(POS):
+                tile = tile - stack[p, part, pl.ds(starts[p], TS), :]
+            done(q, part, tile)
+
+
+def keep(out):
+    def done(q, part, tile):
+        out[0, q, :, part * TS : (part + 1) * TS] = tile
+
+    return done
 
 
 def own_kernel(owners, offsets, tiles, terms, out, stack):
-    clear(stack)
-    out[...] = tiles[...]
-    take_off(terms, lambda p, i: owners[0, p, 3 * i + 1] & (CAP - 1), lambda p: offsets[0, p, 0], stack, out)
+    slots = [[owners[0, p, 3 * i + 1] & (CAP - 1) for i in range(3)] for p in range(POS)]
+    fill(terms, stack)
+    take_off(slots, [offsets[0, p, 0] for p in range(POS)], stack, tiles, keep(out))
 
 
 def own_update(owners, offsets, tiles, terms):
@@ -373,38 +355,76 @@
         out_shape=jax.ShapeDtypeStruct(tiles.shape, F32),
         in_specs=[SMEM, SMEM, VMEM, VMEM],
         out_specs=VMEM,
-        scratch_shapes=[pltpu.VMEM((2, 2 * TS + NP, TS), F32)],
+        scratch_shapes=[STACK],
         compiler_params=params(8),
         cost_estimate=pl.CostEstimate(flops=1_000_000, bytes_accessed=3_000_000, transcendentals=0),
         name="own_update",
     )(owners, offsets, tiles, terms)
 
 
-def early_update_kernel(notes, tiles, terms, out, stack):
-    clear(stack)
+def read_notes(j, terms, lines, notes, sem):
+    lines[...] = terms[POS * NP :, :TS].astype(F32).astype(jnp.int32)
+    copy = pltpu.make_async_copy(lines.at[0:1], notes, sem)
+    copy.start()
+    return copy
+
+
+def noted(j, notes):
+    slots = [[notes[0, p * 16 + 3 * i + j] for i in range(3)] for p in range(POS)]
+    return slots, [notes[0, p * 16 + 9] for p in range(POS)]
+
+
+NOTES = [STACK, pltpu.VMEM((16, TS), jnp.int32), pltpu.SMEM((1, TS), jnp.int32), pltpu.SemaphoreType.DMA(())]
+
+
+def early_update_kernel(tiles, terms, out, stack, lines, notes, sem):
     j = 2 - 2 * early_side()
-    out[...] = tiles[...]
-    take_off(terms, lambda p, i: notes[0, p * 16 + 3 * i + j], lambda p: notes[0, p * 16 + 9], stack, out)
-
-
-def late_update_kernel(notes, tiles, terms, out, stack):
-    clear(stack)
+    copy = read_notes(j, terms, lines, notes, sem)
+    fill(terms, stack)
+    copy.wait()
+    take_off(*noted(j, notes), stack, tiles, keep(out))
+
+
+def early_update(tiles, terms):
+    return pl.pallas_call(
+        early_update_kernel,
+        out_shape=jax.ShapeDtypeStruct(tiles.shape, F32),
+        in_specs=[VMEM, VMEM],
+        out_specs=VMEM,
+        scratch_shapes=NOTES,
+        compiler_params=params(8),
+        cost_estimate=pl.CostEstimate(flops=1_000_000, bytes_accessed=3_000_000, transcendentals=0),
+        name="early_update",
+    )(tiles, terms)
+
+
+def late_update_kernel(tiles, terms, out, stack, lines, notes, sem, work, sems):
     j = 2 * early_side()
-    out[...] = tiles[...]
-    take_off(terms, lambda p, i: notes[0, p * 16 + 3 * i + j], lambda p: notes[0, p * 16 + 9], stack, out)
-
-
-def swap_update(kernel, notes, tiles, terms):
-    return pl.pallas_call(
-        kernel,
+    copy = read_notes(j, terms, lines, notes, sem)
+    fill(terms, stack)
+    copy.wait()
+    copies = [pltpu.make_async_copy(work.at[0, q], out.at[0, q], sems.at[q]) for q in range(CAP)]
+
+    def done(q, part, tile):
+        keep(work)(q, part, tile)
+        if part == 1:
+            copies[q].start()
+
+    take_off(*noted(j, notes), stack, tiles, done)
+    for copy in copies:
+        copy.wait()
+
+
+def late_update(tiles, terms):
+    return pl.pallas_call(
+        late_update_kernel,
         out_shape=jax.ShapeDtypeStruct(tiles.shape, F32),
-        in_specs=[SMEM, VMEM, VMEM],
-        out_specs=VMEM,
-        scratch_shapes=[pltpu.VMEM((2, 2 * TS + NP, TS), F32)],
-        compiler_params=params(8),
-        cost_estimate=pl.CostEstimate(flops=1_000_000, bytes_accessed=3_000_000, transcendentals=0),
-        name="swap_update",
-    )(notes, tiles, terms)
+        in_specs=[VMEM, VMEM],
+        out_specs=HBM,
+        scratch_shapes=NOTES + [pltpu.VMEM((1, CAP, TS, 2 * TS), F32), pltpu.SemaphoreType.DMA((CAP,))],
+        compiler_params=params(8),
+        name="late_update",
+    )(tiles, terms)
 
 
 def swap(value, first):
@@ -417,28 +437,24 @@
     return lax.ppermute(value, "slab", [(0, 1), (1, 0)])
 
 
-def notes_of(packed):
-    return packed[ROWS : ROWS + 1, : 2 * 16].astype(jnp.int32)
-
-
 def shards(probe_modes, tap_weights, object_slices, exit_residual, offsets, owners):
     side = lax.axis_index("slab").astype(jnp.int32).reshape(1)
-    own = pack(owners, offsets, object_slices)
+    own = object_slices[0].astype(BF16)
     late = swap(own, 1)
     early = swap(own, 0)
     *mats, wave = exit_adjoint(side, tap_weights, exit_residual)
-    partly = early_windows(owners, offsets, own, early)
-    t_there = far_window(owners, offsets, late, partly)
+    partly = early_windows(owners, offsets, object_slices, early)
+    t_there, t_near = late_windows(owners, offsets, late, partly)
     t_here = across(t_there)
-    terms_there = near_terms(owners, offsets, late, partly, probe_modes, wave, mats)
+    terms_there = near_terms(t_near, probe_modes, wave, mats)
     terms_far = across(terms_there)
     terms_here = far_terms(t_here, probe_modes, wave, mats)
-    early_out, kept, late_out = split_terms(offsets, terms_here, terms_far)
+    early_out, kept, late_out = split_terms(owners, offsets, terms_here, terms_far)
     late_in = swap(late_out, 1)
     early_in = swap(early_out, 0)
     tiles = own_update(owners, offsets, object_slices, kept)
-    tiles = swap_update(early_update_kernel, notes_of(early), tiles, early_in)
-    return swap_update(late_update_kernel, notes_of(late), tiles, late_in)
+    tiles = early_update(tiles, early_in)
+    return late_update(tiles, late_in)
 
 
 def solution(mesh):

time: 48.4 us -> 46.5 us (0.961)
  Pallas kernels: 14.1 us -> 11.3 us
  other arithmetic: 0.01 us -> 1.28 us
    pallas_call x5 -> x4, Pallas kernels: 6.27 us -> 4.09 us  [the longest x1 1.64 us: late_update(): pl.pallas_call(late_update_kernel, out_shape=jax.ShapeDtypeStruct(tiles.s...]
    convert_element_type x2 -> x1, other arithmetic: 0.01 us -> 1.28 us  [shards(): own = object_slices[0].astype(BF16)]
    pallas_call x1, Pallas kernels: 2.62 us -> 1.92 us  [near_terms(): pl.pallas_call(near_kernel, out_shape=jax.ShapeDtypeStruct((2, NP, NP), B...]
    unnamed x14 -> x12, local copies, waits for them, and re-layouts: 2.3 us -> 2.29 us
  transfers between devices with their start and end apart: 6 -> 6, of which waited for: 2 -> 2; matrix products, arithmetic and copies ran while one was open for 0% -> 0% of each run, Pallas kernels for 18% -> 17%
where the time goes in v3:
time: 46.5 us; the launch traced here: 46.3 us
  starting transfers between devices  20.7 us (45%)
  Pallas kernels  11.3 us (24%)
  waiting for transfers between devices  10.6 us (23%)
  local copies, waits for them, and re-layouts  2.29 us (5%)
  other arithmetic  1.28 us (3%)
    ppermute x4, starting transfers between devices, swap(): return lax.ppermute(value, 'scan', pairs + [(j, i) for i, j in pairs])  18.9 us
    ppermute x4, waiting for transfers between devices, swap(): return lax.ppermute(value, 'scan', pairs + [(j, i) for i, j in pairs])  10.6 us
    unnamed x12, local copies, waits for them, and re-layouts  2.29 us
    pallas_call x1, Pallas kernels, near_terms(): pl.pallas_call(near_kernel, out_shape=jax.ShapeDtypeStruct((2, NP, NP), B...  1.92 us
    pallas_call x1, Pallas kernels, far_terms(): pl.pallas_call(far_kernel, out_shape=jax.ShapeDtypeStruct((2, NP, NP), F3...  1.78 us
    pallas_call x1, Pallas kernels, exit_adjoint(): pl.pallas_call(lambda side, *refs: exit_kernel(*refs), grid_spec=pltpu.Pr...  1.73 us
    ppermute x2, starting transfers between devices, across(): return lax.ppermute(value, 'slab', [(0, 1), (1, 0)])  1.73 us
    pallas_call x1, Pallas kernels, late_update(): pl.pallas_call(late_update_kernel, out_shape=jax.ShapeDtypeStruct(tiles.s...  1.64 us
  transfers between devices with their start and end apart: 6, of which 2 were waited for; matrix products, arithmetic and copies ran while one was open for 0% of the time, Pallas kernels for 17%

profile of v3, /device:TPU:1, one launch (start us, length us, event | category | flops | bytes accessed | tf_op | source)
XLA Modules:
  0.0 46.3 jit_solution(7493627255623316018)
XLA Ops:
  0.0 1.3 %convert_bitcast_fusion = bf16[8,128,256]{2,1,0:T(8,128)(2,1)S(1)} fusion(f32[1,8,128,256]{3,2,1,0:T(8,128)} %tiles.1), kind=kLoop, calls=%fused_computation | loop fusion | flops 262144 | bytes 1572864 | tf_op jit(solution)/shard_map/convert_element_type | solution.py:442
  1.3 0.0 copy-start
  1.3 0.0 copy-start.2
  1.3 0.0 copy-start.3
  1.3 2.6 %collective-permute-start.1 = (bf16[8,128,256]{2,1,0:T(8,128)(2,1)S(1)}, bf16[8,128,256]{2,1,0:T(8,128)(2,1)S(1)}, u32[]{:S(2)}, u32[]{:S(2)}) collective-permute-start(bf16[8,128,256]{2,1,0:T(8,128)(2,1)S(1)} %convert_bitcast_fusion), channel_id=1, source_target_pairs={{0,1},{2,3},{4,5},{6,7},{8,9},{10,11},{12,13},{14,15},{16,17},{18,... | collective-permute-start | bytes 1572872 | tf_op jit(solution)/shard_map/ppermute | solution.py:433
  3.9 9.3 %collective-permute-start = (bf16[8,128,256]{2,1,0:T(8,128)(2,1)S(1)}, bf16[8,128,256]{2,1,0:T(8,128)(2,1)S(1)}, u32[]{:S(2)}, u32[]{:S(2)}) collective-permute-start(bf16[8,128,256]{2,1,0:T(8,128)(2,1)S(1)} %convert_bitcast_fusion), channel_id=1, source_target_pairs={{1,2},{3,4},{5,6},{7,8},{9,10},{11,12},{13,14},{15,16},{17,18},{19... | collective-permute-start | bytes 1572872 | tf_op jit(solution)/shard_map/ppermute | solution.py:433
  13.2 0.0 copy-start.4
  13.2 1.6 %copy-done.4 = bf16[1,2,4,256,512]{4,3,2,1,0:T(8,128)(2,1)S(1)} copy-done((bf16[1,2,4,256,512]{4,3,2,1,0:T(8,128)(2,1)S(1)}, bf16[1,2,4,256,512]{4,3,2,1,0:T(8,128)(2,1)}, u32[]{:S(2)}) %copy-start.4) | copy-done | bytes 2097176
  14.8 0.0 copy-start.5
  14.8 0.7 %copy-done.5 = bf16[2,2,31]{2,1,0:T(2,128)(2,1)S(1)} copy-done((bf16[2,2,31]{2,1,0:T(2,128)(2,1)S(1)}, bf16[2,2,31]{2,1,0:T(2,128)(2,1)}, u32[]{:S(2)}) %copy-start.5) | copy-done | bytes 272
  15.5 1.7 %exit_adjoint.1 = (bf16[512,512]{1,0:T(8,128)(2,1)S(1)}, bf16[512,512]{1,0:T(8,128)(2,1)S(1)}, bf16[512,512]{1,0:T(8,128)(2,1)S(1)}, bf16[512,512]{1,0:T(8,128)(2,1)S(1)}, bf16[4,512,256]{2,1,0:T(8,128)(2,1)S(1)}) custom-call(s32[1]{0:T(128)} %bitcast.1.side, bf16[2,2,31]{2,1,0:T(2,128)(2,1)S(1)} %copy-done.5, bf16[1,2,4,256,512]{4,3,2,1,0:T(8,128)(2,1)S(1)} %copy-done.4), custom_call_target="tpu_custom_call" | custom-call | flops 1100000000 | bytes 6000000 | tf_op jit(solution)/shard_map/exit_adjoint/pallas_call | solution.py:63
  17.2 0.0 copy-start.1
  17.2 0.0 collective-permute-done.1.early
  17.2 0.0 copy-done
  17.2 0.0 copy-done.2
  17.2 0.0 copy-done.3
  17.2 1.0 %early_windows.1.partly = f32[2,2,256,256]{3,2,1,0:T(8,128)S(1)} custom-call(s32[1,2,9]{2,1,0:T(2,128)S(1)} %copy-done.2, s32[1,2,2]{2,1,0:T(2,128)S(1)} %copy-done.3, f32[1,8,128,256]{3,2,1,0:T(8,128)S(1)} %copy-done, bf16[8,128,256]{2,1,0:T(8,128)(2,1)S(1)} %collective-permute-done.1.early), custom_call_target="tpu_custom_call" | custom-call | flops 2000000 | bytes 2000000 | tf_op jit(solution)/shard_map/early_windows/pallas_call | solution.py:135
  18.2 6.3 %collective-permute-done.late = bf16[8,128,256]{2,1,0:T(8,128)(2,1)S(1)} collective-permute-done((bf16[8,128,256]{2,1,0:T(8,128)(2,1)S(1)}, bf16[8,128,256]{2,1,0:T(8,128)(2,1)S(1)}, u32[]{:S(2)}, u32[]{:S(2)}) %collective-permute-start) | collective-permute-done | bytes 524320 | tf_op jit(solution)/shard_map/ppermute | solution.py:433
  24.5 0.8 %late_windows.1 = (bf16[2,256,256]{2,1,0:T(8,128)(2,1)S(1)}, bf16[2,256,256]{2,1,0:T(8,128)(2,1)S(1)}) custom-call(s32[1,2,9]{2,1,0:T(2,128)S(1)} %copy-done.2, s32[1,2,2]{2,1,0:T(2,128)S(1)} %copy-done.3, bf16[8,128,256]{2,1,0:T(8,128)(2,1)S(1)} %collective-permute-done.late, f32[2,2,256,256]{3,2,1,0:T(8,128)S(1)} %early_windows.1.partly), custom_call_target="tpu_custom_call" | custom-call | flops 1000000 | bytes 2000000 | tf_op jit(solution)/shard_map/late_windows/pallas_call | solution.py:167
  25.3 1.6 %collective-permute-start.2 = (bf16[2,256,256]{2,1,0:T(8,128)(2,1)S(1)}, bf16[2,256,256]{2,1,0:T(8,128)(2,1)S(1)}, u32[]{:S(2)}, u32[]{:S(2)}) collective-permute-start(bf16[2,256,256]{2,1,0:T(8,128)(2,1)S(1)} %get-tuple-element.15), channel_id=1, source_target_pairs={{0,128},{128,0},{1,129},{129,1},{2,130},{130,2},{3,131},{131,3},{4... | collective-permute-start | bytes 786440 | tf_op jit(solution)/shard_map/ppermute | solution.py:437
  26.9 0.0 copy-done.1
  26.9 1.9 %near_terms.1 = bf16[2,256,256]{2,1,0:T(8,128)(2,1)S(1)} custom-call(bf16[2,256,256]{2,1,0:T(8,128)(2,1)S(1)} %get-tuple-element.21.t, bf16[4,256,512]{2,1,0:T(8,128)(2,1)S(1)} %copy-done.1, bf16[4,512,256]{2,1,0:T(8,128)(2,1)S(1)} %get-tuple-element.16.wave, bf16[512,512]{1,0:T(8,128)(2,1)S(1)} %get-tuple-element.17.left, ...), custom_call_target="tpu_custom_call" | custom-call | flops 1100000000 | bytes 5000000 | tf_op jit(solution)/shard_map/near_terms/pallas_call | solution.py:249
  28.9 0.1 collective-permute-start.3
  29.0 0.0 collective-permute-done.2.t
  29.0 1.8 %far_terms.1.mine = f32[2,256,256]{2,1,0:T(8,128)S(1)} custom-call(bf16[2,256,256]{2,1,0:T(8,128)(2,1)S(1)} %collective-permute-done.2.t, bf16[4,256,512]{2,1,0:T(8,128)(2,1)S(1)} %copy-done.1, bf16[4,512,256]{2,1,0:T(8,128)(2,1)S(1)} %get-tuple-element.16.wave, bf16[512,512]{1,0:T(8,128)(2,1)S(1)} %get-tuple-element.17.left, ...), custom_call_target="tpu_custom_call" | custom-call | flops 1100000000 | bytes 5000000 | tf_op jit(solution)/shard_map/far_terms/pallas_call | solution.py:262
  30.8 0.0 collective-permute-done.3.others
  30.8 0.9 %split_terms.1 = (bf16[528,256]{1,0:T(8,128)(2,1)S(1)}, f32[512,256]{1,0:T(8,128)S(1)}, bf16[528,256]{1,0:T(8,128)(2,1)S(1)}) custom-call(s32[1,2,9]{2,1,0:T(2,128)S(1)} %copy-done.2, s32[1,2,2]{2,1,0:T(2,128)S(1)} %copy-done.3, f32[2,256,256]{2,1,0:T(8,128)S(1)} %far_terms.1.mine, bf16[2,256,256]{2,1,0:T(8,128)(2,1)S(1)} %collective-permute-done.3.others), custom_call_target="tpu_custom_call" | custom-call | tf_op jit(solution)/shard_map/split_terms/pallas_call | solution.py:302
  31.6 0.1 collective-permute-start.4
  31.7 7.0 %collective-permute-start.5 = (bf16[528,256]{1,0:T(8,128)(2,1)S(1)}, bf16[528,256]{1,0:T(8,128)(2,1)S(1)}, u32[]{:S(2)}, u32[]{:S(2)}) collective-permute-start(bf16[528,256]{1,0:T(8,128)(2,1)S(1)} %get-tuple-element.24), channel_id=1, source_target_pairs={{1,2},{3,4},{5,6},{7,8},{9,10},{11,12},{13,14},{15,16},{17,18},{19... | collective-permute-start | bytes 811016 | tf_op jit(solution)/shard_map/ppermute | solution.py:433
  38.7 0.8 %own_update.1.tiles = f32[1,8,128,256]{3,2,1,0:T(8,128)S(1)} custom-call(s32[1,2,9]{2,1,0:T(2,128)S(1)} %copy-done.2, s32[1,2,2]{2,1,0:T(2,128)S(1)} %copy-done.3, f32[1,8,128,256]{3,2,1,0:T(8,128)S(1)} %copy-done, f32[512,256]{1,0:T(8,128)S(1)} %get-tuple-element.22.terms), custom_call_target="tpu_custom_call" | custom-call | flops 1000000 | bytes 3000000 | tf_op jit(solution)/shard_map/own_update/pallas_call | solution.py:353
  39.5 0.0 collective-permute-done.4.terms
  39.5 0.8 %early_update.1.tiles = f32[1,8,128,256]{3,2,1,0:T(8,128)S(1)} custom-call(f32[1,8,128,256]{3,2,1,0:T(8,128)S(1)} %own_update.1.tiles, bf16[528,256]{1,0:T(8,128)(2,1)S(1)} %collective-permute-done.4.terms), custom_call_target="tpu_custom_call" | custom-call | flops 1000000 | bytes 3000000 | tf_op jit(solution)/shard_map/early_update/pallas_call | solution.py:389
  40.3 4.3 %collective-permute-done.5.terms = bf16[528,256]{1,0:T(8,128)(2,1)S(1)} collective-permute-done((bf16[528,256]{1,0:T(8,128)(2,1)S(1)}, bf16[528,256]{1,0:T(8,128)(2,1)S(1)}, u32[]{:S(2)}, u32[]{:S(2)}) %collective-permute-start.5) | collective-permute-done | bytes 270368 | tf_op jit(solution)/shard_map/ppermute | solution.py:433
  44.7 1.6 %late_update.1 = f32[1,8,128,256]{3,2,1,0:T(8,128)} custom-call(f32[1,8,128,256]{3,2,1,0:T(8,128)S(1)} %early_update.1.tiles, bf16[528,256]{1,0:T(8,128)(2,1)S(1)} %collective-permute-done.5.terms), custom_call_target="tpu_custom_call" | custom-call | tf_op jit(solution)/shard_map/late_update/pallas_call | solution.py:419
Async XLA Ops:
  1.3 15.9 %copy-start = (f32[1,8,128,256]{3,2,1,0:T(8,128)S(1)}, f32[1,8,128,256]{3,2,1,0:T(8,128)}, u32[]{:S(2)}) copy-start(f32[1,8,128,256]{3,2,1,0:T(8,128)} %tiles.1) | copy-start | bytes 3145732
  1.3 15.9 %copy-start.2 = (s32[1,2,9]{2,1,0:T(2,128)S(1)}, s32[1,2,9]{2,1,0:T(2,128)}, u32[]{:S(2)}) copy-start(s32[1,2,9]{2,1,0:T(2,128)} %owners.7) | copy-start | bytes 220
  1.3 15.9 %copy-start.3 = (s32[1,2,2]{2,1,0:T(2,128)S(1)}, s32[1,2,2]{2,1,0:T(2,128)}, u32[]{:S(2)}) copy-start(s32[1,2,2]{2,1,0:T(2,128)} %offsets.7) | copy-start | bytes 52
  1.3 15.9 %collective-permute-start.1 = (bf16[8,128,256]{2,1,0:T(8,128)(2,1)S(1)}, bf16[8,128,256]{2,1,0:T(8,128)(2,1)S(1)}, u32[]{:S(2)}, u32[]{:S(2)}) collective-permute-start(bf16[8,128,256]{2,1,0:T(8,128)(2,1)S(1)} %convert_bitcast_fusion), channel_id=1, source_target_pairs={{0,1},{2,3},{4,5},{6,7},{8,9},{10,11},{12,13},{14,15},{16,17},{18,... | collective-permute-start | bytes 1572872 | tf_op jit(solution)/shard_map/ppermute | solution.py:433
  3.9 20.6 %collective-permute-start = (bf16[8,128,256]{2,1,0:T(8,128)(2,1)S(1)}, bf16[8,128,256]{2,1,0:T(8,128)(2,1)S(1)}, u32[]{:S(2)}, u32[]{:S(2)}) collective-permute-start(bf16[8,128,256]{2,1,0:T(8,128)(2,1)S(1)} %convert_bitcast_fusion), channel_id=1, source_target_pairs={{1,2},{3,4},{5,6},{7,8},{9,10},{11,12},{13,14},{15,16},{17,18},{19... | collective-permute-start | bytes 1572872 | tf_op jit(solution)/shard_map/ppermute | solution.py:433
  13.2 1.6 %copy-start.4 = (bf16[1,2,4,256,512]{4,3,2,1,0:T(8,128)(2,1)S(1)}, bf16[1,2,4,256,512]{4,3,2,1,0:T(8,128)(2,1)}, u32[]{:S(2)}) copy-start(bf16[1,2,4,256,512]{4,3,2,1,0:T(8,128)(2,1)} %refs_1_.1) | copy-start | bytes 6291460
  14.8 0.7 %copy-start.5 = (bf16[2,2,31]{2,1,0:T(2,128)(2,1)S(1)}, bf16[2,2,31]{2,1,0:T(2,128)(2,1)}, u32[]{:S(2)}) copy-start(bf16[2,2,31]{2,1,0:T(2,128)(2,1)} %refs_0_.1) | copy-start | bytes 748
  17.2 9.7 %copy-start.1 = (bf16[4,256,512]{2,1,0:T(8,128)(2,1)S(1)}, bf16[4,256,512]{2,1,0:T(8,128)(2,1)}, u32[]{:S(2)}) copy-start(bf16[4,256,512]{2,1,0:T(8,128)(2,1)} %probe.3) | copy-start | bytes 3145732
  25.3 3.7 %collective-permute-start.2 = (bf16[2,256,256]{2,1,0:T(8,128)(2,1)S(1)}, bf16[2,256,256]{2,1,0:T(8,128)(2,1)S(1)}, u32[]{:S(2)}, u32[]{:S(2)}) collective-permute-start(bf16[2,256,256]{2,1,0:T(8,128)(2,1)S(1)} %get-tuple-element.15), channel_id=1, source_target_pairs={{0,128},{128,0},{1,129},{129,1},{2,130},{130,2},{3,131},{131,3},{4... | collective-permute-start | bytes 786440 | tf_op jit(solution)/shard_map/ppermute | solution.py:437
  28.9 1.9 %collective-permute-start.3 = (bf16[2,256,256]{2,1,0:T(8,128)(2,1)S(1)}, bf16[2,256,256]{2,1,0:T(8,128)(2,1)S(1)}, u32[]{:S(2)}, u32[]{:S(2)}) collective-permute-start(bf16[2,256,256]{2,1,0:T(8,128)(2,1)S(1)} %near_terms.1), channel_id=1, source_target_pairs={{0,128},{128,0},{1,129},{129,1},{2,130},{130,2},{3,131},{131,3},{4... | collective-permute-start | bytes 786440 | tf_op jit(solution)/shard_map/ppermute | solution.py:437
  31.6 7.9 %collective-permute-start.4 = (bf16[528,256]{1,0:T(8,128)(2,1)S(1)}, bf16[528,256]{1,0:T(8,128)(2,1)S(1)}, u32[]{:S(2)}, u32[]{:S(2)}) collective-permute-start(bf16[528,256]{1,0:T(8,128)(2,1)S(1)} %get-tuple-element.23), channel_id=1, source_target_pairs={{0,1},{2,3},{4,5},{6,7},{8,9},{10,11},{12,13},{14,15},{16,17},{18,... | collective-permute-start | bytes 811016 | tf_op jit(solution)/shard_map/ppermute | solution.py:433
  31.7 12.9 %collective-permute-start.5 = (bf16[528,256]{1,0:T(8,128)(2,1)S(1)}, bf16[528,256]{1,0:T(8,128)(2,1)S(1)}, u32[]{:S(2)}, u32[]{:S(2)}) collective-permute-start(bf16[528,256]{1,0:T(8,128)(2,1)S(1)} %get-tuple-element.24), channel_id=1, source_target_pairs={{1,2},{3,4},{5,6},{7,8},{9,10},{11,12},{13,14},{15,16},{17,18},{19... | collective-permute-start | bytes 811016 | tf_op jit(solution)/shard_map/ppermute | solution.py:433

commit v4 on v3

--- a/solution.py
+++ b/solution.py
@@ -80,6 +80,16 @@
     )(side, taps, residual)
 
 
+FIRST, SECOND, THIRD = (0, 2, 4), (5, 7), (1, 3, 6)
+
+
+def part_in(members):
+    z = lax.axis_index("scan") % 8
+    right = functools.reduce(jnp.logical_or, [z == i for i in members])
+    left = functools.reduce(jnp.logical_or, [z == (i + 1) % 8 for i in members])
+    return jnp.logical_or(left, right), right.astype(jnp.int32)
+
+
 def early_side():
     return 1 - lax.axis_index("scan") % 2
 
@@ -113,8 +123,8 @@
     return past * (1 - 2 * side) - side < 0
 
 
-def early_kernel(owners, offsets, own, early, out, stack):
-    side = early_side()
+def early_kernel(owners, offsets, own, first, out, stack):
+    inside, side = part_in(FIRST)
     for p in range(POS):
 
         def put_own(part, at, turned):
@@ -122,16 +132,24 @@
             out[p, part, at : at + STEP, TS:] = turned
 
         cut_column(p, 1, owners, offsets, plain_tile(own), stack.at[0], put_own)
-        mask = taken(side, offsets[0, p, 1])
-
-        def put_early(part, at, turned):
-            place = (p, part, slice(at, at + STEP), half(side))
-            out[place] = jnp.where(mask, turned, out[place])
-
-        cut_column(p, 2 * side, owners, offsets, packed_tile(early), stack.at[1], put_early)
-
-
-def early_windows(owners, offsets, own, early):
+
+    @pl.when(inside)
+    def _():
+        for p in range(POS):
+            overlay(p, side, owners, offsets, first, stack.at[1], out.at[p], out.at[p])
+
+
+def overlay(p, side, owners, offsets, tiles, stack, base, out):
+    mask = taken(side, offsets[0, p, 1])
+
+    def put(part, at, turned):
+        place = (part, slice(at, at + STEP), half(side))
+        out[place] = jnp.where(mask, turned, base[place]).astype(out.dtype)
+
+    cut_column(p, 2 * side, owners, offsets, packed_tile(tiles), stack, put)
+
+
+def early_windows(owners, offsets, own, first):
     return pl.pallas_call(
         early_kernel,
         out_shape=jax.ShapeDtypeStruct((POS, 2, NP, NP), F32),
@@ -141,39 +159,33 @@
         compiler_params=params(8),
         cost_estimate=pl.CostEstimate(flops=2_000_000, bytes_accessed=2_000_000, transcendentals=0),
         name="early_windows",
-    )(owners, offsets, own, early)
-
-
-def complete(p, owners, offsets, late, partly, stack, out):
-    side = 1 - early_side()
-    mask = taken(side, offsets[0, p, 1])
-
-    def put(part, at, turned):
-        rows = slice(at, at + STEP)
-        kept = partly[p, part, rows, half(side)]
-        out[part, rows, half(side)] = jnp.where(mask, turned, kept).astype(out.dtype)
-        out[part, rows, half(1 - side)] = partly[p, part, rows, half(1 - side)].astype(out.dtype)
-
-    cut_column(p, 2 * side, owners, offsets, packed_tile(late), stack, put)
-
-
-def late_kernel(owners, offsets, late, partly, far, near, stack):
+    )(owners, offsets, own, first)
+
+
+def late_kernel(owners, offsets, third, second, partly, far, near, stack):
     here = lax.axis_index("slab")
-    complete(1 - here, owners, offsets, late, partly, stack.at[0], far)
-    complete(here, owners, offsets, late, partly, stack.at[1], near)
-
-
-def late_windows(owners, offsets, late, partly):
+    far[...] = partly[1 - here].astype(BF16)
+    near[...] = partly[here].astype(BF16)
+    for k, (members, tiles) in enumerate(((SECOND, second), (THIRD, third))):
+        inside, side = part_in(members)
+
+        @pl.when(inside)
+        def _():
+            for n, (p, out) in enumerate(((1 - here, far), (here, near))):
+                overlay(p, side, owners, offsets, tiles, stack.at[2 * k + n], partly.at[p], out)
+
+
+def late_windows(owners, offsets, second, third, partly):
     return pl.pallas_call(
         late_kernel,
         out_shape=[jax.ShapeDtypeStruct((2, NP, NP), BF16)] * 2,
-        in_specs=[SMEM, SMEM, VMEM, VMEM],
+        in_specs=[SMEM, SMEM, VMEM, VMEM, VMEM],
         out_specs=[VMEM] * 2,
-        scratch_shapes=[pltpu.VMEM((2, 2, 3 * TS, TS), F32)],
+        scratch_shapes=[pltpu.VMEM((4, 2, 3 * TS, TS), F32)],
         compiler_params=params(8),
         cost_estimate=pl.CostEstimate(flops=1_000_000, bytes_accessed=2_000_000, transcendentals=0),
         name="late_windows",
-    )(owners, offsets, late, partly)
+    )(owners, offsets, third, second, partly)
 
 
 def times(a, b, conjugate):
@@ -191,82 +203,75 @@
     return ref[m, :NP, :].astype(F32), ref[m, NP:, :].astype(F32)
 
 
-def lower_terms(t, probe, wave, left, right, total):
+def summed(pairs, total):
+    for at in range(0, NP, STEP):
+        rows = slice(at, at + STEP)
+        re = im = None
+        for left, right in pairs(rows):
+            one_re, one_im = times(left, right, True)
+            re, im = (one_re, one_im) if re is None else (re + one_re, im + one_im)
+        total[0, rows, :], total[1, rows, :] = re.astype(total.dtype), im.astype(total.dtype)
+
+
+def wide(ref, m, rows):
+    return ref[m, rows, :NP].astype(F32), ref[m, rows, NP:].astype(F32)
+
+
+def tall(ref, m, rows):
+    return ref[m, rows, :].astype(F32), ref[m, slice(NP + rows.start, NP + rows.stop), :].astype(F32)
+
+
+def lower_terms(t, probe, wave, left, right, total, rows_in, waves):
+    window = (t[0].astype(F32), t[1].astype(F32))
     for m in range(MODES):
-        window = (t[0].astype(F32), t[1].astype(F32))
         u = jnp.concatenate(times(beside(probe, m), window, False), 0).astype(BF16)
         v = dot(left[...], u).astype(BF16)
-        v = jnp.concatenate([v[:NP], v[NP:]], 1)
-        psi = dot(v, right[...]).astype(BF16).astype(F32)
-        re, im = times((psi[:, :NP], psi[:, NP:]), above(wave, m), True)
-        if m == 0:
-            total[0], total[1] = re, im
-        else:
-            total[0] += re
-            total[1] += im
-
-
-def upper_terms(t, probe, wave, left_adj, right_adj, total):
+        rows_in[m * NP : (m + 1) * NP, :NP] = v[:NP]
+        rows_in[m * NP : (m + 1) * NP, NP:] = v[NP:]
+    waves[...] = dot(rows_in[...], right[...]).reshape(MODES, NP, 2 * NP)
+    summed(lambda rows: [(wide(waves, m, rows), tall(wave, m, rows)) for m in range(MODES)], total)
+
+
+def upper_terms(t, probe, wave, left_adj, right_adj, total, rows_in, waves):
+    window = (t[0].astype(F32), t[1].astype(F32))
     for m in range(MODES):
-        window = (t[0].astype(F32), t[1].astype(F32))
-        b = jnp.concatenate(times(window, above(wave, m), True), 1).astype(BF16)
-        w = dot(b, right_adj[...]).astype(BF16)
-        w = jnp.concatenate([w[:, :NP], w[:, NP:]], 0)
-        a = dot(left_adj[...], w).astype(BF16).astype(F32)
-        re, im = times(beside(probe, m), (a[:NP], a[NP:]), True)
-        if m == 0:
-            total[0], total[1] = re, im
-        else:
-            total[0] += re
-            total[1] += im
-
-
-def both_ways(chosen, t, probe, wave, left, left_adj, right, right_adj, total):
+        re, im = times(window, above(wave, m), True)
+        rows_in[m * NP : (m + 1) * NP, :NP] = re.astype(BF16)
+        rows_in[m * NP : (m + 1) * NP, NP:] = im.astype(BF16)
+    w = dot(rows_in[...], right_adj[...]).astype(BF16)
+    for m in range(MODES):
+        part = w[m * NP : (m + 1) * NP]
+        waves[m] = dot(left_adj[...], jnp.concatenate([part[:, :NP], part[:, NP:]], 0))
+    summed(lambda rows: [(wide(probe, m, rows), tall(waves, m, rows)) for m in range(MODES)], total)
+
+
+def terms_kernel(far, t, probe, wave, left, left_adj, right, right_adj, out, rows_in, lower, upper):
+    side = lax.axis_index("slab")
+    chosen = 1 - side if far else side
+
     @pl.when(chosen == 0)
     def _():
-        lower_terms(t, probe, wave, left, right, total)
+        lower_terms(t, probe, wave, left, right, out, rows_in, lower)
 
     @pl.when(chosen == 1)
     def _():
-        upper_terms(t, probe, wave, left_adj, right_adj, total)
-
-
-def near_kernel(t, probe, wave, left, left_adj, right, right_adj, out, total):
-    side = lax.axis_index("slab")
-    both_ways(side, t, probe, wave, left, left_adj, right, right_adj, total)
-    out[...] = total[...].astype(BF16)
-
-
-def far_kernel(t, probe, wave, left, left_adj, right, right_adj, out):
-    side = lax.axis_index("slab")
-    both_ways(1 - side, t, probe, wave, left, left_adj, right, right_adj, out)
-
-
-COST = pl.CostEstimate(flops=1_100_000_000, bytes_accessed=5_000_000, transcendentals=0)
-
-
-def near_terms(t, probe, wave, mats):
-    return pl.pallas_call(
-        near_kernel,
-        out_shape=jax.ShapeDtypeStruct((2, NP, NP), BF16),
+        upper_terms(t, probe, wave, left_adj, right_adj, out, rows_in, upper)
+
+
+def slice_terms(far, t, probe, wave, mats):
+    return pl.pallas_call(
+        functools.partial(terms_kernel, far),
+        out_shape=jax.ShapeDtypeStruct((2, NP, NP), F32 if far else BF16),
         in_specs=[VMEM] * 7,
         out_specs=VMEM,
-        scratch_shapes=[pltpu.VMEM((2, NP, NP), F32)],
-        compiler_params=params(24),
-        cost_estimate=COST,
-        name="near_terms",
-    )(t, probe, wave, *mats)
-
-
-def far_terms(t, probe, wave, mats):
-    return pl.pallas_call(
-        far_kernel,
-        out_shape=jax.ShapeDtypeStruct((2, NP, NP), F32),
-        in_specs=[VMEM] * 7,
-        out_specs=VMEM,
-        compiler_params=params(24),
-        cost_estimate=COST,
-        name="far_terms",
+        scratch_shapes=[
+            pltpu.VMEM((MODES * NP, 2 * NP), BF16),
+            pltpu.VMEM((MODES, NP, 2 * NP), F32),
+            pltpu.VMEM((MODES, 2 * NP, NP), F32),
+        ],
+        compiler_params=params(32),
+        cost_estimate=pl.CostEstimate(flops=1_100_000_000, bytes_accessed=5_000_000, transcendentals=0),
+        name="far_terms" if far else "near_terms",
     )(t, probe, wave, *mats)
 
 
@@ -427,9 +432,9 @@
     )(tiles, terms)
 
 
-def swap(value, first):
+def swap(value, members, period):
     count = lax.axis_size("scan")
-    pairs = [(i, (i + 1) % count) for i in range(first, count, 2)]
+    pairs = [(i, (i + 1) % count) for i in range(count) if i % period in members]
     return lax.ppermute(value, "scan", pairs + [(j, i) for i, j in pairs])
 
 
@@ -440,18 +445,17 @@
 def shards(probe_modes, tap_weights, object_slices, exit_residual, offsets, owners):
     side = lax.axis_index("slab").astype(jnp.int32).reshape(1)
     own = object_slices[0].astype(BF16)
-    late = swap(own, 1)
-    early = swap(own, 0)
+    first, second, third = swap(own, FIRST, 8), swap(own, SECOND, 8), swap(own, THIRD, 8)
     *mats, wave = exit_adjoint(side, tap_weights, exit_residual)
-    partly = early_windows(owners, offsets, object_slices, early)
-    t_there, t_near = late_windows(owners, offsets, late, partly)
+    partly = early_windows(owners, offsets, object_slices, first)
+    t_there, t_near = late_windows(owners, offsets, second, third, partly)
     t_here = across(t_there)
-    terms_there = near_terms(t_near, probe_modes, wave, mats)
+    terms_there = slice_terms(False, t_near, probe_modes, wave, mats)
     terms_far = across(terms_there)
-    terms_here = far_terms(t_here, probe_modes, wave, mats)
+    terms_here = slice_terms(True, t_here, probe_modes, wave, mats)
     early_out, kept, late_out = split_terms(owners, offsets, terms_here, terms_far)
-    late_in = swap(late_out, 1)
-    early_in = swap(early_out, 0)
+    late_in = swap(late_out, (1,), 2)
+    early_in = swap(early_out, (0,), 2)
     tiles = own_update(owners, offsets, object_slices, kept)
     tiles = early_update(tiles, early_in)
     return late_update(tiles, late_in)

time: 46.5 us -> 48.3 us (1.039)
  starting transfers between devices: 20.7 us -> 23.2 us
  Pallas kernels: 11.3 us -> 10.8 us
    ppermute x4 -> x5, starting transfers between devices: 18.9 us -> 21.7 us  [swap(): return lax.ppermute(value, 'scan', pairs + [(j, i) for i, j in pairs])]
    pallas_call x2, Pallas kernels: 3.7 us -> 3.06 us  [slice_terms(): pl.pallas_call(functools.partial(terms_kernel, far), out_shape=jax.ShapeD...]
    ppermute x4 -> x5, waiting for transfers between devices: 10.6 us -> 10.3 us  [swap(): return lax.ppermute(value, 'scan', pairs + [(j, i) for i, j in pairs])]
  transfers between devices with their start and end apart: 6 -> 7, of which waited for: 2 -> 2; matrix products, arithmetic and copies ran while one was open for 0% -> 0% of each run, Pallas kernels for 17% -> 15%
where the time goes in v4:
time: 48.3 us; the launch traced here: 48.1 us
  starting transfers between devices  23.2 us (48%)
  Pallas kernels  10.8 us (22%)
  waiting for transfers between devices  10.3 us (21%)
  local copies, waits for them, and re-layouts  2.29 us (5%)
  other arithmetic  1.28 us (3%)
    ppermute x5, starting transfers between devices, swap(): return lax.ppermute(value, 'scan', pairs + [(j, i) for i, j in pairs])  21.7 us
    ppermute x5, waiting for transfers between devices, swap(): return lax.ppermute(value, 'scan', pairs + [(j, i) for i, j in pairs])  10.3 us
    pallas_call x2, Pallas kernels, slice_terms(): pl.pallas_call(functools.partial(terms_kernel, far), out_shape=jax.ShapeD...  3.06 us
    unnamed x12, local copies, waits for them, and re-layouts  2.29 us
    pallas_call x1, Pallas kernels, exit_adjoint(): pl.pallas_call(lambda side, *refs: exit_kernel(*refs), grid_spec=pltpu.Pr...  1.73 us
    pallas_call x1, Pallas kernels, late_update(): pl.pallas_call(late_update_kernel, out_shape=jax.ShapeDtypeStruct(tiles.s...  1.65 us
    ppermute x2, starting transfers between devices, across(): return lax.ppermute(value, 'slab', [(0, 1), (1, 0)])  1.5 us
    convert_element_type x1, other arithmetic, shards(): own = object_slices[0].astype(BF16)  1.28 us
  transfers between devices with their start and end apart: 7, of which 2 were waited for; matrix products, arithmetic and copies ran while one was open for 0% of the time, Pallas kernels for 15%

profile of v4, /device:TPU:1, one launch (start us, length us, event | category | flops | bytes accessed | tf_op | source)
XLA Modules:
  0.0 48.1 jit_solution(2263118290401134427)
XLA Ops:
  0.0 1.3 %convert_bitcast_fusion = bf16[8,128,256]{2,1,0:T(8,128)(2,1)S(1)} fusion(f32[1,8,128,256]{3,2,1,0:T(8,128)} %tiles.1), kind=kLoop, calls=%fused_computation | loop fusion | flops 262144 | bytes 1572864 | tf_op jit(solution)/shard_map/convert_element_type | solution.py:447
  1.3 0.0 copy-start
  1.3 0.0 copy-start.2
  1.3 0.0 copy-start.3
  1.3 4.5 %collective-permute-start.2 = (bf16[8,128,256]{2,1,0:T(8,128)(2,1)S(1)}, bf16[8,128,256]{2,1,0:T(8,128)(2,1)S(1)}, u32[]{:S(2)}, u32[]{:S(2)}) collective-permute-start(bf16[8,128,256]{2,1,0:T(8,128)(2,1)S(1)} %convert_bitcast_fusion), channel_id=1, source_target_pairs={{0,1},{2,3},{4,5},{8,9},{10,11},{12,13},{16,17},{18,19},{20,21},{2... | collective-permute-start | bytes 1572872 | tf_op jit(solution)/shard_map/ppermute | solution.py:438
  5.8 9.3 %collective-permute-start.1 = (bf16[8,128,256]{2,1,0:T(8,128)(2,1)S(1)}, bf16[8,128,256]{2,1,0:T(8,128)(2,1)S(1)}, u32[]{:S(2)}, u32[]{:S(2)}) collective-permute-start(bf16[8,128,256]{2,1,0:T(8,128)(2,1)S(1)} %convert_bitcast_fusion), channel_id=1, source_target_pairs={{5,6},{7,8},{13,14},{15,16},{21,22},{23,24},{29,30},{31,32},{37,38... | collective-permute-start | bytes 1572872 | tf_op jit(solution)/shard_map/ppermute | solution.py:438
  15.1 0.7 %collective-permute-start = (bf16[8,128,256]{2,1,0:T(8,128)(2,1)S(1)}, bf16[8,128,256]{2,1,0:T(8,128)(2,1)S(1)}, u32[]{:S(2)}, u32[]{:S(2)}) collective-permute-start(bf16[8,128,256]{2,1,0:T(8,128)(2,1)S(1)} %convert_bitcast_fusion), channel_id=1, source_target_pairs={{1,2},{3,4},{6,7},{9,10},{11,12},{14,15},{17,18},{19,20},{22,23},{... | collective-permute-start | bytes 1572872 | tf_op jit(solution)/shard_map/ppermute | solution.py:438
  15.8 0.0 copy-start.4
  15.8 1.6 %copy-done.4 = bf16[1,2,4,256,512]{4,3,2,1,0:T(8,128)(2,1)S(1)} copy-done((bf16[1,2,4,256,512]{4,3,2,1,0:T(8,128)(2,1)S(1)}, bf16[1,2,4,256,512]{4,3,2,1,0:T(8,128)(2,1)}, u32[]{:S(2)}) %copy-start.4) | copy-done | bytes 2097176
  17.4 0.0 copy-start.5
  17.4 0.7 %copy-done.5 = bf16[2,2,31]{2,1,0:T(2,128)(2,1)S(1)} copy-done((bf16[2,2,31]{2,1,0:T(2,128)(2,1)S(1)}, bf16[2,2,31]{2,1,0:T(2,128)(2,1)}, u32[]{:S(2)}) %copy-start.5) | copy-done | bytes 272
  18.1 1.7 %exit_adjoint.1 = (bf16[512,512]{1,0:T(8,128)(2,1)S(1)}, bf16[512,512]{1,0:T(8,128)(2,1)S(1)}, bf16[512,512]{1,0:T(8,128)(2,1)S(1)}, bf16[512,512]{1,0:T(8,128)(2,1)S(1)}, bf16[4,512,256]{2,1,0:T(8,128)(2,1)S(1)}) custom-call(s32[1]{0:T(128)} %bitcast.1.side, bf16[2,2,31]{2,1,0:T(2,128)(2,1)S(1)} %copy-done.5, bf16[1,2,4,256,512]{4,3,2,1,0:T(8,128)(2,1)S(1)} %copy-done.4), custom_call_target="tpu_custom_call" | custom-call | flops 1100000000 | bytes 6000000 | tf_op jit(solution)/shard_map/exit_adjoint/pallas_call | solution.py:63
  19.8 0.0 copy-start.1
  19.9 0.0 collective-permute-done.2.first
  19.9 0.0 copy-done
  19.9 0.0 copy-done.2
  19.9 0.0 copy-done.3
  19.9 1.0 %early_windows.1.partly = f32[2,2,256,256]{3,2,1,0:T(8,128)S(1)} custom-call(s32[1,2,9]{2,1,0:T(2,128)S(1)} %copy-done.2, s32[1,2,2]{2,1,0:T(2,128)S(1)} %copy-done.3, f32[1,8,128,256]{3,2,1,0:T(8,128)S(1)} %copy-done, bf16[8,128,256]{2,1,0:T(8,128)(2,1)S(1)} %collective-permute-done.2.first), custom_call_target="tpu_custom_call" | custom-call | flops 2000000 | bytes 2000000 | tf_op jit(solution)/shard_map/early_windows/pallas_call | solution.py:153
  20.9 5.7 %collective-permute-done.1.second = bf16[8,128,256]{2,1,0:T(8,128)(2,1)S(1)} collective-permute-done((bf16[8,128,256]{2,1,0:T(8,128)(2,1)S(1)}, bf16[8,128,256]{2,1,0:T(8,128)(2,1)S(1)}, u32[]{:S(2)}, u32[]{:S(2)}) %collective-permute-start.1) | collective-permute-done | bytes 524320 | tf_op jit(solution)/shard_map/ppermute | solution.py:438
  26.7 0.0 collective-permute-done.third
  26.7 0.8 %late_windows.1 = (bf16[2,256,256]{2,1,0:T(8,128)(2,1)S(1)}, bf16[2,256,256]{2,1,0:T(8,128)(2,1)S(1)}) custom-call(s32[1,2,9]{2,1,0:T(2,128)S(1)} %copy-done.2, s32[1,2,2]{2,1,0:T(2,128)S(1)} %copy-done.3, bf16[8,128,256]{2,1,0:T(8,128)(2,1)S(1)} %collective-permute-done.third, bf16[8,128,256]{2,1,0:T(8,128)(2,1)S(1)} %collective-permute-done.1.second, ...), custom_call_target="tpu_custom_call" | custom-call | flops 1000000 | bytes 2000000 | tf_op jit(solution)/shard_map/late_windows/pallas_call | solution.py:179
  27.5 1.4 %collective-permute-start.3 = (bf16[2,256,256]{2,1,0:T(8,128)(2,1)S(1)}, bf16[2,256,256]{2,1,0:T(8,128)(2,1)S(1)}, u32[]{:S(2)}, u32[]{:S(2)}) collective-permute-start(bf16[2,256,256]{2,1,0:T(8,128)(2,1)S(1)} %get-tuple-element.15), channel_id=1, source_target_pairs={{0,128},{128,0},{1,129},{129,1},{2,130},{130,2},{3,131},{131,3},{4... | collective-permute-start | bytes 786440 | tf_op jit(solution)/shard_map/ppermute | solution.py:442
  28.9 0.0 copy-done.1
  28.9 1.6 %near_terms.1 = bf16[2,256,256]{2,1,0:T(8,128)(2,1)S(1)} custom-call(bf16[2,256,256]{2,1,0:T(8,128)(2,1)S(1)} %get-tuple-element.21.t, bf16[4,256,512]{2,1,0:T(8,128)(2,1)S(1)} %copy-done.1, bf16[4,512,256]{2,1,0:T(8,128)(2,1)S(1)} %get-tuple-element.16.wave, bf16[512,512]{1,0:T(8,128)(2,1)S(1)} %get-tuple-element.17.left, ...), custom_call_target="tpu_custom_call" | custom-call | flops 1100000000 | bytes 5000000 | tf_op jit(solution)/shard_map/near_terms/pallas_call | solution.py:262
  30.5 0.1 collective-permute-start.4
  30.6 0.0 collective-permute-done.3.t
  30.6 1.5 %far_terms.1.mine = f32[2,256,256]{2,1,0:T(8,128)S(1)} custom-call(bf16[2,256,256]{2,1,0:T(8,128)(2,1)S(1)} %collective-permute-done.3.t, bf16[4,256,512]{2,1,0:T(8,128)(2,1)S(1)} %copy-done.1, bf16[4,512,256]{2,1,0:T(8,128)(2,1)S(1)} %get-tuple-element.16.wave, bf16[512,512]{1,0:T(8,128)(2,1)S(1)} %get-tuple-element.17.left, ...), custom_call_target="tpu_custom_call" | custom-call | flops 1100000000 | bytes 5000000 | tf_op jit(solution)/shard_map/far_terms/pallas_call | solution.py:262
  32.1 0.0 collective-permute-done.4.others
  32.1 0.9 %split_terms.1 = (bf16[528,256]{1,0:T(8,128)(2,1)S(1)}, f32[512,256]{1,0:T(8,128)S(1)}, bf16[528,256]{1,0:T(8,128)(2,1)S(1)}) custom-call(s32[1,2,9]{2,1,0:T(2,128)S(1)} %copy-done.2, s32[1,2,2]{2,1,0:T(2,128)S(1)} %copy-done.3, f32[2,256,256]{2,1,0:T(8,128)S(1)} %far_terms.1.mine, bf16[2,256,256]{2,1,0:T(8,128)(2,1)S(1)} %collective-permute-done.4.others), custom_call_target="tpu_custom_call" | custom-call | tf_op jit(solution)/shard_map/split_terms/pallas_call | solution.py:307
  33.0 0.1 collective-permute-start.5
  33.1 7.2 %collective-permute-start.6 = (bf16[528,256]{1,0:T(8,128)(2,1)S(1)}, bf16[528,256]{1,0:T(8,128)(2,1)S(1)}, u32[]{:S(2)}, u32[]{:S(2)}) collective-permute-start(bf16[528,256]{1,0:T(8,128)(2,1)S(1)} %get-tuple-element.24), channel_id=1, source_target_pairs={{1,2},{3,4},{5,6},{7,8},{9,10},{11,12},{13,14},{15,16},{17,18},{19... | collective-permute-start | bytes 811016 | tf_op jit(solution)/shard_map/ppermute | solution.py:438
  40.2 0.8 %own_update.1.tiles = f32[1,8,128,256]{3,2,1,0:T(8,128)S(1)} custom-call(s32[1,2,9]{2,1,0:T(2,128)S(1)} %copy-done.2, s32[1,2,2]{2,1,0:T(2,128)S(1)} %copy-done.3, f32[1,8,128,256]{3,2,1,0:T(8,128)S(1)} %copy-done, f32[512,256]{1,0:T(8,128)S(1)} %get-tuple-element.22.terms), custom_call_target="tpu_custom_call" | custom-call | flops 1000000 | bytes 3000000 | tf_op jit(solution)/shard_map/own_update/pallas_call | solution.py:358
  41.0 0.0 collective-permute-done.5.terms
  41.0 0.8 %early_update.1.tiles = f32[1,8,128,256]{3,2,1,0:T(8,128)S(1)} custom-call(f32[1,8,128,256]{3,2,1,0:T(8,128)S(1)} %own_update.1.tiles, bf16[528,256]{1,0:T(8,128)(2,1)S(1)} %collective-permute-done.5.terms), custom_call_target="tpu_custom_call" | custom-call | flops 1000000 | bytes 3000000 | tf_op jit(solution)/shard_map/early_update/pallas_call | solution.py:394
  41.9 4.6 %collective-permute-done.6.terms = bf16[528,256]{1,0:T(8,128)(2,1)S(1)} collective-permute-done((bf16[528,256]{1,0:T(8,128)(2,1)S(1)}, bf16[528,256]{1,0:T(8,128)(2,1)S(1)}, u32[]{:S(2)}, u32[]{:S(2)}) %collective-permute-start.6) | collective-permute-done | bytes 270368 | tf_op jit(solution)/shard_map/ppermute | solution.py:438
  46.5 1.6 %late_update.1 = f32[1,8,128,256]{3,2,1,0:T(8,128)} custom-call(f32[1,8,128,256]{3,2,1,0:T(8,128)S(1)} %early_update.1.tiles, bf16[528,256]{1,0:T(8,128)(2,1)S(1)} %collective-permute-done.6.terms), custom_call_target="tpu_custom_call" | custom-call | tf_op jit(solution)/shard_map/late_update/pallas_call | solution.py:424
Async XLA Ops:
  1.3 18.6 %copy-start = (f32[1,8,128,256]{3,2,1,0:T(8,128)S(1)}, f32[1,8,128,256]{3,2,1,0:T(8,128)}, u32[]{:S(2)}) copy-start(f32[1,8,128,256]{3,2,1,0:T(8,128)} %tiles.1) | copy-start | bytes 3145732
  1.3 18.6 %copy-start.2 = (s32[1,2,9]{2,1,0:T(2,128)S(1)}, s32[1,2,9]{2,1,0:T(2,128)}, u32[]{:S(2)}) copy-start(s32[1,2,9]{2,1,0:T(2,128)} %owners.7) | copy-start | bytes 220
  1.3 18.6 %copy-start.3 = (s32[1,2,2]{2,1,0:T(2,128)S(1)}, s32[1,2,2]{2,1,0:T(2,128)}, u32[]{:S(2)}) copy-start(s32[1,2,2]{2,1,0:T(2,128)} %offsets.7) | copy-start | bytes 52
  1.3 18.5 %collective-permute-start.2 = (bf16[8,128,256]{2,1,0:T(8,128)(2,1)S(1)}, bf16[8,128,256]{2,1,0:T(8,128)(2,1)S(1)}, u32[]{:S(2)}, u32[]{:S(2)}) collective-permute-start(bf16[8,128,256]{2,1,0:T(8,128)(2,1)S(1)} %convert_bitcast_fusion), channel_id=1, source_target_pairs={{0,1},{2,3},{4,5},{8,9},{10,11},{12,13},{16,17},{18,19},{20,21},{2... | collective-permute-start | bytes 1572872 | tf_op jit(solution)/shard_map/ppermute | solution.py:438
  5.8 20.8 %collective-permute-start.1 = (bf16[8,128,256]{2,1,0:T(8,128)(2,1)S(1)}, bf16[8,128,256]{2,1,0:T(8,128)(2,1)S(1)}, u32[]{:S(2)}, u32[]{:S(2)}) collective-permute-start(bf16[8,128,256]{2,1,0:T(8,128)(2,1)S(1)} %convert_bitcast_fusion), channel_id=1, source_target_pairs={{5,6},{7,8},{13,14},{15,16},{21,22},{23,24},{29,30},{31,32},{37,38... | collective-permute-start | bytes 1572872 | tf_op jit(solution)/shard_map/ppermute | solution.py:438
  15.1 11.5 %collective-permute-start = (bf16[8,128,256]{2,1,0:T(8,128)(2,1)S(1)}, bf16[8,128,256]{2,1,0:T(8,128)(2,1)S(1)}, u32[]{:S(2)}, u32[]{:S(2)}) collective-permute-start(bf16[8,128,256]{2,1,0:T(8,128)(2,1)S(1)} %convert_bitcast_fusion), channel_id=1, source_target_pairs={{1,2},{3,4},{6,7},{9,10},{11,12},{14,15},{17,18},{19,20},{22,23},{... | collective-permute-start | bytes 1572872 | tf_op jit(solution)/shard_map/ppermute | solution.py:438
  15.8 1.6 %copy-start.4 = (bf16[1,2,4,256,512]{4,3,2,1,0:T(8,128)(2,1)S(1)}, bf16[1,2,4,256,512]{4,3,2,1,0:T(8,128)(2,1)}, u32[]{:S(2)}) copy-start(bf16[1,2,4,256,512]{4,3,2,1,0:T(8,128)(2,1)} %refs_1_.1) | copy-start | bytes 6291460
  17.4 0.7 %copy-start.5 = (bf16[2,2,31]{2,1,0:T(2,128)(2,1)S(1)}, bf16[2,2,31]{2,1,0:T(2,128)(2,1)}, u32[]{:S(2)}) copy-start(bf16[2,2,31]{2,1,0:T(2,128)(2,1)} %refs_0_.1) | copy-start | bytes 748
  19.8 9.1 %copy-start.1 = (bf16[4,256,512]{2,1,0:T(8,128)(2,1)S(1)}, bf16[4,256,512]{2,1,0:T(8,128)(2,1)}, u32[]{:S(2)}) copy-start(bf16[4,256,512]{2,1,0:T(8,128)(2,1)} %probe.3) | copy-start | bytes 3145732
  27.5 3.1 %collective-permute-start.3 = (bf16[2,256,256]{2,1,0:T(8,128)(2,1)S(1)}, bf16[2,256,256]{2,1,0:T(8,128)(2,1)S(1)}, u32[]{:S(2)}, u32[]{:S(2)}) collective-permute-start(bf16[2,256,256]{2,1,0:T(8,128)(2,1)S(1)} %get-tuple-element.15), channel_id=1, source_target_pairs={{0,128},{128,0},{1,129},{129,1},{2,130},{130,2},{3,131},{131,3},{4... | collective-permute-start | bytes 786440 | tf_op jit(solution)/shard_map/ppermute | solution.py:442
  30.5 1.6 %collective-permute-start.4 = (bf16[2,256,256]{2,1,0:T(8,128)(2,1)S(1)}, bf16[2,256,256]{2,1,0:T(8,128)(2,1)S(1)}, u32[]{:S(2)}, u32[]{:S(2)}) collective-permute-start(bf16[2,256,256]{2,1,0:T(8,128)(2,1)S(1)} %near_terms.1), channel_id=1, source_target_pairs={{0,128},{128,0},{1,129},{129,1},{2,130},{130,2},{3,131},{131,3},{4... | collective-permute-start | bytes 786440 | tf_op jit(solution)/shard_map/ppermute | solution.py:442
  33.0 8.1 %collective-permute-start.5 = (bf16[528,256]{1,0:T(8,128)(2,1)S(1)}, bf16[528,256]{1,0:T(8,128)(2,1)S(1)}, u32[]{:S(2)}, u32[]{:S(2)}) collective-permute-start(bf16[528,256]{1,0:T(8,128)(2,1)S(1)} %get-tuple-element.23), channel_id=1, source_target_pairs={{0,1},{2,3},{4,5},{6,7},{8,9},{10,11},{12,13},{14,15},{16,17},{18,... | collective-permute-start | bytes 811016 | tf_op jit(solution)/shard_map/ppermute | solution.py:438
  33.1 13.4 %collective-permute-start.6 = (bf16[528,256]{1,0:T(8,128)(2,1)S(1)}, bf16[528,256]{1,0:T(8,128)(2,1)S(1)}, u32[]{:S(2)}, u32[]{:S(2)}) collective-permute-start(bf16[528,256]{1,0:T(8,128)(2,1)S(1)} %get-tuple-element.24), channel_id=1, source_target_pairs={{1,2},{3,4},{5,6},{7,8},{9,10},{11,12},{13,14},{15,16},{17,18},{19... | collective-permute-start | bytes 811016 | tf_op jit(solution)/shard_map/ppermute | solution.py:438

commit v5 on v4

--- a/solution.py
+++ b/solution.py
@@ -275,7 +275,7 @@
     )(t, probe, wave, *mats)
 
 
-def split_kernel(owners, offsets, mine, others, early, own, late):
+def split_kernel(owners, offsets, mine, others, early, late):
     here = lax.axis_index("slab")
     place = lax.broadcasted_iota(jnp.int32, (16, 2 * TS), 1)
     notes = jnp.zeros((16, 2 * TS), jnp.int32)
@@ -297,7 +297,6 @@
                 place = (pl.ds(p * NP + at, STEP), slice(part * TS, (part + 1) * TS))
                 left = jnp.where(spot >= c, low, 0.0)
                 right = jnp.where(spot < c, high, 0.0)
-                own[place] = jnp.where(spot < c, low, high)
                 early[place] = jnp.where(to_right, right, left).astype(BF16)
                 late[place] = jnp.where(to_right, left, right).astype(BF16)
 
@@ -306,9 +305,9 @@
     sent = jax.ShapeDtypeStruct((POS * NP + 16, 2 * TS), BF16)
     return pl.pallas_call(
         split_kernel,
-        out_shape=[sent, jax.ShapeDtypeStruct((POS * NP, 2 * TS), F32), sent],
+        out_shape=[sent, sent],
         in_specs=[SMEM, SMEM, VMEM, VMEM],
-        out_specs=[VMEM] * 3,
+        out_specs=[VMEM] * 2,
         compiler_params=params(8),
         name="split_terms",
     )(owners, offsets, mine, others)
@@ -317,13 +316,19 @@
 STACK = pltpu.VMEM((POS, 2, 2 * TS + NP, TS), F32)
 
 
+def clear(stack):
+    for p in range(POS):
+        for part in range(2):
+            stack[p, part, :TS, :] = jnp.zeros((TS, TS), F32)
+            stack[p, part, TS + NP :, :] = jnp.zeros((TS, TS), F32)
+
+
 def fill(terms, stack):
+    clear(stack)
     for p in range(POS):
         for part in range(2):
             cols = slice(part * TS, (part + 1) * TS)
-            stack[p, part, :TS, :] = jnp.zeros((TS, TS), F32)
             stack[p, part, TS : TS + NP, :] = terms[p * NP : (p + 1) * NP, cols].astype(F32) * step_rate
-            stack[p, part, TS + NP :, :] = jnp.zeros((TS, TS), F32)
 
 
 def take_off(slots, rows, stack, tiles, done):
@@ -348,23 +353,33 @@
     return done
 
 
-def own_kernel(owners, offsets, tiles, terms, out, stack):
+def own_kernel(owners, offsets, tiles, mine, others, out, stack):
+    here = lax.axis_index("slab")
+    spot = lanes(STEP)
+    clear(stack)
+    for k, terms in ((0, mine), (1, others)):
+        p = here if k == 0 else 1 - here
+        c = offsets[0, p, 1]
+        for at in range(0, NP, STEP):
+            for part in range(2):
+                low = pltpu.roll(terms[part, at : at + STEP, 0:TS].astype(F32), c, 1)
+                high = pltpu.roll(terms[part, at : at + STEP, TS:].astype(F32), c, 1)
+                stack[p, part, TS + at : TS + at + STEP, :] = jnp.where(spot < c, low, high) * step_rate
     slots = [[owners[0, p, 3 * i + 1] & (CAP - 1) for i in range(3)] for p in range(POS)]
-    fill(terms, stack)
     take_off(slots, [offsets[0, p, 0] for p in range(POS)], stack, tiles, keep(out))
 
 
-def own_update(owners, offsets, tiles, terms):
+def own_update(owners, offsets, tiles, mine, others):
     return pl.pallas_call(
         own_kernel,
         out_shape=jax.ShapeDtypeStruct(tiles.shape, F32),
-        in_specs=[SMEM, SMEM, VMEM, VMEM],
+        in_specs=[SMEM, SMEM, VMEM, VMEM, VMEM],
         out_specs=VMEM,
         scratch_shapes=[STACK],
         compiler_params=params(8),
         cost_estimate=pl.CostEstimate(flops=1_000_000, bytes_accessed=3_000_000, transcendentals=0),
         name="own_update",
-    )(owners, offsets, tiles, terms)
+    )(owners, offsets, tiles, mine, others)
 
 
 def read_notes(j, terms, lines, notes, sem):
@@ -435,7 +450,9 @@
 def swap(value, members, period):
     count = lax.axis_size("scan")
     pairs = [(i, (i + 1) % count) for i in range(count) if i % period in members]
-    return lax.ppermute(value, "scan", pairs + [(j, i) for i, j in pairs])
+    pairs += [(j, i) for i, j in pairs]
+    inside = {i for i, _ in pairs}
+    return lax.ppermute(value, "scan", pairs + [(i, i) for i in range(count) if i not in inside])
 
 
 def across(value):
@@ -453,10 +470,10 @@
     terms_there = slice_terms(False, t_near, probe_modes, wave, mats)
     terms_far = across(terms_there)
     terms_here = slice_terms(True, t_here, probe_modes, wave, mats)
-    early_out, kept, late_out = split_terms(owners, offsets, terms_here, terms_far)
+    early_out, late_out = split_terms(owners, offsets, terms_here, terms_far)
     late_in = swap(late_out, (1,), 2)
     early_in = swap(early_out, (0,), 2)
-    tiles = own_update(owners, offsets, object_slices, kept)
+    tiles = own_update(owners, offsets, object_slices, terms_here, terms_far)
     tiles = early_update(tiles, early_in)
     return late_update(tiles, late_in)
 

time: 48.3 us -> 48.3 us (level)
  transfers between devices with their start and end apart: 7 -> 7, of which waited for: 2 -> 2; matrix products, arithmetic and copies ran while one was open for 0% -> 0% of each run, Pallas kernels for 15% -> 16%
where the time goes in v5:
time: 48.3 us; the launch traced here: 48 us
  starting transfers between devices  23.2 us (48%)
  Pallas kernels  10.9 us (23%)
  waiting for transfers between devices  10.1 us (21%)
  local copies, waits for them, and re-layouts  2.29 us (5%)
  other arithmetic  1.28 us (3%)
    ppermute x5, starting transfers between devices, swap(): lax.ppermute(value, 'scan', pairs + [(i, i) for i in range(count) if i no...  21.7 us
    ppermute x5, waiting for transfers between devices, swap(): lax.ppermute(value, 'scan', pairs + [(i, i) for i in range(count) if i no...  10.1 us
    pallas_call x2, Pallas kernels, slice_terms(): pl.pallas_call(functools.partial(terms_kernel, far), out_shape=jax.ShapeD...  3.06 us
    unnamed x12, local copies, waits for them, and re-layouts  2.29 us
    pallas_call x1, Pallas kernels, exit_adjoint(): pl.pallas_call(lambda side, *refs: exit_kernel(*refs), grid_spec=pltpu.Pr...  1.73 us
    pallas_call x1, Pallas kernels, late_update(): pl.pallas_call(late_update_kernel, out_shape=jax.ShapeDtypeStruct(tiles.s...  1.64 us
    ppermute x2, starting transfers between devices, across(): return lax.ppermute(value, 'slab', [(0, 1), (1, 0)])  1.5 us
    convert_element_type x1, other arithmetic, shards(): own = object_slices[0].astype(BF16)  1.28 us
  transfers between devices with their start and end apart: 7, of which 2 were waited for; matrix products, arithmetic and copies ran while one was open for 0% of the time, Pallas kernels for 16%

profile of v5, /device:TPU:1, one launch (start us, length us, event | category | flops | bytes accessed | tf_op | source)
XLA Modules:
  0.0 48.0 jit_solution(5171306414956010537)
XLA Ops:
  0.0 1.3 %convert_bitcast_fusion = bf16[8,128,256]{2,1,0:T(8,128)(2,1)S(1)} fusion(f32[1,8,128,256]{3,2,1,0:T(8,128)} %tiles.1), kind=kLoop, calls=%fused_computation | loop fusion | flops 262144 | bytes 1572864 | tf_op jit(solution)/shard_map/convert_element_type | solution.py:464
  1.3 0.0 copy-start
  1.3 0.0 copy-start.2
  1.3 0.0 copy-start.3
  1.3 4.5 %collective-permute-start.2 = (bf16[8,128,256]{2,1,0:T(8,128)(2,1)S(1)}, bf16[8,128,256]{2,1,0:T(8,128)(2,1)S(1)}, u32[]{:S(2)}, u32[]{:S(2)}) collective-permute-start(bf16[8,128,256]{2,1,0:T(8,128)(2,1)S(1)} %convert_bitcast_fusion), channel_id=1, source_target_pairs={{0,1},{2,3},{4,5},{8,9},{10,11},{12,13},{16,17},{18,19},{20,21},{2... | collective-permute-start | bytes 1572872 | tf_op jit(solution)/shard_map/ppermute | solution.py:455
  5.8 9.3 %collective-permute-start.1 = (bf16[8,128,256]{2,1,0:T(8,128)(2,1)S(1)}, bf16[8,128,256]{2,1,0:T(8,128)(2,1)S(1)}, u32[]{:S(2)}, u32[]{:S(2)}) collective-permute-start(bf16[8,128,256]{2,1,0:T(8,128)(2,1)S(1)} %convert_bitcast_fusion), channel_id=1, source_target_pairs={{5,6},{7,8},{13,14},{15,16},{21,22},{23,24},{29,30},{31,32},{37,38... | collective-permute-start | bytes 1572872 | tf_op jit(solution)/shard_map/ppermute | solution.py:455
  15.1 0.7 %collective-permute-start = (bf16[8,128,256]{2,1,0:T(8,128)(2,1)S(1)}, bf16[8,128,256]{2,1,0:T(8,128)(2,1)S(1)}, u32[]{:S(2)}, u32[]{:S(2)}) collective-permute-start(bf16[8,128,256]{2,1,0:T(8,128)(2,1)S(1)} %convert_bitcast_fusion), channel_id=1, source_target_pairs={{1,2},{3,4},{6,7},{9,10},{11,12},{14,15},{17,18},{19,20},{22,23},{... | collective-permute-start | bytes 1572872 | tf_op jit(solution)/shard_map/ppermute | solution.py:455
  15.8 0.0 copy-start.4
  15.8 1.6 %copy-done.4 = bf16[1,2,4,256,512]{4,3,2,1,0:T(8,128)(2,1)S(1)} copy-done((bf16[1,2,4,256,512]{4,3,2,1,0:T(8,128)(2,1)S(1)}, bf16[1,2,4,256,512]{4,3,2,1,0:T(8,128)(2,1)}, u32[]{:S(2)}) %copy-start.4) | copy-done | bytes 2097176
  17.4 0.0 copy-start.5
  17.4 0.7 %copy-done.5 = bf16[2,2,31]{2,1,0:T(2,128)(2,1)S(1)} copy-done((bf16[2,2,31]{2,1,0:T(2,128)(2,1)S(1)}, bf16[2,2,31]{2,1,0:T(2,128)(2,1)}, u32[]{:S(2)}) %copy-start.5) | copy-done | bytes 272
  18.1 1.7 %exit_adjoint.1 = (bf16[512,512]{1,0:T(8,128)(2,1)S(1)}, bf16[512,512]{1,0:T(8,128)(2,1)S(1)}, bf16[512,512]{1,0:T(8,128)(2,1)S(1)}, bf16[512,512]{1,0:T(8,128)(2,1)S(1)}, bf16[4,512,256]{2,1,0:T(8,128)(2,1)S(1)}) custom-call(s32[1]{0:T(128)} %bitcast.1.side, bf16[2,2,31]{2,1,0:T(2,128)(2,1)S(1)} %copy-done.5, bf16[1,2,4,256,512]{4,3,2,1,0:T(8,128)(2,1)S(1)} %copy-done.4), custom_call_target="tpu_custom_call" | custom-call | flops 1100000000 | bytes 6000000 | tf_op jit(solution)/shard_map/exit_adjoint/pallas_call | solution.py:63
  19.8 0.0 copy-start.1
  19.9 0.0 collective-permute-done.2.first
  19.9 0.0 copy-done
  19.9 0.0 copy-done.2
  19.9 0.0 copy-done.3
  19.9 1.0 %early_windows.1.partly = f32[2,2,256,256]{3,2,1,0:T(8,128)S(1)} custom-call(s32[1,2,9]{2,1,0:T(2,128)S(1)} %copy-done.2, s32[1,2,2]{2,1,0:T(2,128)S(1)} %copy-done.3, f32[1,8,128,256]{3,2,1,0:T(8,128)S(1)} %copy-done, bf16[8,128,256]{2,1,0:T(8,128)(2,1)S(1)} %collective-permute-done.2.first), custom_call_target="tpu_custom_call" | custom-call | flops 2000000 | bytes 2000000 | tf_op jit(solution)/shard_map/early_windows/pallas_call | solution.py:153
  20.9 5.7 %collective-permute-done.1.second = bf16[8,128,256]{2,1,0:T(8,128)(2,1)S(1)} collective-permute-done((bf16[8,128,256]{2,1,0:T(8,128)(2,1)S(1)}, bf16[8,128,256]{2,1,0:T(8,128)(2,1)S(1)}, u32[]{:S(2)}, u32[]{:S(2)}) %collective-permute-start.1) | collective-permute-done | bytes 524320 | tf_op jit(solution)/shard_map/ppermute | solution.py:455
  26.7 0.0 collective-permute-done.third
  26.7 0.8 %late_windows.1 = (bf16[2,256,256]{2,1,0:T(8,128)(2,1)S(1)}, bf16[2,256,256]{2,1,0:T(8,128)(2,1)S(1)}) custom-call(s32[1,2,9]{2,1,0:T(2,128)S(1)} %copy-done.2, s32[1,2,2]{2,1,0:T(2,128)S(1)} %copy-done.3, bf16[8,128,256]{2,1,0:T(8,128)(2,1)S(1)} %collective-permute-done.third, bf16[8,128,256]{2,1,0:T(8,128)(2,1)S(1)} %collective-permute-done.1.second, ...), custom_call_target="tpu_custom_call" | custom-call | flops 1000000 | bytes 2000000 | tf_op jit(solution)/shard_map/late_windows/pallas_call | solution.py:179
  27.5 1.4 %collective-permute-start.3 = (bf16[2,256,256]{2,1,0:T(8,128)(2,1)S(1)}, bf16[2,256,256]{2,1,0:T(8,128)(2,1)S(1)}, u32[]{:S(2)}, u32[]{:S(2)}) collective-permute-start(bf16[2,256,256]{2,1,0:T(8,128)(2,1)S(1)} %get-tuple-element.14), channel_id=1, source_target_pairs={{0,128},{128,0},{1,129},{129,1},{2,130},{130,2},{3,131},{131,3},{4... | collective-permute-start | bytes 786440 | tf_op jit(solution)/shard_map/ppermute | solution.py:459
  28.9 0.0 copy-done.1
  28.9 1.6 %near_terms.1 = bf16[2,256,256]{2,1,0:T(8,128)(2,1)S(1)} custom-call(bf16[2,256,256]{2,1,0:T(8,128)(2,1)S(1)} %get-tuple-element.20.t, bf16[4,256,512]{2,1,0:T(8,128)(2,1)S(1)} %copy-done.1, bf16[4,512,256]{2,1,0:T(8,128)(2,1)S(1)} %get-tuple-element.15.wave, bf16[512,512]{1,0:T(8,128)(2,1)S(1)} %get-tuple-element.16.left, ...), custom_call_target="tpu_custom_call" | custom-call | flops 1100000000 | bytes 5000000 | tf_op jit(solution)/shard_map/near_terms/pallas_call | solution.py:262
  30.5 0.1 collective-permute-start.4
  30.6 0.0 collective-permute-done.3.t
  30.6 1.5 %far_terms.1.mine = f32[2,256,256]{2,1,0:T(8,128)S(1)} custom-call(bf16[2,256,256]{2,1,0:T(8,128)(2,1)S(1)} %collective-permute-done.3.t, bf16[4,256,512]{2,1,0:T(8,128)(2,1)S(1)} %copy-done.1, bf16[4,512,256]{2,1,0:T(8,128)(2,1)S(1)} %get-tuple-element.15.wave, bf16[512,512]{1,0:T(8,128)(2,1)S(1)} %get-tuple-element.16.left, ...), custom_call_target="tpu_custom_call" | custom-call | flops 1100000000 | bytes 5000000 | tf_op jit(solution)/shard_map/far_terms/pallas_call | solution.py:262
  32.1 0.0 collective-permute-done.4.others
  32.1 0.8 %split_terms.1 = (bf16[528,256]{1,0:T(8,128)(2,1)S(1)}, bf16[528,256]{1,0:T(8,128)(2,1)S(1)}) custom-call(s32[1,2,9]{2,1,0:T(2,128)S(1)} %copy-done.2, s32[1,2,2]{2,1,0:T(2,128)S(1)} %copy-done.3, f32[2,256,256]{2,1,0:T(8,128)S(1)} %far_terms.1.mine, bf16[2,256,256]{2,1,0:T(8,128)(2,1)S(1)} %collective-permute-done.4.others), custom_call_target="tpu_custom_call" | custom-call | tf_op jit(solution)/shard_map/split_terms/pallas_call | solution.py:306
  32.9 0.1 collective-permute-start.5
  33.0 7.2 %collective-permute-start.6 = (bf16[528,256]{1,0:T(8,128)(2,1)S(1)}, bf16[528,256]{1,0:T(8,128)(2,1)S(1)}, u32[]{:S(2)}, u32[]{:S(2)}) collective-permute-start(bf16[528,256]{1,0:T(8,128)(2,1)S(1)} %get-tuple-element.22), channel_id=1, source_target_pairs={{1,2},{3,4},{5,6},{7,8},{9,10},{11,12},{13,14},{15,16},{17,18},{19... | collective-permute-start | bytes 811016 | tf_op jit(solution)/shard_map/ppermute | solution.py:455
  40.2 1.0 %own_update.1.tiles = f32[1,8,128,256]{3,2,1,0:T(8,128)S(1)} custom-call(s32[1,2,9]{2,1,0:T(2,128)S(1)} %copy-done.2, s32[1,2,2]{2,1,0:T(2,128)S(1)} %copy-done.3, f32[1,8,128,256]{3,2,1,0:T(8,128)S(1)} %copy-done, f32[2,256,256]{2,1,0:T(8,128)S(1)} %far_terms.1.mine, bf16[2,256,256]{2,1,0:T(8,128)(2,1)S(1)} %collective-permute-done.4.others), custom_call_target="tpu_custom_call" | custom-call | flops 1000000 | bytes 3000000 | tf_op jit(solution)/shard_map/own_update/pallas_call | solution.py:373
  41.2 0.0 collective-permute-done.5.terms
  41.2 0.8 %early_update.1.tiles = f32[1,8,128,256]{3,2,1,0:T(8,128)S(1)} custom-call(f32[1,8,128,256]{3,2,1,0:T(8,128)S(1)} %own_update.1.tiles, bf16[528,256]{1,0:T(8,128)(2,1)S(1)} %collective-permute-done.5.terms), custom_call_target="tpu_custom_call" | custom-call | flops 1000000 | bytes 3000000 | tf_op jit(solution)/shard_map/early_update/pallas_call | solution.py:409
  42.0 4.4 %collective-permute-done.6.terms = bf16[528,256]{1,0:T(8,128)(2,1)S(1)} collective-permute-done((bf16[528,256]{1,0:T(8,128)(2,1)S(1)}, bf16[528,256]{1,0:T(8,128)(2,1)S(1)}, u32[]{:S(2)}, u32[]{:S(2)}) %collective-permute-start.6) | collective-permute-done | bytes 270368 | tf_op jit(solution)/shard_map/ppermute | solution.py:455
  46.4 1.6 %late_update.1 = f32[1,8,128,256]{3,2,1,0:T(8,128)} custom-call(f32[1,8,128,256]{3,2,1,0:T(8,128)S(1)} %early_update.1.tiles, bf16[528,256]{1,0:T(8,128)(2,1)S(1)} %collective-permute-done.6.terms), custom_call_target="tpu_custom_call" | custom-call | tf_op jit(solution)/shard_map/late_update/pallas_call | solution.py:439
Async XLA Ops:
  1.3 18.6 %copy-start = (f32[1,8,128,256]{3,2,1,0:T(8,128)S(1)}, f32[1,8,128,256]{3,2,1,0:T(8,128)}, u32[]{:S(2)}) copy-start(f32[1,8,128,256]{3,2,1,0:T(8,128)} %tiles.1) | copy-start | bytes 3145732
  1.3 18.6 %copy-start.2 = (s32[1,2,9]{2,1,0:T(2,128)S(1)}, s32[1,2,9]{2,1,0:T(2,128)}, u32[]{:S(2)}) copy-start(s32[1,2,9]{2,1,0:T(2,128)} %owners.7) | copy-start | bytes 220
  1.3 18.6 %copy-start.3 = (s32[1,2,2]{2,1,0:T(2,128)S(1)}, s32[1,2,2]{2,1,0:T(2,128)}, u32[]{:S(2)}) copy-start(s32[1,2,2]{2,1,0:T(2,128)} %offsets.7) | copy-start | bytes 52
  1.3 18.5 %collective-permute-start.2 = (bf16[8,128,256]{2,1,0:T(8,128)(2,1)S(1)}, bf16[8,128,256]{2,1,0:T(8,128)(2,1)S(1)}, u32[]{:S(2)}, u32[]{:S(2)}) collective-permute-start(bf16[8,128,256]{2,1,0:T(8,128)(2,1)S(1)} %convert_bitcast_fusion), channel_id=1, source_target_pairs={{0,1},{2,3},{4,5},{8,9},{10,11},{12,13},{16,17},{18,19},{20,21},{2... | collective-permute-start | bytes 1572872 | tf_op jit(solution)/shard_map/ppermute | solution.py:455
  5.8 20.8 %collective-permute-start.1 = (bf16[8,128,256]{2,1,0:T(8,128)(2,1)S(1)}, bf16[8,128,256]{2,1,0:T(8,128)(2,1)S(1)}, u32[]{:S(2)}, u32[]{:S(2)}) collective-permute-start(bf16[8,128,256]{2,1,0:T(8,128)(2,1)S(1)} %convert_bitcast_fusion), channel_id=1, source_target_pairs={{5,6},{7,8},{13,14},{15,16},{21,22},{23,24},{29,30},{31,32},{37,38... | collective-permute-start | bytes 1572872 | tf_op jit(solution)/shard_map/ppermute | solution.py:455
  15.1 11.5 %collective-permute-start = (bf16[8,128,256]{2,1,0:T(8,128)(2,1)S(1)}, bf16[8,128,256]{2,1,0:T(8,128)(2,1)S(1)}, u32[]{:S(2)}, u32[]{:S(2)}) collective-permute-start(bf16[8,128,256]{2,1,0:T(8,128)(2,1)S(1)} %convert_bitcast_fusion), channel_id=1, source_target_pairs={{1,2},{3,4},{6,7},{9,10},{11,12},{14,15},{17,18},{19,20},{22,23},{... | collective-permute-start | bytes 1572872 | tf_op jit(solution)/shard_map/ppermute | solution.py:455
  15.8 1.6 %copy-start.4 = (bf16[1,2,4,256,512]{4,3,2,1,0:T(8,128)(2,1)S(1)}, bf16[1,2,4,256,512]{4,3,2,1,0:T(8,128)(2,1)}, u32[]{:S(2)}) copy-start(bf16[1,2,4,256,512]{4,3,2,1,0:T(8,128)(2,1)} %refs_1_.1) | copy-start | bytes 6291460
  17.4 0.7 %copy-start.5 = (bf16[2,2,31]{2,1,0:T(2,128)(2,1)S(1)}, bf16[2,2,31]{2,1,0:T(2,128)(2,1)}, u32[]{:S(2)}) copy-start(bf16[2,2,31]{2,1,0:T(2,128)(2,1)} %refs_0_.1) | copy-start | bytes 748
  19.8 9.1 %copy-start.1 = (bf16[4,256,512]{2,1,0:T(8,128)(2,1)S(1)}, bf16[4,256,512]{2,1,0:T(8,128)(2,1)}, u32[]{:S(2)}) copy-start(bf16[4,256,512]{2,1,0:T(8,128)(2,1)} %probe.3) | copy-start | bytes 3145732
  27.5 3.1 %collective-permute-start.3 = (bf16[2,256,256]{2,1,0:T(8,128)(2,1)S(1)}, bf16[2,256,256]{2,1,0:T(8,128)(2,1)S(1)}, u32[]{:S(2)}, u32[]{:S(2)}) collective-permute-start(bf16[2,256,256]{2,1,0:T(8,128)(2,1)S(1)} %get-tuple-element.14), channel_id=1, source_target_pairs={{0,128},{128,0},{1,129},{129,1},{2,130},{130,2},{3,131},{131,3},{4... | collective-permute-start | bytes 786440 | tf_op jit(solution)/shard_map/ppermute | solution.py:459
  30.5 1.6 %collective-permute-start.4 = (bf16[2,256,256]{2,1,0:T(8,128)(2,1)S(1)}, bf16[2,256,256]{2,1,0:T(8,128)(2,1)S(1)}, u32[]{:S(2)}, u32[]{:S(2)}) collective-permute-start(bf16[2,256,256]{2,1,0:T(8,128)(2,1)S(1)} %near_terms.1), channel_id=1, source_target_pairs={{0,128},{128,0},{1,129},{129,1},{2,130},{130,2},{3,131},{131,3},{4... | collective-permute-start | bytes 786440 | tf_op jit(solution)/shard_map/ppermute | solution.py:459
  32.9 8.3 %collective-permute-start.5 = (bf16[528,256]{1,0:T(8,128)(2,1)S(1)}, bf16[528,256]{1,0:T(8,128)(2,1)S(1)}, u32[]{:S(2)}, u32[]{:S(2)}) collective-permute-start(bf16[528,256]{1,0:T(8,128)(2,1)S(1)} %get-tuple-element.21), channel_id=1, source_target_pairs={{0,1},{2,3},{4,5},{6,7},{8,9},{10,11},{12,13},{14,15},{16,17},{18,... | collective-permute-start | bytes 811016 | tf_op jit(solution)/shard_map/ppermute | solution.py:455
  33.0 13.4 %collective-permute-start.6 = (bf16[528,256]{1,0:T(8,128)(2,1)S(1)}, bf16[528,256]{1,0:T(8,128)(2,1)S(1)}, u32[]{:S(2)}, u32[]{:S(2)}) collective-permute-start(bf16[528,256]{1,0:T(8,128)(2,1)S(1)} %get-tuple-element.22), channel_id=1, source_target_pairs={{1,2},{3,4},{5,6},{7,8},{9,10},{11,12},{13,14},{15,16},{17,18},{19... | collective-permute-start | bytes 811016 | tf_op jit(solution)/shard_map/ppermute | solution.py:455

commit v6 on v5

--- a/solution.py
+++ b/solution.py
@@ -12,7 +12,6 @@
 NP, TS, HALF = 256, 128, 15
 MODES, POS, CAP = 4, 2, 8
 STEP = 32
-SMEM = pl.BlockSpec(memory_space=pltpu.SMEM)
 VMEM = pl.BlockSpec(memory_space=pltpu.VMEM)
 HBM = pl.BlockSpec(memory_space=pltpu.HBM)
 
@@ -23,6 +22,15 @@
 
 def dot(left, right):
     return jnp.dot(left, right, preferred_element_type=F32)
+
+
+class Table:
+    def __init__(self, values):
+        self.values = values.astype(F32)
+        self.row, self.lane = (lax.broadcasted_iota(jnp.int32, values.shape, axis) for axis in range(2))
+
+    def at(self, row, lane):
+        return jnp.sum(jnp.where((self.row == row) & (self.lane == lane), self.values, 0.0)).astype(jnp.int32)
 
 
 def lanes(rows):
@@ -80,16 +88,6 @@
     )(side, taps, residual)
 
 
-FIRST, SECOND, THIRD = (0, 2, 4), (5, 7), (1, 3, 6)
-
-
-def part_in(members):
-    z = lax.axis_index("scan") % 8
-    right = functools.reduce(jnp.logical_or, [z == i for i in members])
-    left = functools.reduce(jnp.logical_or, [z == (i + 1) % 8 for i in members])
-    return jnp.logical_or(left, right), right.astype(jnp.int32)
-
-
 def early_side():
     return 1 - lax.axis_index("scan") % 2
 
@@ -104,10 +102,10 @@
 
 def cut_column(p, j, owners, offsets, tile_at, stack, put):
     for i in range(3):
-        tile = tile_at(owners[0, p, 3 * i + j] & (CAP - 1))
+        tile = tile_at(owners.at(p, 3 * i + j) & (CAP - 1))
         stack[0, i * TS : (i + 1) * TS, :] = tile[:, :TS]
         stack[1, i * TS : (i + 1) * TS, :] = tile[:, TS:]
-    r, c = offsets[0, p, 0], offsets[0, p, 1]
+    r, c = offsets.at(p, 0), offsets.at(p, 1)
     back = (TS - c) & (TS - 1)
     for at in range(0, NP, STEP):
         for part in range(2):
@@ -123,8 +121,9 @@
     return past * (1 - 2 * side) - side < 0
 
 
-def early_kernel(owners, offsets, own, first, out, stack):
-    inside, side = part_in(FIRST)
+def early_kernel(owners, offsets, own, early, out, stack):
+    owners, offsets = Table(owners[0]), Table(offsets[0])
+    side = early_side()
     for p in range(POS):
 
         def put_own(part, at, turned):
@@ -132,60 +131,59 @@
             out[p, part, at : at + STEP, TS:] = turned
 
         cut_column(p, 1, owners, offsets, plain_tile(own), stack.at[0], put_own)
-
-    @pl.when(inside)
-    def _():
-        for p in range(POS):
-            overlay(p, side, owners, offsets, first, stack.at[1], out.at[p], out.at[p])
-
-
-def overlay(p, side, owners, offsets, tiles, stack, base, out):
-    mask = taken(side, offsets[0, p, 1])
-
-    def put(part, at, turned):
-        place = (part, slice(at, at + STEP), half(side))
-        out[place] = jnp.where(mask, turned, base[place]).astype(out.dtype)
-
-    cut_column(p, 2 * side, owners, offsets, packed_tile(tiles), stack, put)
-
-
-def early_windows(owners, offsets, own, first):
+        mask = taken(side, offsets.at(p, 1))
+
+        def put_early(part, at, turned):
+            place = (p, part, slice(at, at + STEP), half(side))
+            out[place] = jnp.where(mask, turned, out[place])
+
+        cut_column(p, 2 * side, owners, offsets, packed_tile(early), stack.at[1], put_early)
+
+
+def early_windows(owners, offsets, own, early):
     return pl.pallas_call(
         early_kernel,
         out_shape=jax.ShapeDtypeStruct((POS, 2, NP, NP), F32),
-        in_specs=[SMEM, SMEM, VMEM, VMEM],
+        in_specs=[VMEM] * 4,
         out_specs=VMEM,
         scratch_shapes=[pltpu.VMEM((2, 2, 3 * TS, TS), F32)],
         compiler_params=params(8),
         cost_estimate=pl.CostEstimate(flops=2_000_000, bytes_accessed=2_000_000, transcendentals=0),
         name="early_windows",
-    )(owners, offsets, own, first)
-
-
-def late_kernel(owners, offsets, third, second, partly, far, near, stack):
+    )(owners, offsets, own, early)
+
+
+def complete(p, owners, offsets, late, partly, stack, out):
+    side = 1 - early_side()
+    mask = taken(side, offsets.at(p, 1))
+
+    def put(part, at, turned):
+        rows = slice(at, at + STEP)
+        kept = partly[p, part, rows, half(side)]
+        out[part, rows, half(side)] = jnp.where(mask, turned, kept).astype(out.dtype)
+        out[part, rows, half(1 - side)] = partly[p, part, rows, half(1 - side)].astype(out.dtype)
+
+    cut_column(p, 2 * side, owners, offsets, packed_tile(late), stack, put)
+
+
+def late_kernel(owners, offsets, late, partly, far, near, stack):
+    owners, offsets = Table(owners[0]), Table(offsets[0])
     here = lax.axis_index("slab")
-    far[...] = partly[1 - here].astype(BF16)
-    near[...] = partly[here].astype(BF16)
-    for k, (members, tiles) in enumerate(((SECOND, second), (THIRD, third))):
-        inside, side = part_in(members)
-
-        @pl.when(inside)
-        def _():
-            for n, (p, out) in enumerate(((1 - here, far), (here, near))):
-                overlay(p, side, owners, offsets, tiles, stack.at[2 * k + n], partly.at[p], out)
-
-
-def late_windows(owners, offsets, second, third, partly):
+    complete(1 - here, owners, offsets, late, partly, stack.at[0], far)
+    complete(here, owners, offsets, late, partly, stack.at[1], near)
+
+
+def late_windows(owners, offsets, late, partly):
     return pl.pallas_call(
         late_kernel,
         out_shape=[jax.ShapeDtypeStruct((2, NP, NP), BF16)] * 2,
-        in_specs=[SMEM, SMEM, VMEM, VMEM, VMEM],
+        in_specs=[VMEM] * 4,
         out_specs=[VMEM] * 2,
-        scratch_shapes=[pltpu.VMEM((4, 2, 3 * TS, TS), F32)],
+        scratch_shapes=[pltpu.VMEM((2, 2, 3 * TS, TS), F32)],
         compiler_params=params(8),
         cost_estimate=pl.CostEstimate(flops=1_000_000, bytes_accessed=2_000_000, transcendentals=0),
         name="late_windows",
-    )(owners, offsets, third, second, partly)
+    )(owners, offsets, late, partly)
 
 
 def times(a, b, conjugate):
@@ -275,21 +273,19 @@
     )(t, probe, wave, *mats)
 
 
-def split_kernel(owners, offsets, mine, others, early, late):
+def split_kernel(owners, offsets, mine, others, early, late, notes):
     here = lax.axis_index("slab")
-    place = lax.broadcasted_iota(jnp.int32, (16, 2 * TS), 1)
-    notes = jnp.zeros((16, 2 * TS), jnp.int32)
-    for p in range(POS):
-        for k in range(9):
-            notes = jnp.where(place == p * 16 + k, owners[0, p, k] & (CAP - 1), notes)
-        notes = jnp.where(place == p * 16 + 9, offsets[0, p, 0], notes)
-    early[POS * NP :, :] = notes.astype(F32).astype(BF16)
-    late[POS * NP :, :] = notes.astype(F32).astype(BF16)
+    notes[...] = jnp.zeros_like(notes)
+    notes[0:POS, 0:9] = (owners[0] & (CAP - 1)).astype(F32)
+    notes[POS : 2 * POS, 0:2] = offsets[0].astype(F32)
+    early[POS * NP :, :] = notes[...].astype(BF16)
+    late[POS * NP :, :] = notes[...].astype(BF16)
+    offsets = Table(offsets[0])
     to_right = early_side() == 1
     spot = lanes(STEP)
     for k, terms in ((0, mine), (1, others)):
         p = here if k == 0 else 1 - here
-        c = offsets[0, p, 1]
+        c = offsets.at(p, 1)
         for at in range(0, NP, STEP):
             for part in range(2):
                 low = pltpu.roll(terms[part, at : at + STEP, 0:TS].astype(F32), c, 1)
@@ -306,8 +302,9 @@
     return pl.pallas_call(
         split_kernel,
         out_shape=[sent, sent],
-        in_specs=[SMEM, SMEM, VMEM, VMEM],
+        in_specs=[VMEM] * 4,
         out_specs=[VMEM] * 2,
+        scratch_shapes=[pltpu.VMEM((16, 2 * TS), F32)],
         compiler_params=params(8),
         name="split_terms",
     )(owners, offsets, mine, others)
@@ -331,49 +328,44 @@
             stack[p, part, TS : TS + NP, :] = terms[p * NP : (p + 1) * NP, cols].astype(F32) * step_rate
 
 
-def take_off(slots, rows, stack, tiles, done):
-    for q in range(CAP):
-        starts = []
+def take_off(q, slots, rows, stack, tiles, out):
+    starts = []
+    for p in range(POS):
+        start = jnp.int32(0)
+        for i in range(3):
+            start = jnp.where(slots[p][i] == q, TS + i * TS - rows[p], start)
+        starts.append(start)
+    for part in range(2):
+        cols = slice(part * TS, (part + 1) * TS)
+        tile = tiles[0, q, :, cols]
         for p in range(POS):
-            start = jnp.int32(0)
-            for i in range(3):
-                start = jnp.where(slots[p][i] == q, TS + i * TS - rows[p], start)
-            starts.append(start)
-        for part in range(2):
-            tile = tiles[0, q, :, part * TS : (part + 1) * TS]
-            for p in range(POS):
-                tile = tile - stack[p, part, pl.ds(starts[p], TS), :]
-            done(q, part, tile)
-
-
-def keep(out):
-    def done(q, part, tile):
-        out[0, q, :, part * TS : (part + 1) * TS] = tile
-
-    return done
+            tile = tile - stack[p, part, pl.ds(starts[p], TS), :]
+        out[0, q, :, cols] = tile
 
 
 def own_kernel(owners, offsets, tiles, mine, others, out, stack):
+    owners, offsets = Table(owners[0]), Table(offsets[0])
     here = lax.axis_index("slab")
     spot = lanes(STEP)
     clear(stack)
     for k, terms in ((0, mine), (1, others)):
         p = here if k == 0 else 1 - here
-        c = offsets[0, p, 1]
+        c = offsets.at(p, 1)
         for at in range(0, NP, STEP):
             for part in range(2):
                 low = pltpu.roll(terms[part, at : at + STEP, 0:TS].astype(F32), c, 1)
                 high = pltpu.roll(terms[part, at : at + STEP, TS:].astype(F32), c, 1)
                 stack[p, part, TS + at : TS + at + STEP, :] = jnp.where(spot < c, low, high) * step_rate
-    slots = [[owners[0, p, 3 * i + 1] & (CAP - 1) for i in range(3)] for p in range(POS)]
-    take_off(slots, [offsets[0, p, 0] for p in range(POS)], stack, tiles, keep(out))
+    slots = [[owners.at(p, 3 * i + 1) & (CAP - 1) for i in range(3)] for p in range(POS)]
+    for q in range(CAP):
+        take_off(q, slots, [offsets.at(p, 0) for p in range(POS)], stack, tiles, out)
 
 
 def own_update(owners, offsets, tiles, mine, others):
     return pl.pallas_call(
         own_kernel,
         out_shape=jax.ShapeDtypeStruct(tiles.shape, F32),
-        in_specs=[SMEM, SMEM, VMEM, VMEM, VMEM],
+        in_specs=[VMEM] * 5,
         out_specs=VMEM,
         scratch_shapes=[STACK],
         compiler_params=params(8),
@@ -382,77 +374,74 @@
     )(owners, offsets, tiles, mine, others)
 
 
-def read_notes(j, terms, lines, notes, sem):
-    lines[...] = terms[POS * NP :, :TS].astype(F32).astype(jnp.int32)
-    copy = pltpu.make_async_copy(lines.at[0:1], notes, sem)
-    copy.start()
-    return copy
-
-
-def noted(j, notes):
-    slots = [[notes[0, p * 16 + 3 * i + j] for i in range(3)] for p in range(POS)]
-    return slots, [notes[0, p * 16 + 9] for p in range(POS)]
-
-
-NOTES = [STACK, pltpu.VMEM((16, TS), jnp.int32), pltpu.SMEM((1, TS), jnp.int32), pltpu.SemaphoreType.DMA(())]
-
-
-def early_update_kernel(tiles, terms, out, stack, lines, notes, sem):
+def noted(j, terms):
+    notes = Table(terms[POS * NP :, :TS])
+    slots = [[notes.at(p, 3 * i + j) for i in range(3)] for p in range(POS)]
+    return slots, [notes.at(POS + p, 0) for p in range(POS)]
+
+
+def early_update_kernel(tiles, terms, out, whole, stack, sems):
     j = 2 - 2 * early_side()
-    copy = read_notes(j, terms, lines, notes, sem)
+    slots, rows = noted(j, terms)
     fill(terms, stack)
-    copy.wait()
-    take_off(*noted(j, notes), stack, tiles, keep(out))
+    for q in range(CAP):
+        take_off(q, slots, rows, stack, tiles, out)
+        pltpu.make_async_copy(out.at[0, q], whole.at[0, q], sems.at[q]).start()
+    for q in range(CAP):
+        pltpu.make_async_copy(out.at[0, q], whole.at[0, q], sems.at[q]).wait()
 
 
 def early_update(tiles, terms):
     return pl.pallas_call(
         early_update_kernel,
-        out_shape=jax.ShapeDtypeStruct(tiles.shape, F32),
+        out_shape=[jax.ShapeDtypeStruct(tiles.shape, F32)] * 2,
         in_specs=[VMEM, VMEM],
-        out_specs=VMEM,
-        scratch_shapes=NOTES,
+        out_specs=[VMEM, HBM],
+        scratch_shapes=[STACK, pltpu.SemaphoreType.DMA((CAP,))],
         compiler_params=params(8),
         cost_estimate=pl.CostEstimate(flops=1_000_000, bytes_accessed=3_000_000, transcendentals=0),
         name="early_update",
     )(tiles, terms)
 
 
-def late_update_kernel(tiles, terms, out, stack, lines, notes, sem, work, sems):
+def late_update_kernel(tiles, terms, whole, out, stack, work, sems):
     j = 2 * early_side()
-    copy = read_notes(j, terms, lines, notes, sem)
+    slots, rows = noted(j, terms)
     fill(terms, stack)
-    copy.wait()
-    copies = [pltpu.make_async_copy(work.at[0, q], out.at[0, q], sems.at[q]) for q in range(CAP)]
-
-    def done(q, part, tile):
-        keep(work)(q, part, tile)
-        if part == 1:
-            copies[q].start()
-
-    take_off(*noted(j, notes), stack, tiles, done)
-    for copy in copies:
-        copy.wait()
-
-
-def late_update(tiles, terms):
+    touched = [
+        functools.reduce(jnp.logical_or, [slots[p][i] == q for p in range(POS) for i in range(3)]) for q in range(CAP)
+    ]
+    for q in range(CAP):
+
+        @pl.when(touched[q])
+        def _():
+            take_off(q, slots, rows, stack, tiles, work)
+            pltpu.make_async_copy(work.at[0, q], out.at[0, q], sems.at[q]).start()
+
+    for q in range(CAP):
+
+        @pl.when(touched[q])
+        def _():
+            pltpu.make_async_copy(work.at[0, q], out.at[0, q], sems.at[q]).wait()
+
+
+def late_update(tiles, terms, whole):
     return pl.pallas_call(
         late_update_kernel,
         out_shape=jax.ShapeDtypeStruct(tiles.shape, F32),
-        in_specs=[VMEM, VMEM],
+        in_specs=[VMEM, VMEM, HBM],
         out_specs=HBM,
-        scratch_shapes=NOTES + [pltpu.VMEM((1, CAP, TS, 2 * TS), F32), pltpu.SemaphoreType.DMA((CAP,))],
+        input_output_aliases={2: 0},
+        scratch_shapes=[STACK, pltpu.VMEM((1, CAP, TS, 2 * TS), F32), pltpu.SemaphoreType.DMA((CAP,))],
         compiler_params=params(8),
         name="late_update",
-    )(tiles, terms)
-
-
-def swap(value, members, period):
+    )(tiles, terms, whole)
+
+
+def swap(value, first):
     count = lax.axis_size("scan")
-    pairs = [(i, (i + 1) % count) for i in range(count) if i % period in members]
-    pairs += [(j, i) for i, j in pairs]
-    inside = {i for i, _ in pairs}
-    return lax.ppermute(value, "scan", pairs + [(i, i) for i in range(count) if i not in inside])
+    pairs = [(i, (i + 1) % count) for i in range(first, count, 2)]
+    return lax.ppermute(value, "scan", pairs + [(j, i) for i, j in pairs])
 
 
 def across(value):
@@ -462,20 +451,21 @@
 def shards(probe_modes, tap_weights, object_slices, exit_residual, offsets, owners):
     side = lax.axis_index("slab").astype(jnp.int32).reshape(1)
     own = object_slices[0].astype(BF16)
-    first, second, third = swap(own, FIRST, 8), swap(own, SECOND, 8), swap(own, THIRD, 8)
+    late = swap(own, 1)
+    early = swap(own, 0)
     *mats, wave = exit_adjoint(side, tap_weights, exit_residual)
-    partly = early_windows(owners, offsets, object_slices, first)
-    t_there, t_near = late_windows(owners, offsets, second, third, partly)
+    partly = early_windows(owners, offsets, object_slices, early)
+    t_there, t_near = late_windows(owners, offsets, late, partly)
     t_here = across(t_there)
     terms_there = slice_terms(False, t_near, probe_modes, wave, mats)
     terms_far = across(terms_there)
     terms_here = slice_terms(True, t_here, probe_modes, wave, mats)
     early_out, late_out = split_terms(owners, offsets, terms_here, terms_far)
-    late_in = swap(late_out, (1,), 2)
-    early_in = swap(early_out, (0,), 2)
+    late_in = swap(late_out, 1)
+    early_in = swap(early_out, 0)
     tiles = own_update(owners, offsets, object_slices, terms_here, terms_far)
-    tiles = early_update(tiles, early_in)
-    return late_update(tiles, late_in)
+    tiles, whole = early_update(tiles, early_in)
+    return late_update(tiles, late_in, whole)
 
 
 def solution(mesh):

time: 48.3 us -> 44.5 us (0.921)
  starting transfers between devices: 23.2 us -> 20.7 us
  Pallas kernels: 10.9 us -> 9.35 us
  waiting for transfers between devices: 10.1 us -> 10.6 us
    ppermute x5 -> x4, starting transfers between devices: 21.7 us -> 18.9 us  [swap(): return lax.ppermute(value, 'scan', pairs + [(j, i) for i, j in pairs])]
    pallas_call x1, Pallas kernels: 0.83 us -> 0.32 us  [late_windows(): pl.pallas_call(late_kernel, out_shape=[jax.ShapeDtypeStruct((2, NP, NP),...]
    ppermute x5 -> x4, waiting for transfers between devices: 10.1 us -> 10.6 us  [swap(): return lax.ppermute(value, 'scan', pairs + [(j, i) for i, j in pairs])]
  transfers between devices with their start and end apart: 7 -> 6, of which waited for: 2 -> 2; matrix products, arithmetic and copies ran while one was open for 0% -> 0% of each run, Pallas kernels for 16% -> 17%
where the time goes in v6:
time: 44.5 us; the launch traced here: 44.3 us
  starting transfers between devices  20.7 us (47%)
  waiting for transfers between devices  10.6 us (24%)
  Pallas kernels  9.35 us (21%)
  local copies, waits for them, and re-layouts  2.29 us (5%)
  other arithmetic  1.28 us (3%)
    ppermute x4, starting transfers between devices, swap(): return lax.ppermute(value, 'scan', pairs + [(j, i) for i, j in pairs])  18.9 us
    ppermute x4, waiting for transfers between devices, swap(): return lax.ppermute(value, 'scan', pairs + [(j, i) for i, j in pairs])  10.6 us
    pallas_call x2, Pallas kernels, slice_terms(): pl.pallas_call(functools.partial(terms_kernel, far), out_shape=jax.ShapeD...  3.07 us
    unnamed x12, local copies, waits for them, and re-layouts  2.29 us
    pallas_call x1, Pallas kernels, exit_adjoint(): pl.pallas_call(lambda side, *refs: exit_kernel(*refs), grid_spec=pltpu.Pr...  1.73 us
    ppermute x2, starting transfers between devices, across(): return lax.ppermute(value, 'slab', [(0, 1), (1, 0)])  1.73 us
    convert_element_type x1, other arithmetic, shards(): own = object_slices[0].astype(BF16)  1.28 us
    pallas_call x1, Pallas kernels, early_update(): pl.pallas_call(early_update_kernel, out_shape=[jax.ShapeDtypeStruct(tiles...  1.25 us
  transfers between devices with their start and end apart: 6, of which 2 were waited for; matrix products, arithmetic and copies ran while one was open for 0% of the time, Pallas kernels for 17%

profile of v6, /device:TPU:1, one launch (start us, length us, event | category | flops | bytes accessed | tf_op | source)
XLA Modules:
  0.0 44.3 jit_solution(2031284128114258259)
XLA Ops:
  0.0 1.3 %convert_bitcast_fusion = bf16[8,128,256]{2,1,0:T(8,128)(2,1)S(1)} fusion(f32[1,8,128,256]{3,2,1,0:T(8,128)} %tiles.1), kind=kLoop, calls=%fused_computation | loop fusion | flops 262144 | bytes 1572864 | tf_op jit(solution)/shard_map/convert_element_type | solution.py:453
  1.3 0.0 copy-start
  1.3 0.0 copy-start.2
  1.3 0.0 copy-start.3
  1.3 2.6 %collective-permute-start.1 = (bf16[8,128,256]{2,1,0:T(8,128)(2,1)S(1)}, bf16[8,128,256]{2,1,0:T(8,128)(2,1)S(1)}, u32[]{:S(2)}, u32[]{:S(2)}) collective-permute-start(bf16[8,128,256]{2,1,0:T(8,128)(2,1)S(1)} %convert_bitcast_fusion), channel_id=1, source_target_pairs={{0,1},{2,3},{4,5},{6,7},{8,9},{10,11},{12,13},{14,15},{16,17},{18,... | collective-permute-start | bytes 1572872 | tf_op jit(solution)/shard_map/ppermute | solution.py:444
  3.9 9.3 %collective-permute-start = (bf16[8,128,256]{2,1,0:T(8,128)(2,1)S(1)}, bf16[8,128,256]{2,1,0:T(8,128)(2,1)S(1)}, u32[]{:S(2)}, u32[]{:S(2)}) collective-permute-start(bf16[8,128,256]{2,1,0:T(8,128)(2,1)S(1)} %convert_bitcast_fusion), channel_id=1, source_target_pairs={{1,2},{3,4},{5,6},{7,8},{9,10},{11,12},{13,14},{15,16},{17,18},{19... | collective-permute-start | bytes 1572872 | tf_op jit(solution)/shard_map/ppermute | solution.py:444
  13.2 0.0 copy-start.4
  13.2 1.6 %copy-done.4 = bf16[1,2,4,256,512]{4,3,2,1,0:T(8,128)(2,1)S(1)} copy-done((bf16[1,2,4,256,512]{4,3,2,1,0:T(8,128)(2,1)S(1)}, bf16[1,2,4,256,512]{4,3,2,1,0:T(8,128)(2,1)}, u32[]{:S(2)}) %copy-start.4) | copy-done | bytes 2097176
  14.8 0.0 copy-start.5
  14.8 0.7 %copy-done.5 = bf16[2,2,31]{2,1,0:T(2,128)(2,1)S(1)} copy-done((bf16[2,2,31]{2,1,0:T(2,128)(2,1)S(1)}, bf16[2,2,31]{2,1,0:T(2,128)(2,1)}, u32[]{:S(2)}) %copy-start.5) | copy-done | bytes 272
  15.5 1.7 %exit_adjoint.1 = (bf16[512,512]{1,0:T(8,128)(2,1)S(1)}, bf16[512,512]{1,0:T(8,128)(2,1)S(1)}, bf16[512,512]{1,0:T(8,128)(2,1)S(1)}, bf16[512,512]{1,0:T(8,128)(2,1)S(1)}, bf16[4,512,256]{2,1,0:T(8,128)(2,1)S(1)}) custom-call(s32[1]{0:T(128)} %bitcast.1.side, bf16[2,2,31]{2,1,0:T(2,128)(2,1)S(1)} %copy-done.5, bf16[1,2,4,256,512]{4,3,2,1,0:T(8,128)(2,1)S(1)} %copy-done.4), custom_call_target="tpu_custom_call" | custom-call | flops 1100000000 | bytes 6000000 | tf_op jit(solution)/shard_map/exit_adjoint/pallas_call | solution.py:71
  17.2 0.0 copy-start.1
  17.2 0.0 collective-permute-done.1.early
  17.2 0.0 copy-done
  17.2 0.0 copy-done.2
  17.2 0.0 copy-done.3
  17.2 0.7 %early_windows.1.partly = f32[2,2,256,256]{3,2,1,0:T(8,128)S(1)} custom-call(s32[1,2,9]{2,1,0:T(2,128)S(1)} %copy-done.2, s32[1,2,2]{2,1,0:T(2,128)S(1)} %copy-done.3, f32[1,8,128,256]{3,2,1,0:T(8,128)S(1)} %copy-done, bf16[8,128,256]{2,1,0:T(8,128)(2,1)S(1)} %collective-permute-done.1.early), custom_call_target="tpu_custom_call" | custom-call | flops 2000000 | bytes 2000000 | tf_op jit(solution)/shard_map/early_windows/pallas_call | solution.py:144
  17.9 6.6 %collective-permute-done.late = bf16[8,128,256]{2,1,0:T(8,128)(2,1)S(1)} collective-permute-done((bf16[8,128,256]{2,1,0:T(8,128)(2,1)S(1)}, bf16[8,128,256]{2,1,0:T(8,128)(2,1)S(1)}, u32[]{:S(2)}, u32[]{:S(2)}) %collective-permute-start) | collective-permute-done | bytes 524320 | tf_op jit(solution)/shard_map/ppermute | solution.py:444
  24.5 0.3 late_windows.1
  24.9 1.6 %collective-permute-start.2 = (bf16[2,256,256]{2,1,0:T(8,128)(2,1)S(1)}, bf16[2,256,256]{2,1,0:T(8,128)(2,1)S(1)}, u32[]{:S(2)}, u32[]{:S(2)}) collective-permute-start(bf16[2,256,256]{2,1,0:T(8,128)(2,1)S(1)} %get-tuple-element.16), channel_id=1, source_target_pairs={{0,128},{128,0},{1,129},{129,1},{2,130},{130,2},{3,131},{131,3},{4... | collective-permute-start | bytes 786440 | tf_op jit(solution)/shard_map/ppermute | solution.py:448
  26.5 0.0 copy-done.1
  26.5 1.6 %near_terms.1 = bf16[2,256,256]{2,1,0:T(8,128)(2,1)S(1)} custom-call(bf16[2,256,256]{2,1,0:T(8,128)(2,1)S(1)} %get-tuple-element.22.t, bf16[4,256,512]{2,1,0:T(8,128)(2,1)S(1)} %copy-done.1, bf16[4,512,256]{2,1,0:T(8,128)(2,1)S(1)} %get-tuple-element.17.wave, bf16[512,512]{1,0:T(8,128)(2,1)S(1)} %get-tuple-element.18.left, ...), custom_call_target="tpu_custom_call" | custom-call | flops 1100000000 | bytes 5000000 | tf_op jit(solution)/shard_map/near_terms/pallas_call | solution.py:260
  28.1 0.1 collective-permute-start.3
  28.2 0.0 collective-permute-done.2.t
  28.2 1.5 %far_terms.1.mine = f32[2,256,256]{2,1,0:T(8,128)S(1)} custom-call(bf16[2,256,256]{2,1,0:T(8,128)(2,1)S(1)} %collective-permute-done.2.t, bf16[4,256,512]{2,1,0:T(8,128)(2,1)S(1)} %copy-done.1, bf16[4,512,256]{2,1,0:T(8,128)(2,1)S(1)} %get-tuple-element.17.wave, bf16[512,512]{1,0:T(8,128)(2,1)S(1)} %get-tuple-element.18.left, ...), custom_call_target="tpu_custom_call" | custom-call | flops 1100000000 | bytes 5000000 | tf_op jit(solution)/shard_map/far_terms/pallas_call | solution.py:260
  29.7 0.0 collective-permute-done.3.others
  29.7 0.4 split_terms.1
  30.1 0.1 collective-permute-start.4
  30.2 7.0 %collective-permute-start.5 = (bf16[528,256]{1,0:T(8,128)(2,1)S(1)}, bf16[528,256]{1,0:T(8,128)(2,1)S(1)}, u32[]{:S(2)}, u32[]{:S(2)}) collective-permute-start(bf16[528,256]{1,0:T(8,128)(2,1)S(1)} %get-tuple-element.25), channel_id=1, source_target_pairs={{1,2},{3,4},{5,6},{7,8},{9,10},{11,12},{13,14},{15,16},{17,18},{19... | collective-permute-start | bytes 811016 | tf_op jit(solution)/shard_map/ppermute | solution.py:444
  37.1 0.8 %own_update.1.tiles = f32[1,8,128,256]{3,2,1,0:T(8,128)S(1)} custom-call(s32[1,2,9]{2,1,0:T(2,128)S(1)} %copy-done.2, s32[1,2,2]{2,1,0:T(2,128)S(1)} %copy-done.3, f32[1,8,128,256]{3,2,1,0:T(8,128)S(1)} %copy-done, f32[2,256,256]{2,1,0:T(8,128)S(1)} %far_terms.1.mine, bf16[2,256,256]{2,1,0:T(8,128)(2,1)S(1)} %collective-permute-done.3.others), custom_call_target="tpu_custom_call" | custom-call | flops 1000000 | bytes 3000000 | tf_op jit(solution)/shard_map/own_update/pallas_call | solution.py:365
  37.9 0.0 collective-permute-done.4.terms
  37.9 1.2 %early_update.1 = (f32[1,8,128,256]{3,2,1,0:T(8,128)S(1)}, f32[1,8,128,256]{3,2,1,0:T(8,128)}) custom-call(f32[1,8,128,256]{3,2,1,0:T(8,128)S(1)} %own_update.1.tiles, bf16[528,256]{1,0:T(8,128)(2,1)S(1)} %collective-permute-done.4.terms), custom_call_target="tpu_custom_call" | custom-call | flops 1000000 | bytes 3000000 | tf_op jit(solution)/shard_map/early_update/pallas_call | solution.py:395
  39.2 4.0 %collective-permute-done.5.terms = bf16[528,256]{1,0:T(8,128)(2,1)S(1)} collective-permute-done((bf16[528,256]{1,0:T(8,128)(2,1)S(1)}, bf16[528,256]{1,0:T(8,128)(2,1)S(1)}, u32[]{:S(2)}, u32[]{:S(2)}) %collective-permute-start.5) | collective-permute-done | bytes 270368 | tf_op jit(solution)/shard_map/ppermute | solution.py:444
  43.1 1.2 %late_update.1 = f32[1,8,128,256]{3,2,1,0:T(8,128)} custom-call(f32[1,8,128,256]{3,2,1,0:T(8,128)S(1)} %get-tuple-element.24.tiles, bf16[528,256]{1,0:T(8,128)(2,1)S(1)} %collective-permute-done.5.terms, f32[1,8,128,256]{3,2,1,0:T(8,128)} %get-tuple-element.26.whole), custom_call_target="tpu_custom_call", output_to_operand_aliasing={{}: (2, {})} | custom-call | tf_op jit(solution)/shard_map/late_update/pallas_call | solution.py:429
Async XLA Ops:
  1.3 15.9 %copy-start = (f32[1,8,128,256]{3,2,1,0:T(8,128)S(1)}, f32[1,8,128,256]{3,2,1,0:T(8,128)}, u32[]{:S(2)}) copy-start(f32[1,8,128,256]{3,2,1,0:T(8,128)} %tiles.1) | copy-start | bytes 3145732
  1.3 15.9 %copy-start.2 = (s32[1,2,9]{2,1,0:T(2,128)S(1)}, s32[1,2,9]{2,1,0:T(2,128)}, u32[]{:S(2)}) copy-start(s32[1,2,9]{2,1,0:T(2,128)} %owners.7) | copy-start | bytes 220
  1.3 15.9 %copy-start.3 = (s32[1,2,2]{2,1,0:T(2,128)S(1)}, s32[1,2,2]{2,1,0:T(2,128)}, u32[]{:S(2)}) copy-start(s32[1,2,2]{2,1,0:T(2,128)} %offsets.7) | copy-start | bytes 52
  1.3 15.9 %collective-permute-start.1 = (bf16[8,128,256]{2,1,0:T(8,128)(2,1)S(1)}, bf16[8,128,256]{2,1,0:T(8,128)(2,1)S(1)}, u32[]{:S(2)}, u32[]{:S(2)}) collective-permute-start(bf16[8,128,256]{2,1,0:T(8,128)(2,1)S(1)} %convert_bitcast_fusion), channel_id=1, source_target_pairs={{0,1},{2,3},{4,5},{6,7},{8,9},{10,11},{12,13},{14,15},{16,17},{18,... | collective-permute-start | bytes 1572872 | tf_op jit(solution)/shard_map/ppermute | solution.py:444
  3.9 20.6 %collective-permute-start = (bf16[8,128,256]{2,1,0:T(8,128)(2,1)S(1)}, bf16[8,128,256]{2,1,0:T(8,128)(2,1)S(1)}, u32[]{:S(2)}, u32[]{:S(2)}) collective-permute-start(bf16[8,128,256]{2,1,0:T(8,128)(2,1)S(1)} %convert_bitcast_fusion), channel_id=1, source_target_pairs={{1,2},{3,4},{5,6},{7,8},{9,10},{11,12},{13,14},{15,16},{17,18},{19... | collective-permute-start | bytes 1572872 | tf_op jit(solution)/shard_map/ppermute | solution.py:444
  13.2 1.6 %copy-start.4 = (bf16[1,2,4,256,512]{4,3,2,1,0:T(8,128)(2,1)S(1)}, bf16[1,2,4,256,512]{4,3,2,1,0:T(8,128)(2,1)}, u32[]{:S(2)}) copy-start(bf16[1,2,4,256,512]{4,3,2,1,0:T(8,128)(2,1)} %refs_1_.1) | copy-start | bytes 6291460
  14.8 0.7 %copy-start.5 = (bf16[2,2,31]{2,1,0:T(2,128)(2,1)S(1)}, bf16[2,2,31]{2,1,0:T(2,128)(2,1)}, u32[]{:S(2)}) copy-start(bf16[2,2,31]{2,1,0:T(2,128)(2,1)} %refs_0_.1) | copy-start | bytes 748
  17.2 9.3 %copy-start.1 = (bf16[4,256,512]{2,1,0:T(8,128)(2,1)S(1)}, bf16[4,256,512]{2,1,0:T(8,128)(2,1)}, u32[]{:S(2)}) copy-start(bf16[4,256,512]{2,1,0:T(8,128)(2,1)} %probe.3) | copy-start | bytes 3145732
  24.9 3.3 %collective-permute-start.2 = (bf16[2,256,256]{2,1,0:T(8,128)(2,1)S(1)}, bf16[2,256,256]{2,1,0:T(8,128)(2,1)S(1)}, u32[]{:S(2)}, u32[]{:S(2)}) collective-permute-start(bf16[2,256,256]{2,1,0:T(8,128)(2,1)S(1)} %get-tuple-element.16), channel_id=1, source_target_pairs={{0,128},{128,0},{1,129},{129,1},{2,130},{130,2},{3,131},{131,3},{4... | collective-permute-start | bytes 786440 | tf_op jit(solution)/shard_map/ppermute | solution.py:448
  28.1 1.6 %collective-permute-start.3 = (bf16[2,256,256]{2,1,0:T(8,128)(2,1)S(1)}, bf16[2,256,256]{2,1,0:T(8,128)(2,1)S(1)}, u32[]{:S(2)}, u32[]{:S(2)}) collective-permute-start(bf16[2,256,256]{2,1,0:T(8,128)(2,1)S(1)} %near_terms.1), channel_id=1, source_target_pairs={{0,128},{128,0},{1,129},{129,1},{2,130},{130,2},{3,131},{131,3},{4... | collective-permute-start | bytes 786440 | tf_op jit(solution)/shard_map/ppermute | solution.py:448
  30.1 7.8 %collective-permute-start.4 = (bf16[528,256]{1,0:T(8,128)(2,1)S(1)}, bf16[528,256]{1,0:T(8,128)(2,1)S(1)}, u32[]{:S(2)}, u32[]{:S(2)}) collective-permute-start(bf16[528,256]{1,0:T(8,128)(2,1)S(1)} %get-tuple-element.23), channel_id=1, source_target_pairs={{0,1},{2,3},{4,5},{6,7},{8,9},{10,11},{12,13},{14,15},{16,17},{18,... | collective-permute-start | bytes 811016 | tf_op jit(solution)/shard_map/ppermute | solution.py:444
  30.2 13.0 %collective-permute-start.5 = (bf16[528,256]{1,0:T(8,128)(2,1)S(1)}, bf16[528,256]{1,0:T(8,128)(2,1)S(1)}, u32[]{:S(2)}, u32[]{:S(2)}) collective-permute-start(bf16[528,256]{1,0:T(8,128)(2,1)S(1)} %get-tuple-element.25), channel_id=1, source_target_pairs={{1,2},{3,4},{5,6},{7,8},{9,10},{11,12},{13,14},{15,16},{17,18},{19... | collective-permute-start | bytes 811016 | tf_op jit(solution)/shard_map/ppermute | solution.py:444

commit v7 on v6

--- a/solution.py
+++ b/solution.py
@@ -328,19 +328,27 @@
             stack[p, part, TS : TS + NP, :] = terms[p * NP : (p + 1) * NP, cols].astype(F32) * step_rate
 
 
-def take_off(q, slots, rows, stack, tiles, out):
+def starts_of(q, slots, rows):
     starts = []
     for p in range(POS):
         start = jnp.int32(0)
         for i in range(3):
             start = jnp.where(slots[p][i] == q, TS + i * TS - rows[p], start)
         starts.append(start)
+    return starts
+
+
+def subtract(q, pieces, stack, tiles, out):
     for part in range(2):
         cols = slice(part * TS, (part + 1) * TS)
         tile = tiles[0, q, :, cols]
-        for p in range(POS):
-            tile = tile - stack[p, part, pl.ds(starts[p], TS), :]
+        for p, start in pieces:
+            tile = tile - stack[p, part, pl.ds(start, TS), :]
         out[0, q, :, cols] = tile
+
+
+def take_off(q, slots, rows, stack, tiles, out):
+    subtract(q, list(enumerate(starts_of(q, slots, rows))), stack, tiles, out)
 
 
 def own_kernel(owners, offsets, tiles, mine, others, out, stack):
@@ -408,14 +416,20 @@
     j = 2 * early_side()
     slots, rows = noted(j, terms)
     fill(terms, stack)
-    touched = [
-        functools.reduce(jnp.logical_or, [slots[p][i] == q for p in range(POS) for i in range(3)]) for q in range(CAP)
-    ]
-    for q in range(CAP):
+    starts = [starts_of(q, slots, rows) for q in range(CAP)]
+    touched = [first + second > 0 for first, second in starts]
+    for q, (first, second) in enumerate(starts):
+
+        @pl.when((first > 0) != (second > 0))
+        def _():
+            subtract(q, [((second > 0).astype(jnp.int32), first + second)], stack, tiles, work)
+
+        @pl.when((first > 0) & (second > 0))
+        def _():
+            subtract(q, [(0, first), (1, second)], stack, tiles, work)
 
         @pl.when(touched[q])
         def _():
-            take_off(q, slots, rows, stack, tiles, work)
             pltpu.make_async_copy(work.at[0, q], out.at[0, q], sems.at[q]).start()
 
     for q in range(CAP):

time: 44.5 us -> 44.5 us (level)
  no operation moved by 1% of the time
where the time goes in v7:
time: 44.5 us; the launch traced here: 44.3 us
  starting transfers between devices  20.7 us (47%)
  waiting for transfers between devices  10.6 us (24%)
  Pallas kernels  9.36 us (21%)
  local copies, waits for them, and re-layouts  2.29 us (5%)
  other arithmetic  1.28 us (3%)
    ppermute x4, starting transfers between devices, swap(): return lax.ppermute(value, 'scan', pairs + [(j, i) for i, j in pairs])  18.9 us
    ppermute x4, waiting for transfers between devices, swap(): return lax.ppermute(value, 'scan', pairs + [(j, i) for i, j in pairs])  10.6 us
    pallas_call x2, Pallas kernels, slice_terms(): pl.pallas_call(functools.partial(terms_kernel, far), out_shape=jax.ShapeD...  3.07 us
    unnamed x12, local copies, waits for them, and re-layouts  2.29 us
    pallas_call x1, Pallas kernels, exit_adjoint(): pl.pallas_call(lambda side, *refs: exit_kernel(*refs), grid_spec=pltpu.Pr...  1.73 us
    ppermute x2, starting transfers between devices, across(): return lax.ppermute(value, 'slab', [(0, 1), (1, 0)])  1.73 us
    convert_element_type x1, other arithmetic, shards(): own = object_slices[0].astype(BF16)  1.28 us
    pallas_call x1, Pallas kernels, early_update(): pl.pallas_call(early_update_kernel, out_shape=[jax.ShapeDtypeStruct(tiles...  1.25 us
  transfers between devices with their start and end apart: 6, of which 2 were waited for; matrix products, arithmetic and copies ran while one was open for 0% of the time, Pallas kernels for 17%

profile of v7, /device:TPU:1, one launch (start us, length us, event | category | flops | bytes accessed | tf_op | source)
XLA Modules:
  0.0 44.3 jit_solution(15905673086801588244)
XLA Ops:
  0.0 1.3 %convert_bitcast_fusion = bf16[8,128,256]{2,1,0:T(8,128)(2,1)S(1)} fusion(f32[1,8,128,256]{3,2,1,0:T(8,128)} %tiles.1), kind=kLoop, calls=%fused_computation | loop fusion | flops 262144 | bytes 1572864 | tf_op jit(solution)/shard_map/convert_element_type | solution.py:467
  1.3 0.0 copy-start
  1.3 0.0 copy-start.2
  1.3 0.0 copy-start.3
  1.3 2.6 %collective-permute-start.1 = (bf16[8,128,256]{2,1,0:T(8,128)(2,1)S(1)}, bf16[8,128,256]{2,1,0:T(8,128)(2,1)S(1)}, u32[]{:S(2)}, u32[]{:S(2)}) collective-permute-start(bf16[8,128,256]{2,1,0:T(8,128)(2,1)S(1)} %convert_bitcast_fusion), channel_id=1, source_target_pairs={{0,1},{2,3},{4,5},{6,7},{8,9},{10,11},{12,13},{14,15},{16,17},{18,... | collective-permute-start | bytes 1572872 | tf_op jit(solution)/shard_map/ppermute | solution.py:458
  3.9 9.3 %collective-permute-start = (bf16[8,128,256]{2,1,0:T(8,128)(2,1)S(1)}, bf16[8,128,256]{2,1,0:T(8,128)(2,1)S(1)}, u32[]{:S(2)}, u32[]{:S(2)}) collective-permute-start(bf16[8,128,256]{2,1,0:T(8,128)(2,1)S(1)} %convert_bitcast_fusion), channel_id=1, source_target_pairs={{1,2},{3,4},{5,6},{7,8},{9,10},{11,12},{13,14},{15,16},{17,18},{19... | collective-permute-start | bytes 1572872 | tf_op jit(solution)/shard_map/ppermute | solution.py:458
  13.2 0.0 copy-start.4
  13.2 1.6 %copy-done.4 = bf16[1,2,4,256,512]{4,3,2,1,0:T(8,128)(2,1)S(1)} copy-done((bf16[1,2,4,256,512]{4,3,2,1,0:T(8,128)(2,1)S(1)}, bf16[1,2,4,256,512]{4,3,2,1,0:T(8,128)(2,1)}, u32[]{:S(2)}) %copy-start.4) | copy-done | bytes 2097176
  14.8 0.0 copy-start.5
  14.8 0.7 %copy-done.5 = bf16[2,2,31]{2,1,0:T(2,128)(2,1)S(1)} copy-done((bf16[2,2,31]{2,1,0:T(2,128)(2,1)S(1)}, bf16[2,2,31]{2,1,0:T(2,128)(2,1)}, u32[]{:S(2)}) %copy-start.5) | copy-done | bytes 272
  15.5 1.7 %exit_adjoint.1 = (bf16[512,512]{1,0:T(8,128)(2,1)S(1)}, bf16[512,512]{1,0:T(8,128)(2,1)S(1)}, bf16[512,512]{1,0:T(8,128)(2,1)S(1)}, bf16[512,512]{1,0:T(8,128)(2,1)S(1)}, bf16[4,512,256]{2,1,0:T(8,128)(2,1)S(1)}) custom-call(s32[1]{0:T(128)} %bitcast.1.side, bf16[2,2,31]{2,1,0:T(2,128)(2,1)S(1)} %copy-done.5, bf16[1,2,4,256,512]{4,3,2,1,0:T(8,128)(2,1)S(1)} %copy-done.4), custom_call_target="tpu_custom_call" | custom-call | flops 1100000000 | bytes 6000000 | tf_op jit(solution)/shard_map/exit_adjoint/pallas_call | solution.py:71
  17.2 0.0 copy-start.1
  17.2 0.0 collective-permute-done.1.early
  17.2 0.0 copy-done
  17.2 0.0 copy-done.2
  17.2 0.0 copy-done.3
  17.2 0.7 %early_windows.1.partly = f32[2,2,256,256]{3,2,1,0:T(8,128)S(1)} custom-call(s32[1,2,9]{2,1,0:T(2,128)S(1)} %copy-done.2, s32[1,2,2]{2,1,0:T(2,128)S(1)} %copy-done.3, f32[1,8,128,256]{3,2,1,0:T(8,128)S(1)} %copy-done, bf16[8,128,256]{2,1,0:T(8,128)(2,1)S(1)} %collective-permute-done.1.early), custom_call_target="tpu_custom_call" | custom-call | flops 2000000 | bytes 2000000 | tf_op jit(solution)/shard_map/early_windows/pallas_call | solution.py:144
  17.9 6.6 %collective-permute-done.late = bf16[8,128,256]{2,1,0:T(8,128)(2,1)S(1)} collective-permute-done((bf16[8,128,256]{2,1,0:T(8,128)(2,1)S(1)}, bf16[8,128,256]{2,1,0:T(8,128)(2,1)S(1)}, u32[]{:S(2)}, u32[]{:S(2)}) %collective-permute-start) | collective-permute-done | bytes 524320 | tf_op jit(solution)/shard_map/ppermute | solution.py:458
  24.5 0.3 late_windows.1
  24.9 1.6 %collective-permute-start.2 = (bf16[2,256,256]{2,1,0:T(8,128)(2,1)S(1)}, bf16[2,256,256]{2,1,0:T(8,128)(2,1)S(1)}, u32[]{:S(2)}, u32[]{:S(2)}) collective-permute-start(bf16[2,256,256]{2,1,0:T(8,128)(2,1)S(1)} %get-tuple-element.16), channel_id=1, source_target_pairs={{0,128},{128,0},{1,129},{129,1},{2,130},{130,2},{3,131},{131,3},{4... | collective-permute-start | bytes 786440 | tf_op jit(solution)/shard_map/ppermute | solution.py:462
  26.5 0.0 copy-done.1
  26.5 1.6 %near_terms.1 = bf16[2,256,256]{2,1,0:T(8,128)(2,1)S(1)} custom-call(bf16[2,256,256]{2,1,0:T(8,128)(2,1)S(1)} %get-tuple-element.22.t, bf16[4,256,512]{2,1,0:T(8,128)(2,1)S(1)} %copy-done.1, bf16[4,512,256]{2,1,0:T(8,128)(2,1)S(1)} %get-tuple-element.17.wave, bf16[512,512]{1,0:T(8,128)(2,1)S(1)} %get-tuple-element.18.left, ...), custom_call_target="tpu_custom_call" | custom-call | flops 1100000000 | bytes 5000000 | tf_op jit(solution)/shard_map/near_terms/pallas_call | solution.py:260
  28.1 0.1 collective-permute-start.3
  28.2 0.0 collective-permute-done.2.t
  28.2 1.5 %far_terms.1.mine = f32[2,256,256]{2,1,0:T(8,128)S(1)} custom-call(bf16[2,256,256]{2,1,0:T(8,128)(2,1)S(1)} %collective-permute-done.2.t, bf16[4,256,512]{2,1,0:T(8,128)(2,1)S(1)} %copy-done.1, bf16[4,512,256]{2,1,0:T(8,128)(2,1)S(1)} %get-tuple-element.17.wave, bf16[512,512]{1,0:T(8,128)(2,1)S(1)} %get-tuple-element.18.left, ...), custom_call_target="tpu_custom_call" | custom-call | flops 1100000000 | bytes 5000000 | tf_op jit(solution)/shard_map/far_terms/pallas_call | solution.py:260
  29.7 0.0 collective-permute-done.3.others
  29.7 0.4 split_terms.1
  30.1 0.1 collective-permute-start.4
  30.2 7.0 %collective-permute-start.5 = (bf16[528,256]{1,0:T(8,128)(2,1)S(1)}, bf16[528,256]{1,0:T(8,128)(2,1)S(1)}, u32[]{:S(2)}, u32[]{:S(2)}) collective-permute-start(bf16[528,256]{1,0:T(8,128)(2,1)S(1)} %get-tuple-element.25), channel_id=1, source_target_pairs={{1,2},{3,4},{5,6},{7,8},{9,10},{11,12},{13,14},{15,16},{17,18},{19... | collective-permute-start | bytes 811016 | tf_op jit(solution)/shard_map/ppermute | solution.py:458
  37.1 0.8 %own_update.1.tiles = f32[1,8,128,256]{3,2,1,0:T(8,128)S(1)} custom-call(s32[1,2,9]{2,1,0:T(2,128)S(1)} %copy-done.2, s32[1,2,2]{2,1,0:T(2,128)S(1)} %copy-done.3, f32[1,8,128,256]{3,2,1,0:T(8,128)S(1)} %copy-done, f32[2,256,256]{2,1,0:T(8,128)S(1)} %far_terms.1.mine, bf16[2,256,256]{2,1,0:T(8,128)(2,1)S(1)} %collective-permute-done.3.others), custom_call_target="tpu_custom_call" | custom-call | flops 1000000 | bytes 3000000 | tf_op jit(solution)/shard_map/own_update/pallas_call | solution.py:373
  37.9 0.0 collective-permute-done.4.terms
  37.9 1.3 %early_update.1 = (f32[1,8,128,256]{3,2,1,0:T(8,128)S(1)}, f32[1,8,128,256]{3,2,1,0:T(8,128)}) custom-call(f32[1,8,128,256]{3,2,1,0:T(8,128)S(1)} %own_update.1.tiles, bf16[528,256]{1,0:T(8,128)(2,1)S(1)} %collective-permute-done.4.terms), custom_call_target="tpu_custom_call" | custom-call | flops 1000000 | bytes 3000000 | tf_op jit(solution)/shard_map/early_update/pallas_call | solution.py:403
  39.2 4.0 %collective-permute-done.5.terms = bf16[528,256]{1,0:T(8,128)(2,1)S(1)} collective-permute-done((bf16[528,256]{1,0:T(8,128)(2,1)S(1)}, bf16[528,256]{1,0:T(8,128)(2,1)S(1)}, u32[]{:S(2)}, u32[]{:S(2)}) %collective-permute-start.5) | collective-permute-done | bytes 270368 | tf_op jit(solution)/shard_map/ppermute | solution.py:458
  43.1 1.2 %late_update.1 = f32[1,8,128,256]{3,2,1,0:T(8,128)} custom-call(f32[1,8,128,256]{3,2,1,0:T(8,128)S(1)} %get-tuple-element.24.tiles, bf16[528,256]{1,0:T(8,128)(2,1)S(1)} %collective-permute-done.5.terms, f32[1,8,128,256]{3,2,1,0:T(8,128)} %get-tuple-element.26.whole), custom_call_target="tpu_custom_call", output_to_operand_aliasing={{}: (2, {})} | custom-call | tf_op jit(solution)/shard_map/late_update/pallas_call | solution.py:443
Async XLA Ops:
  1.3 15.9 %copy-start = (f32[1,8,128,256]{3,2,1,0:T(8,128)S(1)}, f32[1,8,128,256]{3,2,1,0:T(8,128)}, u32[]{:S(2)}) copy-start(f32[1,8,128,256]{3,2,1,0:T(8,128)} %tiles.1) | copy-start | bytes 3145732
  1.3 15.9 %copy-start.2 = (s32[1,2,9]{2,1,0:T(2,128)S(1)}, s32[1,2,9]{2,1,0:T(2,128)}, u32[]{:S(2)}) copy-start(s32[1,2,9]{2,1,0:T(2,128)} %owners.7) | copy-start | bytes 220
  1.3 15.9 %copy-start.3 = (s32[1,2,2]{2,1,0:T(2,128)S(1)}, s32[1,2,2]{2,1,0:T(2,128)}, u32[]{:S(2)}) copy-start(s32[1,2,2]{2,1,0:T(2,128)} %offsets.7) | copy-start | bytes 52
  1.3 15.9 %collective-permute-start.1 = (bf16[8,128,256]{2,1,0:T(8,128)(2,1)S(1)}, bf16[8,128,256]{2,1,0:T(8,128)(2,1)S(1)}, u32[]{:S(2)}, u32[]{:S(2)}) collective-permute-start(bf16[8,128,256]{2,1,0:T(8,128)(2,1)S(1)} %convert_bitcast_fusion), channel_id=1, source_target_pairs={{0,1},{2,3},{4,5},{6,7},{8,9},{10,11},{12,13},{14,15},{16,17},{18,... | collective-permute-start | bytes 1572872 | tf_op jit(solution)/shard_map/ppermute | solution.py:458
  3.9 20.6 %collective-permute-start = (bf16[8,128,256]{2,1,0:T(8,128)(2,1)S(1)}, bf16[8,128,256]{2,1,0:T(8,128)(2,1)S(1)}, u32[]{:S(2)}, u32[]{:S(2)}) collective-permute-start(bf16[8,128,256]{2,1,0:T(8,128)(2,1)S(1)} %convert_bitcast_fusion), channel_id=1, source_target_pairs={{1,2},{3,4},{5,6},{7,8},{9,10},{11,12},{13,14},{15,16},{17,18},{19... | collective-permute-start | bytes 1572872 | tf_op jit(solution)/shard_map/ppermute | solution.py:458
  13.2 1.6 %copy-start.4 = (bf16[1,2,4,256,512]{4,3,2,1,0:T(8,128)(2,1)S(1)}, bf16[1,2,4,256,512]{4,3,2,1,0:T(8,128)(2,1)}, u32[]{:S(2)}) copy-start(bf16[1,2,4,256,512]{4,3,2,1,0:T(8,128)(2,1)} %refs_1_.1) | copy-start | bytes 6291460
  14.8 0.7 %copy-start.5 = (bf16[2,2,31]{2,1,0:T(2,128)(2,1)S(1)}, bf16[2,2,31]{2,1,0:T(2,128)(2,1)}, u32[]{:S(2)}) copy-start(bf16[2,2,31]{2,1,0:T(2,128)(2,1)} %refs_0_.1) | copy-start | bytes 748
  17.2 9.3 %copy-start.1 = (bf16[4,256,512]{2,1,0:T(8,128)(2,1)S(1)}, bf16[4,256,512]{2,1,0:T(8,128)(2,1)}, u32[]{:S(2)}) copy-start(bf16[4,256,512]{2,1,0:T(8,128)(2,1)} %probe.3) | copy-start | bytes 3145732
  24.9 3.3 %collective-permute-start.2 = (bf16[2,256,256]{2,1,0:T(8,128)(2,1)S(1)}, bf16[2,256,256]{2,1,0:T(8,128)(2,1)S(1)}, u32[]{:S(2)}, u32[]{:S(2)}) collective-permute-start(bf16[2,256,256]{2,1,0:T(8,128)(2,1)S(1)} %get-tuple-element.16), channel_id=1, source_target_pairs={{0,128},{128,0},{1,129},{129,1},{2,130},{130,2},{3,131},{131,3},{4... | collective-permute-start | bytes 786440 | tf_op jit(solution)/shard_map/ppermute | solution.py:462
  28.1 1.6 %collective-permute-start.3 = (bf16[2,256,256]{2,1,0:T(8,128)(2,1)S(1)}, bf16[2,256,256]{2,1,0:T(8,128)(2,1)S(1)}, u32[]{:S(2)}, u32[]{:S(2)}) collective-permute-start(bf16[2,256,256]{2,1,0:T(8,128)(2,1)S(1)} %near_terms.1), channel_id=1, source_target_pairs={{0,128},{128,0},{1,129},{129,1},{2,130},{130,2},{3,131},{131,3},{4... | collective-permute-start | bytes 786440 | tf_op jit(solution)/shard_map/ppermute | solution.py:462
  30.1 7.8 %collective-permute-start.4 = (bf16[528,256]{1,0:T(8,128)(2,1)S(1)}, bf16[528,256]{1,0:T(8,128)(2,1)S(1)}, u32[]{:S(2)}, u32[]{:S(2)}) collective-permute-start(bf16[528,256]{1,0:T(8,128)(2,1)S(1)} %get-tuple-element.23), channel_id=1, source_target_pairs={{0,1},{2,3},{4,5},{6,7},{8,9},{10,11},{12,13},{14,15},{16,17},{18,... | collective-permute-start | bytes 811016 | tf_op jit(solution)/shard_map/ppermute | solution.py:458
  30.2 13.0 %collective-permute-start.5 = (bf16[528,256]{1,0:T(8,128)(2,1)S(1)}, bf16[528,256]{1,0:T(8,128)(2,1)S(1)}, u32[]{:S(2)}, u32[]{:S(2)}) collective-permute-start(bf16[528,256]{1,0:T(8,128)(2,1)S(1)} %get-tuple-element.25), channel_id=1, source_target_pairs={{1,2},{3,4},{5,6},{7,8},{9,10},{11,12},{13,14},{15,16},{17,18},{19... | collective-permute-start | bytes 811016 | tf_op jit(solution)/shard_map/ppermute | solution.py:458
